TPU v7x, 32 devices: a whole 2x2x4 slice. The times are simulated.
32 devices in a mesh: grp: 2 (over y), hot: 4 (over x, core), patch: 4 (over z).
Axes of the slice: x: 2, y: 2, z: 4, core: 2. Of those that a mesh axis runs over, the one named last changes fastest.
Arguments:
- influence: bfloat16 [3, 4096, 4096], P(None, 'hot', 'patch'), may hold values from -0.09375 to 0.09375
- loads: bfloat16 [8192, 128], P('grp'), parts along dimension 0, may hold values from -6 to 6
- patch_order: int32 [4096], replicated, may hold values from 0 to 4095, each once
- spectral_weights: float32 [128], P('grp'), parts along dimension 0, may hold values from 0.005 to 0.05
- block_position: int32 [4096], replicated, may hold values from 0 to 4095, as said below
- block_pairs: int32 [48, 2], P(('hot', 'patch')), may hold values from 0 to 15, as said below
Outputs:
- cross_spectra: bfloat16 [96, 2, 768, 768], P(('grp', 'hot', 'patch')), parts along dimension 0
There are 2 independent parts, one for each index of `grp`. A program takes and returns all parts, laid end to end along the dimension named above; an argument that names none is the same for every part. Nothing has to cross between parts.
Inputs may be any that keep to these rules, and one draw needn't show every extreme that they name: `patch_order`: a permutation of the patches. `block_position`: a permutation of the hotspots; hotspots h * 1024 to (h + 1) * 1024 - 1 send exactly 256 of their rows into every range of rows d * 1024 to (d + 1) * 1024 - 1 of block order. `block_pairs`: each row holds two block numbers, the first not greater than the second; pairs may repeat.
All inputs are finite; a program needn't handle non-finite values.
Results may differ from a plain program's by a relative error of at most 0.0064.
Values may be sent and summed in bfloat16 or wider, within the bound.
No kernel may reach another device: no remote copies, remote signals or barrier semaphores. Data moves between devices by JAX's collectives and lax.ppermute only.
A program may use at most 128 MiB of HBM per device.

v0:
```python
import jax
import jax.numpy as jnp
from jax import lax
from jax.sharding import PartitionSpec as P

BLK = 256


def block_order(gathered, block_position):
    hotspots = block_position.shape[0]
    inverse = (
        jnp.zeros((hotspots,), jnp.int32)
        .at[block_position]
        .set(jnp.arange(hotspots, dtype=jnp.int32))
    )
    return jnp.take(gathered, inverse, axis=0)


def shards(influence, loads, patch_order, spectral_weights, block_position, block_pairs):
    components, hot_rows, patch_cols = influence.shape
    columns = loads.shape[1]
    half_cols = columns // 2
    row_width = components * columns
    pair_count = block_pairs.shape[0]
    patch_index = lax.axis_index("patch")
    my_order = lax.dynamic_slice_in_dim(patch_order, patch_index * patch_cols, patch_cols)
    my_loads = jnp.take(loads, my_order, axis=0)
    needed_rows = (
        block_pairs.reshape(-1)[:, None] * BLK + jnp.arange(BLK, dtype=jnp.int32)[None, :]
    ).reshape(-1)
    share_rows = hot_rows // lax.axis_size("patch")
    partial_term = jnp.einsum(
        "chp,pf->hcf", influence, my_loads, preferred_element_type=jnp.float32
    )
    stress_share = lax.psum_scatter(
        partial_term.reshape(share_rows * lax.axis_size("patch"), row_width),
        "patch",
        scatter_dimension=0,
        tiled=True,
    ).astype(jnp.bfloat16)
    gathered = lax.all_gather(stress_share, ("hot", "patch"), axis=0, tiled=True)
    pair_rows = jnp.take(block_order(gathered, block_position), needed_rows, axis=0)
    pair_blocks = pair_rows.reshape(pair_count, 2, BLK * components, columns)
    weights_row = jnp.concatenate([spectral_weights, spectral_weights])
    contract_dims = (((1,), (1,)), ((), ()))

    def one_pair(both_blocks):
        left_rows = both_blocks[0]
        right_rows = both_blocks[1]
        scaled = (left_rows.astype(jnp.float32) * weights_row).astype(jnp.bfloat16)
        rotated = jnp.concatenate([-right_rows[:, half_cols:], right_rows[:, :half_cols]], axis=1)
        real_part = lax.dot_general(
            scaled, right_rows, contract_dims, preferred_element_type=jnp.float32
        )
        imag_part = lax.dot_general(
            scaled, rotated, contract_dims, preferred_element_type=jnp.float32
        )
        return jnp.stack([real_part, imag_part]).astype(jnp.bfloat16)

    return lax.map(one_pair, pair_blocks)


def solution(mesh):
    placed = (
        P(None, "hot", "patch"),
        P("grp", None),
        P(),
        P("grp"),
        P(),
        P(("hot", "patch"), None),
    )
    return jax.shard_map(
        shards,
        mesh=mesh,
        in_specs=placed,
        out_specs=P(("grp", "hot", "patch"), None, None, None),
        check_vma=False,
    )
```

profile of v0, /device:TPU:0, one launch (start us, length us, event | category | flops | bytes accessed | tf_op | source)
XLA Modules:
  0.0 148.5 jit_solution(16722454239238065233)
XLA Ops:
  6.5 0.8 fusion.30
  7.3 0.7 compare_and_fusion.1
  8.0 3.2 %gather_fusion = bf16[1024,128]{1,0:T(8,128)(2,1)S(1)} fusion(bf16[4096,128]{1,0:T(8,128)(2,1)S(1)} %copy-done, s32[1024]{0:T(1024)S(1)} %fusion.30), kind=kCustom, calls=%fused_computation | custom fusion | bytes 528384 | tf_op jit(solution)/shard_map/jit(_take)/gather | solution.py:27
  11.2 5.2 %fusion.18 = f32[128,3,1024]{2,0,1:T(8,128)S(1)} fusion(bf16[3,1024,1024]{2,1,0:T(8,128)(2,1)} %param.8, bf16[1024,128]{1,0:T(8,128)(2,1)S(1)} %gather_fusion, pred[1024]{0:T(1024)(128)(4,1)S(1)} %compare_and_fusion.1), kind=kOutput, calls=%fused_computation.29 | convolution fusion | flops 805437440 | bytes 8127488 | tf_op jit(solution)/shard_map/chp,pf->hcf/dot_general | solution.py:32
  16.5 1.6 %copy.13 = f32[1024,384]{1,0:T(8,128)} copy(f32[1024,384]{0,1:T(8,128)S(1)} %bitcast.45) | data formatting | bytes 3145728 | tf_op jit(solution)/shard_map/reshape | solution.py:36
  18.2 38.1 %reduce-scatter.2.cloned.1.call-done = f32[256,384]{1,0:T(8,128)} async-done(((f32[1024,384]{1,0:T(8,128)}), f32[256,384]{1,0:T(8,128)}) %reduce-scatter.2.cloned.1.call-update) | async-done | bytes 393232 | tf_op jit(solution)/shard_map/reduce_scatter | solution.py:35
  56.3 1.7 %convert_element_type.28 = bf16[256,384]{1,0:T(8,128)(2,1)} convert(f32[256,384]{1,0:T(8,128)} %reduce-scatter.2.cloned.1.call-done) | non-fusion elementwise | flops 98304 | bytes 589824 | tf_op jit(solution)/shard_map/convert_element_type | solution.py:40
  58.7 0.6 broadcast_in_dim.50
  59.3 15.5 %scatter_custom_fusion = s32[4096]{0:T(1024)S(1)} fusion(s32[4096]{0:T(1024)S(1)} %compare_select_fusion.1, s32[4096]{0:T(1024)S(1)} %iota.8, s32[]{:T(128)} %constant.36.clone.1), kind=kCustom, calls=%fused_computation.43 | custom fusion | bytes 16388 | tf_op jit(solution)/shard_map/scatter | solution.py:14
  75.0 27.8 %all-gather.2.cloned.1.call-done = bf16[4096,384]{1,0:T(8,128)(2,1)} async-done(((bf16[256,384]{1,0:T(8,128)(2,1)}), bf16[4096,384]{1,0:T(8,128)(2,1)}) %all-gather.2.cloned.1.call-update) | async-done | bytes 3145744 | tf_op jit(solution)/shard_map/all_gather | solution.py:41
  102.8 19.0 %gather_fusion.1 = bf16[4096,384]{1,0:T(8,128)(2,1)} fusion(bf16[4096,384]{1,0:T(8,128)(2,1)} %all-gather.2.cloned.1.call-done, s32[4096]{0:T(1024)S(1)} %fusion.23), kind=kCustom, calls=%fused_computation.1 | custom fusion | bytes 6307840 | tf_op jit(solution)/shard_map/jit(_take)/gather | solution.py:16
  121.8 3.4 %broadcast_select_fusion = bf16[4096,384]{1,0:T(8,128)(2,1)} fusion(bf16[4096,384]{1,0:T(8,128)(2,1)} %gather_fusion.1, pred[4096]{0:T(1024)(128)(4,1)S(1)} %compare_and_fusion), kind=kLoop, calls=%fused_computation.27 | loop fusion | flops 1572864 | bytes 6295552 | tf_op jit(solution)/shard_map/jit(_take)/select_n | solution.py:16
  125.2 6.6 %gather_fusion.2 = bf16[1536,384]{1,0:T(8,128)(2,1)S(1)} fusion(bf16[4096,384]{1,0:T(8,128)(2,1)} %broadcast_select_fusion, s32[2048]{0:T(1024)S(1)} %pad_clamp_fusion), kind=kCustom, calls=%fused_computation.2 | custom fusion | bytes 2365440 | tf_op jit(solution)/shard_map/jit(_take)/gather | solution.py:42
  131.9 0.6 gather.17
  132.5 0.9 broadcast_select_fusion.1
  133.3 8.3 %while.10 = (s32[]{:T(128)}, bf16[3,2,768,768]{3,2,1,0:T(8,128)(2,1)}, bf16[3,2,768,128]{3,2,1,0:T(8,128)(2,1)S(1)}, f32[128]{0:T(128)S(1)}, s32[]{:T(128)}, /*index=5*/s32[]{:T(128)}, s32[]{}) while((s32[]{:T(128)}, bf16[3,2,768,768]{3,2,1,0:T(8,128)(2,1)}, bf16[3,2,768,128]{3,2,1,0:T(8,128)(2,1)S(1)}, f32[128]{0:T(128)S(1)}, s32[]{:T(128)}, ...), condition=%wide.region_3.4_spmd, body=%wide.region_2.3_spmd.sunk | while | flops 308920320 | bytes 8849001 | solution.py:60
  133.5 0.6 fusion.44
  134.1 0.5 fusion.45
  134.6 1.6 %maximum_dynamic-update-slice_fusion.2 = bf16[3,2,768,768]{3,2,1,0:T(8,128)(2,1)} fusion(bf16[3,2,768,768]{3,2,1,0:T(8,128)(2,1)} %get-tuple-element.75, s32[]{:T(128)} %get-tuple-element.74, bf16[1,1,768,768]{3,2,1,0:T(8,128)(2,1)S(1)} %fusion.44, bf16[1,1,768,768]{3,2,1,0:T(8,128)(2,1)S(1)} %fusion.45), kind=kLoop, calls=%fused_computation.4.clone.1 | loop fusion | flops 4718592 | bytes 4719104 | tf_op jit(solution)/shard_map/while/body/jit(dynamic_update_index_in_dim)/dynamic_update_slice | solution.py:60
  136.3 0.6 fusion.44
  137.3 1.6 %maximum_dynamic-update-slice_fusion.2 = bf16[3,2,768,768]{3,2,1,0:T(8,128)(2,1)} fusion(bf16[3,2,768,768]{3,2,1,0:T(8,128)(2,1)} %get-tuple-element.75, s32[]{:T(128)} %get-tuple-element.74, bf16[1,1,768,768]{3,2,1,0:T(8,128)(2,1)S(1)} %fusion.44, bf16[1,1,768,768]{3,2,1,0:T(8,128)(2,1)S(1)} %fusion.45), kind=kLoop, calls=%fused_computation.4.clone.1 | loop fusion | flops 4718592 | bytes 4719104 | tf_op jit(solution)/shard_map/while/body/jit(dynamic_update_index_in_dim)/dynamic_update_slice | solution.py:60
  139.0 0.6 fusion.44
  139.6 0.5 fusion.45
  140.1 1.6 %maximum_dynamic-update-slice_fusion.2 = bf16[3,2,768,768]{3,2,1,0:T(8,128)(2,1)} fusion(bf16[3,2,768,768]{3,2,1,0:T(8,128)(2,1)} %get-tuple-element.75, s32[]{:T(128)} %get-tuple-element.74, bf16[1,1,768,768]{3,2,1,0:T(8,128)(2,1)S(1)} %fusion.44, bf16[1,1,768,768]{3,2,1,0:T(8,128)(2,1)S(1)} %fusion.45), kind=kLoop, calls=%fused_computation.4.clone.1 | loop fusion | flops 4718592 | bytes 4719104 | tf_op jit(solution)/shard_map/while/body/jit(dynamic_update_index_in_dim)/dynamic_update_slice | solution.py:60
  (35 shorter events, 1.8 us)
Async XLA Ops:
  6.5 1.5 copy-start
  6.5 49.8 %reduce-scatter.2.cloned.1.call-start = ((), (), s32[]{:S(2)}) async-start(), calls=%async_computation.1 | async-start | bytes 1966080 | tf_op jit(solution)/shard_map/reduce_scatter | solution.py:35
  16.5 41.6 %copy-start.2 = (s32[3,2]{0,1:T(2,128)S(1)}, s32[3,2]{0,1:T(2,128)}, u32[]{:S(2)}) copy-start(s32[3,2]{0,1:T(2,128)} %param.13) | copy-start | bytes 76
  16.5 42.8 %copy-start.1 = (s32[4096]{0:T(1024)S(1)}, s32[4096]{0:T(1024)}, u32[]{:S(2)}) copy-start(s32[4096]{0:T(1024)} %param.12) | copy-start | bytes 49156
  16.5 58.3 %copy-start.3 = (f32[64]{0:T(128)S(1)}, f32[64]{0:T(128)}, u32[]{:S(2)}) copy-start(f32[64]{0:T(128)} %param.11) | copy-start | bytes 772
  18.1 84.7 %all-gather.2.cloned.1.call-start = ((), (), s32[]{:S(2)}) async-start(), calls=%async_computation.2 | async-start | bytes 3342336 | tf_op jit(solution)/shard_map/all_gather | solution.py:41
Sparse Core Ops, SparseCore 0:
  18.3 37.9 reduce-scatter.1
  58.6 44.1 all-gather.1
where the time goes:
time: 149 us; the launch traced here: 148 us
  waiting for transfers between devices  66 us (44%)
  local copies, waits for them, and re-layouts  47.7 us (32%)
  between operations  13.6 us (9%)
  other arithmetic  12.8 us (9%)
  matrix products  8.3 us (6%)
    reduce_scatter x1, waiting for transfers between devices, shards(): lax.psum_scatter(partial_term.reshape(share_rows * lax.axis_size('patch')...  38.1 us
    all_gather x1, waiting for transfers between devices, shards(): lax.all_gather(stress_share, ('hot', 'patch'), axis=0, tiled=True)  27.8 us
    gather x1, local copies, waits for them, and re-layouts, block_order(): return jnp.take(gathered, inverse, axis=0)  19 us
    scatter x1, local copies, waits for them, and re-layouts, block_order(): inverse = jnp.zeros((hotspots,), jnp.int32).at[block_position].set(jnp.ar...  15.5 us
    gather x2, local copies, waits for them, and re-layouts, shards(): jnp.take(block_order(gathered, block_position), needed_rows, axis=0)  7.21 us
    dot_general x1, matrix products, shards(): jnp.einsum('chp,pf->hcf', influence, my_loads, preferred_element_type=jnp...  5.24 us
    dynamic_update_slice x3, other arithmetic, shards(): return lax.map(one_pair, pair_blocks)  4.69 us
    select_n x1, other arithmetic, block_order(): return jnp.take(gathered, inverse, axis=0)  3.43 us
  transfers between devices with their start and end apart: 2, of which 2 were waited for; matrix products, arithmetic and copies ran while one was open for 11% of the time, Pallas kernels for 0%

commit v1 on v0

v1 whole, which is shorter than its diff:
```python
import functools

import jax
import jax.numpy as jnp
from jax import lax
from jax.experimental import pallas as pl
from jax.experimental.pallas import tpu as pltpu
from jax.sharding import PartitionSpec as P

BLK = 256
LANES = 128
F32 = jnp.float32
BF16 = jnp.bfloat16
VMEM_BYTES = 48 * 1024 * 1024


def params(steps=1):
    return pltpu.CompilerParams(
        dimension_semantics=("arbitrary",) * steps, vmem_limit_bytes=VMEM_BYTES
    )


def share_product(influence_ref, my_loads, out_ref):
    columns = my_loads.shape[1]
    for c in range(influence_ref.shape[0]):
        part = jnp.dot(influence_ref[c], my_loads, preferred_element_type=F32)
        out_ref[:, c * columns : (c + 1) * columns] = part.astype(out_ref.dtype)


def gather_kernel(index_ref, order_ref, loads_ref, *refs):
    shares = (len(refs) - 2) // 2
    influence_refs, out_refs = refs[:shares], refs[shares : 2 * shares]
    my_loads_ref, pick_ref = refs[2 * shares :]
    patches = loads_ref.shape[0]
    lane = lax.broadcasted_iota(jnp.int32, (LANES, LANES), 1)
    for g in range(order_ref.shape[1]):
        row = jnp.broadcast_to(order_ref[0, g : g + 1, :], (LANES, LANES))
        wanted = jnp.transpose(row) - lane
        for j in range(patches // LANES):
            pick_ref[g * LANES : (g + 1) * LANES, j * LANES : (j + 1) * LANES] = jnp.where(
                wanted == j * LANES, 1.0, 0.0
            ).astype(BF16)
    my_loads_ref[...] = jnp.dot(
        pick_ref[...], loads_ref[...], preferred_element_type=F32
    ).astype(BF16)
    my_loads = my_loads_ref[...]
    for influence_ref, out_ref in zip(influence_refs, out_refs):
        share_product(influence_ref, my_loads, out_ref)


def product_kernel(index_ref, my_loads_ref, *refs):
    shares = len(refs) // 2
    my_loads = my_loads_ref[...]
    for influence_ref, out_ref in zip(refs[:shares], refs[shares:]):
        share_product(influence_ref, my_loads, out_ref)


def share_spec(influence, share_rows, which):
    return pl.BlockSpec(
        (influence.shape[0], share_rows, influence.shape[2]),
        lambda i, index_ref: (0, index_ref[which], 0),
    )


def whole_spec(shape):
    return pl.BlockSpec(shape, lambda i, *_: (0,) * len(shape))


def first_products(index, order, loads, influence, share_rows, which):
    components, _, patch_cols = influence.shape
    patches, columns = loads.shape
    share = jax.ShapeDtypeStruct((share_rows, components * columns), BF16)
    out = pl.pallas_call(
        gather_kernel,
        out_shape=[share] * len(which) + [jax.ShapeDtypeStruct((patch_cols, columns), BF16)],
        grid_spec=pltpu.PrefetchScalarGridSpec(
            num_scalar_prefetch=1,
            grid=(1,),
            in_specs=[
                pl.BlockSpec(
                    (1, patch_cols // LANES, LANES), lambda i, index_ref: (index_ref[0], 0, 0)
                ),
                whole_spec(loads.shape),
            ]
            + [share_spec(influence, share_rows, k) for k in which],
            out_specs=[whole_spec(share.shape)] * len(which) + [whole_spec((patch_cols, columns))],
            scratch_shapes=[pltpu.VMEM((patch_cols, patches), BF16)],
        ),
        compiler_params=params(),
        name="first_products",
    )(index, order, loads, *([influence] * len(which)))
    return out[:-1], out[-1]


def more_products(index, my_loads, influence, share_rows, which, kinds):
    components, _, _ = influence.shape
    columns = my_loads.shape[1]
    shape = (share_rows, components * columns)
    return pl.pallas_call(
        product_kernel,
        out_shape=[jax.ShapeDtypeStruct(shape, kind) for kind in kinds],
        grid_spec=pltpu.PrefetchScalarGridSpec(
            num_scalar_prefetch=1,
            grid=(1,),
            in_specs=[whole_spec(my_loads.shape)]
            + [share_spec(influence, share_rows, k) for k in which],
            out_specs=[whole_spec(shape)] * len(which),
        ),
        compiler_params=params(),
        name="more_products",
    )(index, my_loads, *([influence] * len(which)))


def sum_kernel(own_ref, *refs):
    total = own_ref[...]
    for ref in refs[:-1]:
        total = total + ref[...].astype(F32)
    refs[-1][...] = total.astype(BF16)


def share_sum(own, others):
    return pl.pallas_call(
        sum_kernel,
        out_shape=jax.ShapeDtypeStruct(own.shape, BF16),
        compiler_params=pltpu.CompilerParams(vmem_limit_bytes=VMEM_BYTES),
        name="share_sum",
    )(own, *others)


def pick_rows(position_row, block):
    rows = position_row.shape[1]
    wanted = lax.broadcasted_iota(jnp.int32, (BLK, rows), 0) + block * BLK
    return jnp.where(position_row == wanted, 1.0, 0.0).astype(BF16)


def early_kernel(count, pairs_ref, place_ref, position_ref, *refs):
    pieces, out_ref = refs[:-1], refs[-1]
    for s in range(count):
        block = pairs_ref[s // 2, s % 2]
        total = None
        for i, piece in enumerate(pieces):
            pick = pick_rows(position_ref[place_ref[i]], block)
            term = jnp.dot(pick, piece[...], preferred_element_type=F32)
            total = term if total is None else total + term
        out_ref[s] = total


def early_rows(pairs, place, position, pieces):
    count = pairs.shape[0] * 2
    width = pieces[0].shape[1]
    return pl.pallas_call(
        functools.partial(early_kernel, count),
        out_shape=jax.ShapeDtypeStruct((count, BLK, width), F32),
        grid_spec=pltpu.PrefetchScalarGridSpec(
            num_scalar_prefetch=2,
            grid=(1,),
            in_specs=[whole_spec(position.shape)] + [whole_spec(p.shape) for p in pieces],
            out_specs=whole_spec((count, BLK, width)),
        ),
        compiler_params=params(),
        name="early_rows",
    )(pairs, place, position, *pieces)


def cross_kernel(components, pairs_ref, place_ref, position_ref, weights_ref, early_ref, *refs):
    pieces, (out_ref, left_ref, right_ref) = refs[:-3], refs[-3:]
    q = pl.program_id(0)
    columns = weights_ref.shape[1]
    for side, rows_ref in ((0, left_ref), (1, right_ref)):
        block = pairs_ref[q, side]
        total = early_ref[side]
        for i, piece in enumerate(pieces):
            pick = pick_rows(position_ref[place_ref[i]], block)
            total = total + jnp.dot(pick, piece[...], preferred_element_type=F32)
        for c in range(components):
            rows_ref[pl.ds(c, BLK, stride=components), :] = total[:, c * columns : (c + 1) * columns]
    scaled = (left_ref[...] * weights_ref[...]).astype(BF16)
    right = right_ref[...]
    lane = lax.broadcasted_iota(jnp.int32, right.shape, 1)
    turned = pltpu.roll(right, columns // 2, 1)
    turned = jnp.where(lane < columns // 2, -turned, turned)
    for part, other in ((0, right), (1, turned)):
        out_ref[0, part] = lax.dot_general(
            scaled, other.astype(BF16), (((1,), (1,)), ((), ())), preferred_element_type=F32
        ).astype(BF16)


def cross(pairs, place, position, weights, early, pieces, components):
    count = pairs.shape[0]
    columns = weights.shape[1]
    rows = BLK * components
    return pl.pallas_call(
        functools.partial(cross_kernel, components),
        out_shape=jax.ShapeDtypeStruct((count, 2, rows, rows), BF16),
        grid_spec=pltpu.PrefetchScalarGridSpec(
            num_scalar_prefetch=2,
            grid=(count,),
            in_specs=[
                whole_spec(position.shape),
                whole_spec(weights.shape),
                pl.BlockSpec((2,) + early.shape[1:], lambda i, *_: (i, 0, 0)),
            ]
            + [whole_spec(p.shape) for p in pieces],
            out_specs=pl.BlockSpec((1, 2, rows, rows), lambda i, *_: (i, 0, 0, 0)),
            scratch_shapes=[pltpu.VMEM((rows, columns), F32)] * 2,
        ),
        compiler_params=params(),
        name="cross",
    )(pairs, place, position, weights, early, *pieces)


def shards(influence, loads, patch_order, spectral_weights, block_position, block_pairs):
    components, hot_rows, patch_cols = influence.shape
    n_patch, n_hot = lax.axis_size("patch"), lax.axis_size("hot")
    patch_index, hot_index = lax.axis_index("patch"), lax.axis_index("hot")
    share_rows = hot_rows // n_patch
    weights = jnp.concatenate([spectral_weights, spectral_weights])[None, :]
    order = patch_order.reshape(n_patch, patch_cols // LANES, LANES)

    def swap(array, axis, k):
        size = lax.axis_size(axis)
        return lax.ppermute(array, axis, [(i, i ^ k) for i in range(size)])

    index = patch_index ^ jnp.arange(n_patch, dtype=jnp.int32)
    far = list(range(n_patch - 1, n_patch // 2 - 1, -1))
    near = list(range(n_patch // 2 - 1, -1, -1))
    far_terms, my_loads = first_products(index, order, loads, influence, share_rows, far)
    near_terms = more_products(
        index, my_loads, influence, share_rows, near, [BF16] * (len(near) - 1) + [F32]
    )
    received = [swap(t, "patch", k) for k, t in zip(far + near, list(far_terms) + list(near_terms[:-1]))]
    own = share_sum(near_terms[-1], received)

    column = {(0, k): swap(own, "patch", k) if k else own for k in [0] + far + near[:-1]}
    chips = [2 * i for i in range(n_hot // 2)]
    plane = {(j, k): swap(column[0, k], "hot", j) if j else column[0, k] for j in chips for k in range(n_patch)}
    pieces = dict(plane)
    pieces.update({(j + 1, k): swap(piece, "hot", 1) for (j, k), piece in plane.items()})
    late_keys = [(j, k) for j, k in pieces if j >= 2 and k in far]
    early_keys = [key for key in pieces if key not in late_keys]
    position = block_position.reshape(n_hot * n_patch, 1, share_rows)

    def places(keys):
        return jnp.stack([(hot_index ^ j) * n_patch + (patch_index ^ k) for j, k in keys])

    early = early_rows(block_pairs, places(early_keys), position, [pieces[key] for key in early_keys])
    return cross(
        block_pairs, places(late_keys), position, weights, early,
        [pieces[key] for key in late_keys], components,
    )


def solution(mesh):
    placed = (
        P(None, "hot", "patch"),
        P("grp", None),
        P(),
        P("grp"),
        P(),
        P(("hot", "patch"), None),
    )
    return jax.shard_map(
        shards,
        mesh=mesh,
        in_specs=placed,
        out_specs=P(("grp", "hot", "patch"), None, None, None),
        check_vma=False,
    )
```

time: 149 us -> 73.7 us (0.49)
  local copies, waits for them, and re-layouts: 47.7 us -> 2.13 us
  waiting for transfers between devices: 66 us -> 33.2 us
  Pallas kernels: 0 us -> 22.9 us
  starting transfers between devices: 0.04 us -> 15 us
  between operations: 13.6 us -> 0.09 us
  other arithmetic: 12.8 us -> 0.15 us
  matrix products: 8.3 us -> 0 us
    reduce_scatter x1 -> x0, waiting for transfers between devices: 38.1 us -> none  [shards(): lax.psum_scatter(partial_term.reshape(share_rows * lax.axis_size('patch')...]
    ppermute x0 -> x18, waiting for transfers between devices: none -> 33.2 us  [swap(): return lax.ppermute(array, axis, [(i, i ^ k) for i in range(size)])]
    gather x4 -> x0, local copies, waits for them, and re-layouts: 29.4 us -> none  [the longest x1 19 us: block_order(): return jnp.take(gathered, inverse, axis=0)]
    all_gather x1 -> x0, waiting for transfers between devices: 27.8 us -> none  [shards(): lax.all_gather(stress_share, ('hot', 'patch'), axis=0, tiled=True)]
    pallas_call x0 -> x5, Pallas kernels: none -> 22.9 us  [the longest x1 7.34 us: first_products(): pl.pallas_call(gather_kernel, out_shape=[share] * len(which) + [jax.Shape...]
    scatter x1 -> x0, local copies, waits for them, and re-layouts: 15.5 us -> none  [block_order(): inverse = jnp.zeros((hotspots,), jnp.int32).at[block_position].set(jnp.ar...]
    ppermute x0 -> x18, starting transfers between devices: none -> 15 us  [swap(): return lax.ppermute(array, axis, [(i, i ^ k) for i in range(size)])]
    dot_general x7 -> x0, matrix products: 8.3 us -> none  [the longest x1 5.24 us: shards(): jnp.einsum('chp,pf->hcf', influence, my_loads, preferred_element_type=jnp...]
  transfers between devices with their start and end apart: 2 -> 18, of which waited for: 2 -> 8; matrix products, arithmetic and copies ran while one was open for 11% -> 0% of each run, Pallas kernels for 0% -> 12%
where the time goes in v1:
time: 73.7 us; the launch traced here: 73.5 us
  waiting for transfers between devices  33.2 us (45%)
  Pallas kernels  22.9 us (31%)
  starting transfers between devices  15 us (20%)
  local copies, waits for them, and re-layouts  2.13 us (3%)
    ppermute x18, waiting for transfers between devices, swap(): return lax.ppermute(array, axis, [(i, i ^ k) for i in range(size)])  33.2 us
    ppermute x18, starting transfers between devices, swap(): return lax.ppermute(array, axis, [(i, i ^ k) for i in range(size)])  15 us
    pallas_call x1, Pallas kernels, first_products(): pl.pallas_call(gather_kernel, out_shape=[share] * len(which) + [jax.Shape...  7.34 us
    pallas_call x1, Pallas kernels, cross(): pl.pallas_call(functools.partial(cross_kernel, components), out_shape=jax...  6.41 us
    pallas_call x1, Pallas kernels, early_rows(): pl.pallas_call(functools.partial(early_kernel, count), out_shape=jax.Shap...  5.65 us
    pallas_call x1, Pallas kernels, more_products(): pl.pallas_call(product_kernel, out_shape=[jax.ShapeDtypeStruct(shape, kin...  3.42 us
    unnamed x11, local copies, waits for them, and re-layouts  2.04 us
  transfers between devices with their start and end apart: 18, of which 8 were waited for; matrix products, arithmetic and copies ran while one was open for 0% of the time, Pallas kernels for 12%

profile of v1, /device:TPU:0, one launch (start us, length us, event | category | flops | bytes accessed | tf_op | source)
XLA Modules:
  0.0 73.5 jit_solution(613003619125127356)
XLA Ops:
  0.0 1.2 %copy-done = bf16[4096,128]{1,0:T(8,128)(2,1)S(1)} copy-done((bf16[4096,128]{1,0:T(8,128)(2,1)S(1)}, bf16[4096,128]{1,0:T(8,128)(2,1)}, u32[]{:S(2)}) %copy-start) | copy-done | bytes 1048600
  1.2 0.7 copy-done.2
  1.9 7.3 %first_products.1 = (bf16[256,384]{1,0:T(8,128)(2,1)S(1)}, bf16[256,384]{1,0:T(8,128)(2,1)S(1)}, bf16[1024,128]{1,0:T(8,128)(2,1)S(1)}) custom-call(s32[4]{0:T(128)S(1)} %iota_xor_fusion.index_ref, s32[4,8,128]{2,1,0:T(8,128)S(1)} %bitcast.22, bf16[4096,128]{1,0:T(8,128)(2,1)S(1)} %copy-done, bf16[3,1024,1024]{2,1,0:T(8,128)(2,1)} %refs_1_.3, ...), custom_call_target="tpu_custom_call" | custom-call | tf_op jit(solution)/shard_map/first_products/pallas_call | solution.py:73
  9.3 5.1 %collective-permute-start = (bf16[256,384]{1,0:T(8,128)(2,1)S(1)}, bf16[256,384]{1,0:T(8,128)(2,1)S(1)}, u32[]{:S(2)}, u32[]{:S(2)}) collective-permute-start(bf16[256,384]{1,0:T(8,128)(2,1)S(1)} %get-tuple-element.12), channel_id=1, source_target_pairs={{0,3},{1,2},{2,1},{3,0},{4,7},{5,6},{6,5},{7,4},{8,11},{9,10},{10,... | collective-permute-start | bytes 589832 | tf_op jit(solution)/shard_map/ppermute | solution.py:222
  14.4 3.4 %more_products.1 = (bf16[256,384]{1,0:T(8,128)(2,1)S(1)}, f32[256,384]{1,0:T(8,128)S(1)}) custom-call(s32[4]{0:T(128)S(1)} %iota_xor_fusion.index_ref, bf16[1024,128]{1,0:T(8,128)(2,1)S(1)} %get-tuple-element.10.my_loads_ref, bf16[3,1024,1024]{2,1,0:T(8,128)(2,1)} %refs_1_.3, bf16[3,1024,1024]{2,1,0:T(8,128)(2,1)} %refs_1_.3), custom_call_target="tpu_custom_call" | custom-call | tf_op jit(solution)/shard_map/more_products/pallas_call | solution.py:99
  17.8 0.7 collective-permute-start.2
  18.5 1.7 %collective-permute-done.refs_0_ = bf16[256,384]{1,0:T(8,128)(2,1)S(1)} collective-permute-done((bf16[256,384]{1,0:T(8,128)(2,1)S(1)}, bf16[256,384]{1,0:T(8,128)(2,1)S(1)}, u32[]{:S(2)}, u32[]{:S(2)}) %collective-permute-start) | collective-permute-done | bytes 196640 | tf_op jit(solution)/shard_map/ppermute | solution.py:222
  20.2 10.9 %collective-permute-done.1.refs_1_ = bf16[256,384]{1,0:T(8,128)(2,1)S(1)} collective-permute-done((bf16[256,384]{1,0:T(8,128)(2,1)S(1)}, bf16[256,384]{1,0:T(8,128)(2,1)S(1)}, u32[]{:S(2)}, u32[]{:S(2)}) %collective-permute-start.1) | collective-permute-done | bytes 196640 | tf_op jit(solution)/shard_map/ppermute | solution.py:222
  31.1 0.1 share_sum.1.refs_0_
  31.2 1.6 %collective-permute-start.6 = (bf16[256,384]{1,0:T(8,128)(2,1)S(1)}, bf16[256,384]{1,0:T(8,128)(2,1)S(1)}, u32[]{:S(2)}, u32[]{:S(2)}) collective-permute-start(bf16[256,384]{1,0:T(8,128)(2,1)S(1)} %share_sum.1.refs_0_), channel_id=1, source_target_pairs={{0,8},{4,12},{8,0},{12,4},{1,9},{5,13},{9,1},{13,5},{2,10},{6,14},... | collective-permute-start | bytes 589832 | tf_op jit(solution)/shard_map/ppermute | solution.py:222
  32.8 2.5 %collective-permute-start.5 = (bf16[256,384]{1,0:T(8,128)(2,1)S(1)}, bf16[256,384]{1,0:T(8,128)(2,1)S(1)}, u32[]{:S(2)}, u32[]{:S(2)}) collective-permute-start(bf16[256,384]{1,0:T(8,128)(2,1)S(1)} %share_sum.1.refs_0_), channel_id=1, source_target_pairs={{0,3},{1,2},{2,1},{3,0},{4,7},{5,6},{6,5},{7,4},{8,11},{9,10},{10,... | collective-permute-start | bytes 589832 | tf_op jit(solution)/shard_map/ppermute | solution.py:222
  35.2 1.9 %collective-permute-start.3 = (bf16[256,384]{1,0:T(8,128)(2,1)S(1)}, bf16[256,384]{1,0:T(8,128)(2,1)S(1)}, u32[]{:S(2)}, u32[]{:S(2)}) collective-permute-start(bf16[256,384]{1,0:T(8,128)(2,1)S(1)} %share_sum.1.refs_0_), channel_id=1, source_target_pairs={{0,1},{1,0},{2,3},{3,2},{4,5},{5,4},{6,7},{7,6},{8,9},{9,8},{10,11... | collective-permute-start | bytes 589832 | tf_op jit(solution)/shard_map/ppermute | solution.py:222
  37.2 5.3 %collective-permute-done.5.refs_3_ = bf16[256,384]{1,0:T(8,128)(2,1)S(1)} collective-permute-done((bf16[256,384]{1,0:T(8,128)(2,1)S(1)}, bf16[256,384]{1,0:T(8,128)(2,1)S(1)}, u32[]{:S(2)}, u32[]{:S(2)}) %collective-permute-start.5) | collective-permute-done | bytes 196640 | tf_op jit(solution)/shard_map/ppermute | solution.py:222
  42.5 0.5 collective-permute-start.15
  43.1 7.1 %collective-permute-done.4.refs_2_ = bf16[256,384]{1,0:T(8,128)(2,1)S(1)} collective-permute-done((bf16[256,384]{1,0:T(8,128)(2,1)S(1)}, bf16[256,384]{1,0:T(8,128)(2,1)S(1)}, u32[]{:S(2)}, u32[]{:S(2)}) %collective-permute-start.4) | collective-permute-done | bytes 196640 | tf_op jit(solution)/shard_map/ppermute | solution.py:222
  50.2 0.5 collective-permute-start.14
  50.7 1.5 %collective-permute-start.7 = (bf16[256,384]{1,0:T(8,128)(2,1)S(1)}, bf16[256,384]{1,0:T(8,128)(2,1)S(1)}, u32[]{:S(2)}, u32[]{:S(2)}) collective-permute-start(bf16[256,384]{1,0:T(8,128)(2,1)S(1)} %collective-permute-done.3.refs_1_), channel_id=1, source_target_pairs={{0,8},{4,12},{8,0},{12,4},{1,9},{5,13},{9,1},{13,5},{2,10},{6,14},... | collective-permute-start | bytes 589832 | tf_op jit(solution)/shard_map/ppermute | solution.py:222
  52.2 0.1 copy.8.pairs_ref
  52.5 0.5 collective-permute-start.9
  53.1 4.8 %collective-permute-done.14.refs_0_ = bf16[256,384]{1,0:T(8,128)(2,1)S(1)} collective-permute-done((bf16[256,384]{1,0:T(8,128)(2,1)S(1)}, bf16[256,384]{1,0:T(8,128)(2,1)S(1)}, u32[]{:S(2)}, u32[]{:S(2)}) %collective-permute-start.14) | collective-permute-done | bytes 196640 | tf_op jit(solution)/shard_map/ppermute | solution.py:222
  57.9 2.1 %collective-permute-done.7.refs_5_ = bf16[256,384]{1,0:T(8,128)(2,1)S(1)} collective-permute-done((bf16[256,384]{1,0:T(8,128)(2,1)S(1)}, bf16[256,384]{1,0:T(8,128)(2,1)S(1)}, u32[]{:S(2)}, u32[]{:S(2)}) %collective-permute-start.7) | collective-permute-done | bytes 196640 | tf_op jit(solution)/shard_map/ppermute | solution.py:222
  60.1 1.3 %collective-permute-done.13.refs_11_ = bf16[256,384]{1,0:T(8,128)(2,1)S(1)} collective-permute-done((bf16[256,384]{1,0:T(8,128)(2,1)S(1)}, bf16[256,384]{1,0:T(8,128)(2,1)S(1)}, u32[]{:S(2)}, u32[]{:S(2)}) %collective-permute-start.13) | collective-permute-done | bytes 196640 | tf_op jit(solution)/shard_map/ppermute | solution.py:222
  61.4 5.7 %early_rows.1.early_ref = f32[6,256,384]{2,1,0:T(8,128)S(1)} custom-call(s32[3,2]{1,0:T(4,128)S(1)} %copy.8.pairs_ref, s32[12]{0:T(128)S(1)} %stack.71.place_ref, s32[16,1,256]{2,1,0:T(1,128)S(1)} %bitcast.20, bf16[256,384]{1,0:T(8,128)(2,1)S(1)} %share_sum.1.refs_0_, bf16[256,384]{1,0:T(8,128)(2,1)S(1)} %collective-permute-done.3.refs_1_, ...), custom_call_target="tpu_custom_call" | custom-call | tf_op jit(solution)/shard_map/early_rows/pallas_call | solution.py:151
  67.1 6.4 %cross.1 = bf16[3,2,768,768]{3,2,1,0:T(8,128)(2,1)} custom-call(s32[3,2]{1,0:T(4,128)S(1)} %copy.8.pairs_ref, s32[4]{0:T(128)S(1)} %pad_add_fusion.place_ref, s32[16,1,256]{2,1,0:T(1,128)S(1)} %bitcast.21, f32[1,128]{1,0:T(1,128)S(1)} %maximum_bitcast_fusion.weights_ref, f32[6,256,384]{2,1,0:T(8,128)S(1)} %early_rows.1.early_ref, ...), custom_call_target="tpu_custom_call" | custom-call | tf_op jit(solution)/shard_map/cross/pallas_call | solution.py:192
  (32 shorter events, 0.5 us)
Async XLA Ops:
  0.0 1.2 %copy-start = (bf16[4096,128]{1,0:T(8,128)(2,1)S(1)}, bf16[4096,128]{1,0:T(8,128)(2,1)}, u32[]{:S(2)}) copy-start(bf16[4096,128]{1,0:T(8,128)(2,1)} %loads_ref.1) | copy-start | bytes 3145732
  1.2 0.7 copy-start.2
  9.3 10.9 %collective-permute-start = (bf16[256,384]{1,0:T(8,128)(2,1)S(1)}, bf16[256,384]{1,0:T(8,128)(2,1)S(1)}, u32[]{:S(2)}, u32[]{:S(2)}) collective-permute-start(bf16[256,384]{1,0:T(8,128)(2,1)S(1)} %get-tuple-element.12), channel_id=1, source_target_pairs={{0,3},{1,2},{2,1},{3,0},{4,7},{5,6},{6,5},{7,4},{8,11},{9,10},{10,... | collective-permute-start | bytes 589832 | tf_op jit(solution)/shard_map/ppermute | solution.py:222
  14.4 16.7 %collective-permute-start.1 = (bf16[256,384]{1,0:T(8,128)(2,1)S(1)}, bf16[256,384]{1,0:T(8,128)(2,1)S(1)}, u32[]{:S(2)}, u32[]{:S(2)}) collective-permute-start(bf16[256,384]{1,0:T(8,128)(2,1)S(1)} %get-tuple-element.13), channel_id=1, source_target_pairs={{0,2},{1,3},{2,0},{3,1},{4,6},{5,7},{6,4},{7,5},{8,10},{9,11},{10,... | collective-permute-start | bytes 589832 | tf_op jit(solution)/shard_map/ppermute | solution.py:222
  14.4 37.8 %copy-start.3 = (s32[3,2]{0,1:T(2,128)S(1)}, s32[3,2]{0,1:T(2,128)}, u32[]{:S(2)}) copy-start(s32[3,2]{0,1:T(2,128)} %param.11) | copy-start | bytes 76
  14.4 45.6 %copy-start.4 = (f32[64]{0:T(128)S(1)}, f32[64]{0:T(128)}, u32[]{:S(2)}) copy-start(f32[64]{0:T(128)} %param.9) | copy-start | bytes 772
  14.4 47.0 %copy-start.1 = (s32[4096]{0:T(1024)S(1)}, s32[4096]{0:T(1024)}, u32[]{:S(2)}) copy-start(s32[4096]{0:T(1024)} %param.10) | copy-start | bytes 49156
  17.8 13.3 %collective-permute-start.2 = (bf16[256,384]{1,0:T(8,128)(2,1)S(1)}, bf16[256,384]{1,0:T(8,128)(2,1)S(1)}, u32[]{:S(2)}, u32[]{:S(2)}) collective-permute-start(bf16[256,384]{1,0:T(8,128)(2,1)S(1)} %get-tuple-element.14), channel_id=1, source_target_pairs={{0,1},{1,0},{2,3},{3,2},{4,5},{5,4},{6,7},{7,6},{8,9},{9,8},{10,11... | collective-permute-start | bytes 589832 | tf_op jit(solution)/shard_map/ppermute | solution.py:222
  31.2 6.0 %collective-permute-start.6 = (bf16[256,384]{1,0:T(8,128)(2,1)S(1)}, bf16[256,384]{1,0:T(8,128)(2,1)S(1)}, u32[]{:S(2)}, u32[]{:S(2)}) collective-permute-start(bf16[256,384]{1,0:T(8,128)(2,1)S(1)} %share_sum.1.refs_0_), channel_id=1, source_target_pairs={{0,8},{4,12},{8,0},{12,4},{1,9},{5,13},{9,1},{13,5},{2,10},{6,14},... | collective-permute-start | bytes 589832 | tf_op jit(solution)/shard_map/ppermute | solution.py:222
  32.8 9.8 %collective-permute-start.5 = (bf16[256,384]{1,0:T(8,128)(2,1)S(1)}, bf16[256,384]{1,0:T(8,128)(2,1)S(1)}, u32[]{:S(2)}, u32[]{:S(2)}) collective-permute-start(bf16[256,384]{1,0:T(8,128)(2,1)S(1)} %share_sum.1.refs_0_), channel_id=1, source_target_pairs={{0,3},{1,2},{2,1},{3,0},{4,7},{5,6},{6,5},{7,4},{8,11},{9,10},{10,... | collective-permute-start | bytes 589832 | tf_op jit(solution)/shard_map/ppermute | solution.py:222
  35.2 7.8 %collective-permute-start.8 = (bf16[256,384]{1,0:T(8,128)(2,1)S(1)}, bf16[256,384]{1,0:T(8,128)(2,1)S(1)}, u32[]{:S(2)}, u32[]{:S(2)}) collective-permute-start(bf16[256,384]{1,0:T(8,128)(2,1)S(1)} %share_sum.1.refs_0_), channel_id=1, source_target_pairs={{0,4},{4,0},{8,12},{12,8},{1,5},{5,1},{9,13},{13,9},{2,6},{6,2},{1... | collective-permute-start | bytes 589832 | tf_op jit(solution)/shard_map/ppermute | solution.py:222
  35.2 14.9 %collective-permute-start.4 = (bf16[256,384]{1,0:T(8,128)(2,1)S(1)}, bf16[256,384]{1,0:T(8,128)(2,1)S(1)}, u32[]{:S(2)}, u32[]{:S(2)}) collective-permute-start(bf16[256,384]{1,0:T(8,128)(2,1)S(1)} %share_sum.1.refs_0_), channel_id=1, source_target_pairs={{0,2},{1,3},{2,0},{3,1},{4,6},{5,7},{6,4},{7,5},{8,10},{9,11},{10,... | collective-permute-start | bytes 589832 | tf_op jit(solution)/shard_map/ppermute | solution.py:222
  35.2 15.5 %collective-permute-start.3 = (bf16[256,384]{1,0:T(8,128)(2,1)S(1)}, bf16[256,384]{1,0:T(8,128)(2,1)S(1)}, u32[]{:S(2)}, u32[]{:S(2)}) collective-permute-start(bf16[256,384]{1,0:T(8,128)(2,1)S(1)} %share_sum.1.refs_0_), channel_id=1, source_target_pairs={{0,1},{1,0},{2,3},{3,2},{4,5},{5,4},{6,7},{7,6},{8,9},{9,8},{10,11... | collective-permute-start | bytes 589832 | tf_op jit(solution)/shard_map/ppermute | solution.py:222
  37.2 15.2 %collective-permute-start.12 = (bf16[256,384]{1,0:T(8,128)(2,1)S(1)}, bf16[256,384]{1,0:T(8,128)(2,1)S(1)}, u32[]{:S(2)}, u32[]{:S(2)}) collective-permute-start(bf16[256,384]{1,0:T(8,128)(2,1)S(1)} %collective-permute-done.6.refs_4_), channel_id=1, source_target_pairs={{0,4},{4,0},{8,12},{12,8},{1,5},{5,1},{9,13},{13,9},{2,6},{6,2},{1... | collective-permute-start | bytes 589832 | tf_op jit(solution)/shard_map/ppermute | solution.py:222
  42.5 9.9 %collective-permute-start.15 = (bf16[256,384]{1,0:T(8,128)(2,1)S(1)}, bf16[256,384]{1,0:T(8,128)(2,1)S(1)}, u32[]{:S(2)}, u32[]{:S(2)}) collective-permute-start(bf16[256,384]{1,0:T(8,128)(2,1)S(1)} %collective-permute-done.5.refs_3_), channel_id=1, source_target_pairs={{0,8},{4,12},{8,0},{12,4},{1,9},{5,13},{9,1},{13,5},{2,10},{6,14},... | collective-permute-start | bytes 589832 | tf_op jit(solution)/shard_map/ppermute | solution.py:222
  43.1 9.9 %collective-permute-start.11 = (bf16[256,384]{1,0:T(8,128)(2,1)S(1)}, bf16[256,384]{1,0:T(8,128)(2,1)S(1)}, u32[]{:S(2)}, u32[]{:S(2)}) collective-permute-start(bf16[256,384]{1,0:T(8,128)(2,1)S(1)} %collective-permute-done.5.refs_3_), channel_id=1, source_target_pairs={{0,4},{4,0},{8,12},{12,8},{1,5},{5,1},{9,13},{13,9},{2,6},{6,2},{1... | collective-permute-start | bytes 589832 | tf_op jit(solution)/shard_map/ppermute | solution.py:222
  50.2 7.7 %collective-permute-start.14 = (bf16[256,384]{1,0:T(8,128)(2,1)S(1)}, bf16[256,384]{1,0:T(8,128)(2,1)S(1)}, u32[]{:S(2)}, u32[]{:S(2)}) collective-permute-start(bf16[256,384]{1,0:T(8,128)(2,1)S(1)} %collective-permute-done.4.refs_2_), channel_id=1, source_target_pairs={{0,8},{4,12},{8,0},{12,4},{1,9},{5,13},{9,1},{13,5},{2,10},{6,14},... | collective-permute-start | bytes 589832 | tf_op jit(solution)/shard_map/ppermute | solution.py:222
  50.7 9.3 %collective-permute-start.7 = (bf16[256,384]{1,0:T(8,128)(2,1)S(1)}, bf16[256,384]{1,0:T(8,128)(2,1)S(1)}, u32[]{:S(2)}, u32[]{:S(2)}) collective-permute-start(bf16[256,384]{1,0:T(8,128)(2,1)S(1)} %collective-permute-done.3.refs_1_), channel_id=1, source_target_pairs={{0,8},{4,12},{8,0},{12,4},{1,9},{5,13},{9,1},{13,5},{2,10},{6,14},... | collective-permute-start | bytes 589832 | tf_op jit(solution)/shard_map/ppermute | solution.py:222
  52.4 7.7 %collective-permute-start.10 = (bf16[256,384]{1,0:T(8,128)(2,1)S(1)}, bf16[256,384]{1,0:T(8,128)(2,1)S(1)}, u32[]{:S(2)}, u32[]{:S(2)}) collective-permute-start(bf16[256,384]{1,0:T(8,128)(2,1)S(1)} %collective-permute-done.4.refs_2_), channel_id=1, source_target_pairs={{0,4},{4,0},{8,12},{12,8},{1,5},{5,1},{9,13},{13,9},{2,6},{6,2},{1... | collective-permute-start | bytes 589832 | tf_op jit(solution)/shard_map/ppermute | solution.py:222
  52.5 7.6 %collective-permute-start.9 = (bf16[256,384]{1,0:T(8,128)(2,1)S(1)}, bf16[256,384]{1,0:T(8,128)(2,1)S(1)}, u32[]{:S(2)}, u32[]{:S(2)}) collective-permute-start(bf16[256,384]{1,0:T(8,128)(2,1)S(1)} %collective-permute-done.3.refs_1_), channel_id=1, source_target_pairs={{0,4},{4,0},{8,12},{12,8},{1,5},{5,1},{9,13},{13,9},{2,6},{6,2},{1... | collective-permute-start | bytes 589832 | tf_op jit(solution)/shard_map/ppermute | solution.py:222
  53.0 14.1 %collective-permute-start.17 = (bf16[256,384]{1,0:T(8,128)(2,1)S(1)}, bf16[256,384]{1,0:T(8,128)(2,1)S(1)}, u32[]{:S(2)}, u32[]{:S(2)}) collective-permute-start(bf16[256,384]{1,0:T(8,128)(2,1)S(1)} %collective-permute-done.15.refs_1_), channel_id=1, source_target_pairs={{0,4},{4,0},{8,12},{12,8},{1,5},{5,1},{9,13},{13,9},{2,6},{6,2},{1... | collective-permute-start | bytes 589832 | tf_op jit(solution)/shard_map/ppermute | solution.py:222
  57.8 9.2 %collective-permute-start.16 = (bf16[256,384]{1,0:T(8,128)(2,1)S(1)}, bf16[256,384]{1,0:T(8,128)(2,1)S(1)}, u32[]{:S(2)}, u32[]{:S(2)}) collective-permute-start(bf16[256,384]{1,0:T(8,128)(2,1)S(1)} %collective-permute-done.14.refs_0_), channel_id=1, source_target_pairs={{0,4},{4,0},{8,12},{12,8},{1,5},{5,1},{9,13},{13,9},{2,6},{6,2},{1... | collective-permute-start | bytes 589832 | tf_op jit(solution)/shard_map/ppermute | solution.py:222
  60.0 1.4 %collective-permute-start.13 = (bf16[256,384]{1,0:T(8,128)(2,1)S(1)}, bf16[256,384]{1,0:T(8,128)(2,1)S(1)}, u32[]{:S(2)}, u32[]{:S(2)}) collective-permute-start(bf16[256,384]{1,0:T(8,128)(2,1)S(1)} %collective-permute-done.7.refs_5_), channel_id=1, source_target_pairs={{0,4},{4,0},{8,12},{12,8},{1,5},{5,1},{9,13},{13,9},{2,6},{6,2},{1... | collective-permute-start | bytes 589832 | tf_op jit(solution)/shard_map/ppermute | solution.py:222

commit v2 on v1

v2 whole, which is shorter than its diff:
```python
import functools
import math

import jax
import jax.numpy as jnp
from jax import lax
from jax.experimental import pallas as pl
from jax.experimental.pallas import tpu as pltpu
from jax.sharding import PartitionSpec as P

BLK = 256
LANES = 128
F32 = jnp.float32
BF16 = jnp.bfloat16
VMEM_BYTES = 48 * 1024 * 1024
FIRST_VMEM_BYTES = 125 * 512 * 1024


def params(steps=1):
    return pltpu.CompilerParams(
        dimension_semantics=("arbitrary",) * steps, vmem_limit_bytes=VMEM_BYTES
    )


def cost(flops, bytes_accessed):
    return pl.CostEstimate(flops=flops, bytes_accessed=bytes_accessed, transcendentals=0)


def products(influence, my_loads, out_refs):
    shares, components, rows, patch_cols = influence.shape
    columns = my_loads.shape[1]
    part = jnp.dot(
        influence.reshape(shares * components * rows, patch_cols), my_loads,
        preferred_element_type=F32,
    )
    for i, out_ref in enumerate(out_refs):
        for c in range(components):
            top = (i * components + c) * rows
            out_ref[:, c * columns : (c + 1) * columns] = part[top : top + rows].astype(out_ref.dtype)


def share_copies(influence_ref, held_ref, sems, which):
    rows = held_ref.shape[2]
    here = lax.axis_index("patch")
    return [
        pltpu.make_async_copy(
            influence_ref.at[:, pl.ds(pl.multiple_of((here ^ k) * rows, rows), rows), :],
            held_ref.at[i],
            sems.at[i],
        )
        for i, k in enumerate(which)
    ]


def first_kernel(which, order_ref, loads_ref, influence_ref, *refs):
    out_refs, (my_loads_ref, own_order, column_ref, table, pick_ref, held, sems) = refs[:-7], refs[-7:]
    columns = loads_ref.shape[1]
    half = loads_ref.shape[0] // 2
    order_copy = pltpu.make_async_copy(order_ref.at[lax.axis_index("patch")], own_order, sems.at[0])
    low_copy = pltpu.make_async_copy(
        loads_ref.at[pl.ds(0, half)], table.at[:, pl.ds(0, columns)], sems.at[1]
    )
    high_copy = pltpu.make_async_copy(
        loads_ref.at[pl.ds(half, half)], table.at[:, pl.ds(columns, columns)], sems.at[2]
    )
    copies = share_copies(influence_ref, held, sems.at[pl.ds(3, len(which))], which)
    order_copy.start()
    low_copy.start()
    high_copy.start()
    for copy in copies:
        copy.start()
    order_copy.wait()
    lane = lax.broadcasted_iota(jnp.int32, (LANES, LANES), 1)
    for g in range(own_order.shape[0]):
        rows = slice(g * LANES, (g + 1) * LANES)
        wanted = jnp.transpose(jnp.broadcast_to(own_order[g : g + 1, :], (LANES, LANES)))
        column_ref[rows, :] = wanted
        wanted = jnp.where(wanted >= half, wanted - half, wanted) - lane
        for j in range(half // LANES):
            pick_ref[rows, j * LANES : (j + 1) * LANES] = jnp.where(
                wanted == j * LANES, 1.0, 0.0
            ).astype(BF16)
    low_copy.wait()
    high_copy.wait()
    both = jnp.dot(pick_ref[...], table[...], preferred_element_type=F32)
    my_loads_ref[...] = jnp.where(
        column_ref[...] >= half, both[:, columns:], both[:, :columns]
    ).astype(BF16)
    for copy in copies:
        copy.wait()
    products(held[...], my_loads_ref[...], out_refs)


def more_kernel(which, my_loads_ref, influence_ref, *refs):
    out_refs, (held, sems) = refs[:-2], refs[-2:]
    copies = share_copies(influence_ref, held, sems, which)
    for copy in copies:
        copy.start()
    for copy in copies:
        copy.wait()
    products(held[...], my_loads_ref[...], out_refs)


def vmem():
    return pl.BlockSpec(memory_space=pltpu.VMEM)


def hbm():
    return pl.BlockSpec(memory_space=pltpu.HBM)


def first_products(order, loads, influence, share_rows, which):
    components, _, patch_cols = influence.shape
    patches, columns = loads.shape
    share = jax.ShapeDtypeStruct((share_rows, components * columns), BF16)
    held = (len(which), components, share_rows, patch_cols)
    out = pl.pallas_call(
        functools.partial(first_kernel, which),
        out_shape=[share] * len(which) + [jax.ShapeDtypeStruct((patch_cols, columns), BF16)],
        in_specs=[hbm()] * 3,
        out_specs=[vmem()] * (len(which) + 1),
        scratch_shapes=[
            pltpu.VMEM(order.shape[1:], jnp.int32),
            pltpu.VMEM((patch_cols, columns), jnp.int32),
            pltpu.VMEM((patches // 2, 2 * columns), BF16),
            pltpu.VMEM((patch_cols, patches // 2), BF16),
            pltpu.VMEM(held, BF16),
            pltpu.SemaphoreType.DMA((3 + len(which),)),
        ],
        compiler_params=pltpu.CompilerParams(vmem_limit_bytes=FIRST_VMEM_BYTES),
        name="first_products",
    )(order, loads, influence)
    return out[:-1], out[-1]


def more_products(my_loads, influence, share_rows, which, kinds):
    components, _, patch_cols = influence.shape
    columns = my_loads.shape[1]
    shape = (share_rows, components * columns)
    held = (len(which), components, share_rows, patch_cols)
    return pl.pallas_call(
        functools.partial(more_kernel, which),
        out_shape=[jax.ShapeDtypeStruct(shape, kind) for kind in kinds],
        in_specs=[vmem(), hbm()],
        out_specs=[vmem()] * len(which),
        scratch_shapes=[pltpu.VMEM(held, BF16), pltpu.SemaphoreType.DMA((len(which),))],
        compiler_params=pltpu.CompilerParams(vmem_limit_bytes=VMEM_BYTES),
        cost_estimate=cost(8 * share_rows * components * columns * patch_cols, 8 * math.prod(held)),
        name="more_products",
    )(my_loads, influence)


def sum_kernel(own_ref, *refs):
    total = own_ref[...]
    for ref in refs[:-1]:
        total = total + ref[...].astype(F32)
    refs[-1][...] = total.astype(BF16)


def share_sum(own, others):
    return pl.pallas_call(
        sum_kernel,
        out_shape=jax.ShapeDtypeStruct(own.shape, BF16),
        compiler_params=pltpu.CompilerParams(vmem_limit_bytes=VMEM_BYTES),
        name="share_sum",
    )(own, *others)


def pick_rows(position_ref, key, block):
    n_patch = lax.axis_size("patch")
    place = (lax.axis_index("hot") ^ key[0]) * n_patch + (lax.axis_index("patch") ^ key[1])
    rows = position_ref.shape[2]
    wanted = lax.broadcasted_iota(jnp.int32, (BLK, rows), 0) + block * BLK
    return jnp.where(position_ref[place] == wanted, 1.0, 0.0).astype(BF16)


def early_kernel(keys, pairs_ref, position_ref, *refs):
    pieces, befores, out_ref = refs[: len(keys)], refs[len(keys) : -1], refs[-1]
    for s in range(out_ref.shape[0]):
        block = pairs_ref[s // 2, s % 2]
        total = befores[0][s] if befores else None
        for key, piece in zip(keys, pieces):
            pick = pick_rows(position_ref, key, block)
            term = jnp.dot(pick, piece[...], preferred_element_type=F32)
            total = term if total is None else total + term
        out_ref[s] = total


def early_rows(pairs, position, keys, pieces, before=()):
    count = pairs.shape[0] * 2
    rows, width = pieces[0].shape
    flops = 2 * count * BLK * rows * width * len(keys)
    return pl.pallas_call(
        functools.partial(early_kernel, keys),
        out_shape=jax.ShapeDtypeStruct((count, BLK, width), F32),
        in_specs=[pl.BlockSpec(memory_space=pltpu.SMEM)] + [vmem()] * (1 + len(pieces) + len(before)),
        out_specs=vmem(),
        compiler_params=pltpu.CompilerParams(vmem_limit_bytes=VMEM_BYTES),
        cost_estimate=cost(2 * flops, 8 * count * BLK * width),
        name="early_rows",
    )(pairs, position, *pieces, *before)


def cross_kernel(components, keys, pairs_ref, position_ref, weights_ref, early_ref, *refs):
    pieces, (out_ref, left_ref, right_ref) = refs[:-3], refs[-3:]
    q = pl.program_id(0)
    columns = weights_ref.shape[1]
    for side, rows_ref in ((0, left_ref), (1, right_ref)):
        block = pairs_ref[q, side]
        total = early_ref[side]
        for key, piece in zip(keys, pieces):
            pick = pick_rows(position_ref, key, block)
            total = total + jnp.dot(pick, piece[...], preferred_element_type=F32)
        for c in range(components):
            rows_ref[pl.ds(c, BLK, stride=components), :] = total[:, c * columns : (c + 1) * columns]
    scaled = (left_ref[...] * weights_ref[...]).astype(BF16)
    right = right_ref[...]
    lane = lax.broadcasted_iota(jnp.int32, right.shape, 1)
    turned = pltpu.roll(right, columns // 2, 1)
    turned = jnp.where(lane < columns // 2, -turned, turned)
    for part, other in ((0, right), (1, turned)):
        out_ref[0, part] = lax.dot_general(
            scaled, other.astype(BF16), (((1,), (1,)), ((), ())), preferred_element_type=F32
        ).astype(BF16)


def cross(pairs, position, weights, early, keys, pieces, components):
    count = pairs.shape[0]
    columns = weights.shape[1]
    rows = BLK * components
    return pl.pallas_call(
        functools.partial(cross_kernel, components, keys),
        out_shape=jax.ShapeDtypeStruct((count, 2, rows, rows), BF16),
        grid=(count,),
        in_specs=[
            pl.BlockSpec(memory_space=pltpu.SMEM),
            vmem(),
            vmem(),
            pl.BlockSpec((2,) + early.shape[1:], lambda i: (i, 0, 0)),
        ]
        + [vmem()] * len(pieces),
        out_specs=pl.BlockSpec((1, 2, rows, rows), lambda i: (i, 0, 0, 0)),
        scratch_shapes=[pltpu.VMEM((rows, columns), F32)] * 2,
        compiler_params=params(),
        name="cross",
    )(pairs, position, weights, early, *pieces)


def gather_plane(own, swap, n_patch, n_hot):
    plane = {(0, 0): own}
    bits = [1 << b for b in reversed(range((n_patch - 1).bit_length()))]
    for bit in bits:
        for _, k in list(plane):
            plane[0, k ^ bit] = swap(plane[0, k], "patch", bit)
    chip_bits = [2 << b for b in reversed(range((n_hot // 2 - 1).bit_length()))]
    for bit in chip_bits:
        for j, k in list(plane):
            if k != n_patch - 1:
                plane[j ^ bit, k] = swap(plane[j, k], "hot", bit)
    for j in range(2, n_hot, 2):
        plane[j, n_patch - 1] = swap(plane[j, 0], "patch", n_patch - 1)
    return plane


def shards(influence, loads, patch_order, spectral_weights, block_position, block_pairs):
    components, hot_rows, patch_cols = influence.shape
    n_patch, n_hot = lax.axis_size("patch"), lax.axis_size("hot")
    share_rows = hot_rows // n_patch
    weights = jnp.concatenate([spectral_weights, spectral_weights])[None, :]
    order = patch_order.reshape(n_patch, patch_cols // LANES, LANES)

    def swap(array, axis, k):
        size = lax.axis_size(axis)
        return lax.ppermute(array, axis, [(i, i ^ k) for i in range(size)])

    far = list(range(n_patch - 1, n_patch // 2 - 1, -1))
    near = list(range(n_patch // 2 - 1, -1, -1))
    far_terms, my_loads = first_products(order, loads, influence, share_rows, far)
    near_terms = more_products(
        my_loads, influence, share_rows, near, [BF16] * (len(near) - 1) + [F32]
    )
    received = [swap(t, "patch", k) for k, t in zip(far + near, list(far_terms) + list(near_terms[:-1]))]
    own = share_sum(near_terms[-1], received)

    plane = gather_plane(own, swap, n_patch, n_hot)
    pieces = dict(plane)
    pieces.update({(j + 1, k): swap(piece, "hot", 1) for (j, k), piece in plane.items()})
    position = block_position.reshape(n_hot * n_patch, 1, share_rows)
    late = [key for key in pieces if key[0] >= 2 and key[1] in far]
    first = [key for key in pieces if (key[0] < 2 and key[1] not in far) or key[1] == 0]
    second = [key for key in pieces if key not in late and key not in first]
    early = early_rows(block_pairs, position, first, [pieces[key] for key in first])
    early = early_rows(block_pairs, position, second, [pieces[key] for key in second], [early])
    return cross(
        block_pairs, position, weights, early, late, [pieces[key] for key in late], components
    )


def solution(mesh):
    placed = (
        P(None, "hot", "patch"),
        P("grp", None),
        P(),
        P("grp"),
        P(),
        P(("hot", "patch"), None),
    )
    return jax.shard_map(
        shards,
        mesh=mesh,
        in_specs=placed,
        out_specs=P(("grp", "hot", "patch"), None, None, None),
        check_vma=False,
    )
```

time: 73.7 us -> 70.2 us (0.953)
  waiting for transfers between devices: 33.2 us -> 27.3 us
  starting transfers between devices: 15 us -> 19.1 us
  local copies, waits for them, and re-layouts: 2.13 us -> 1.05 us
    ppermute x18, waiting for transfers between devices: 33.2 us -> 27.3 us  [swap(): return lax.ppermute(array, axis, [(i, i ^ k) for i in range(size)])]
    ppermute x18, starting transfers between devices: 15 us -> 19.1 us  [swap(): return lax.ppermute(array, axis, [(i, i ^ k) for i in range(size)])]
    unnamed x11 -> x9, local copies, waits for them, and re-layouts: 2.04 us -> 1.05 us
    pallas_call x4 -> x5, Pallas kernels: 22.8 us -> 22.2 us  [the longest x1 6.54 us: first_products(): pl.pallas_call(functools.partial(first_kernel, which), out_shape=[share]...]
  transfers between devices with their start and end apart: 18 -> 18, of which waited for: 8 -> 7; matrix products, arithmetic and copies ran while one was open for 0% -> 0% of each run, Pallas kernels for 12% -> 13%
where the time goes in v2:
time: 70.2 us; the launch traced here: 70 us
  waiting for transfers between devices  27.3 us (39%)
  Pallas kernels  22.3 us (32%)
  starting transfers between devices  19.1 us (27%)
  local copies, waits for them, and re-layouts  1.05 us (1%)
    ppermute x18, waiting for transfers between devices, swap(): return lax.ppermute(array, axis, [(i, i ^ k) for i in range(size)])  27.3 us
    ppermute x18, starting transfers between devices, swap(): return lax.ppermute(array, axis, [(i, i ^ k) for i in range(size)])  19.1 us
    pallas_call x1, Pallas kernels, first_products(): pl.pallas_call(functools.partial(first_kernel, which), out_shape=[share]...  6.54 us
    pallas_call x2, Pallas kernels, early_rows(): pl.pallas_call(functools.partial(early_kernel, keys), out_shape=jax.Shape...  6.41 us
    pallas_call x1, Pallas kernels, cross(): pl.pallas_call(functools.partial(cross_kernel, components, keys), out_sha...  6.4 us
    pallas_call x1, Pallas kernels, more_products(): pl.pallas_call(functools.partial(more_kernel, which), out_shape=[jax.Shap...  2.87 us
  transfers between devices with their start and end apart: 18, of which 7 were waited for; matrix products, arithmetic and copies ran while one was open for 0% of the time, Pallas kernels for 13%

profile of v2, /device:TPU:0, one launch (start us, length us, event | category | flops | bytes accessed | tf_op | source)
XLA Modules:
  0.0 70.0 jit_solution(8427878985066524747)
XLA Ops:
  0.0 6.5 %first_products.1 = (bf16[256,384]{1,0:T(8,128)(2,1)}, bf16[256,384]{1,0:T(8,128)(2,1)}, bf16[1024,128]{1,0:T(8,128)(2,1)}) custom-call(s32[4,8,128]{2,1,0:T(8,128)} %bitcast.7, bf16[4096,128]{1,0:T(8,128)(2,1)} %loads_ref.1, bf16[3,1024,1024]{2,1,0:T(8,128)(2,1)} %influence_ref.3), custom_call_target="tpu_custom_call" | custom-call | tf_op jit(solution)/shard_map/first_products/pallas_call | solution.py:117
  6.6 5.1 %collective-permute-start = (bf16[256,384]{1,0:T(8,128)(2,1)}, bf16[256,384]{1,0:T(8,128)(2,1)S(1)}, u32[]{:S(2)}, u32[]{:S(2)}) collective-permute-start(bf16[256,384]{1,0:T(8,128)(2,1)} %get-tuple-element.12), channel_id=1, source_target_pairs={{0,3},{1,2},{2,1},{3,0},{4,7},{5,6},{6,5},{7,4},{8,11},{9,10},{10,... | collective-permute-start | bytes 589832 | tf_op jit(solution)/shard_map/ppermute | solution.py:274
  11.7 0.9 %copy-done = bf16[1024,128]{1,0:T(8,128)(2,1)S(1)} copy-done((bf16[1024,128]{1,0:T(8,128)(2,1)S(1)}, bf16[1024,128]{1,0:T(8,128)(2,1)}, u32[]{:S(2)}) %copy-start) | copy-done | bytes 262168
  12.6 2.9 %more_products.1 = (bf16[256,384]{1,0:T(8,128)(2,1)S(1)}, f32[256,384]{1,0:T(8,128)S(1)}) custom-call(bf16[1024,128]{1,0:T(8,128)(2,1)S(1)} %copy-done, bf16[3,1024,1024]{2,1,0:T(8,128)(2,1)} %influence_ref.3), custom_call_target="tpu_custom_call" | custom-call | flops 805306368 | bytes 12582912 | tf_op jit(solution)/shard_map/more_products/pallas_call | solution.py:141
  15.5 0.7 %collective-permute-start.2 = (bf16[256,384]{1,0:T(8,128)(2,1)S(1)}, bf16[256,384]{1,0:T(8,128)(2,1)S(1)}, u32[]{:S(2)}, u32[]{:S(2)}) collective-permute-start(bf16[256,384]{1,0:T(8,128)(2,1)S(1)} %get-tuple-element.14), channel_id=1, source_target_pairs={{0,1},{1,0},{2,3},{3,2},{4,5},{5,4},{6,7},{7,6},{8,9},{9,8},{10,11... | collective-permute-start | bytes 589832 | tf_op jit(solution)/shard_map/ppermute | solution.py:274
  16.2 1.5 %collective-permute-done.refs_0_ = bf16[256,384]{1,0:T(8,128)(2,1)S(1)} collective-permute-done((bf16[256,384]{1,0:T(8,128)(2,1)}, bf16[256,384]{1,0:T(8,128)(2,1)S(1)}, u32[]{:S(2)}, u32[]{:S(2)}) %collective-permute-start) | collective-permute-done | bytes 196640 | tf_op jit(solution)/shard_map/ppermute | solution.py:274
  17.7 10.9 %collective-permute-done.1.refs_1_ = bf16[256,384]{1,0:T(8,128)(2,1)S(1)} collective-permute-done((bf16[256,384]{1,0:T(8,128)(2,1)}, bf16[256,384]{1,0:T(8,128)(2,1)S(1)}, u32[]{:S(2)}, u32[]{:S(2)}) %collective-permute-start.1) | collective-permute-done | bytes 196640 | tf_op jit(solution)/shard_map/ppermute | solution.py:274
  28.6 0.1 share_sum.1.refs_0_
  28.7 1.6 %collective-permute-start.10 = (bf16[256,384]{1,0:T(8,128)(2,1)S(1)}, bf16[256,384]{1,0:T(8,128)(2,1)S(1)}, u32[]{:S(2)}, u32[]{:S(2)}) collective-permute-start(bf16[256,384]{1,0:T(8,128)(2,1)S(1)} %share_sum.1.refs_0_), channel_id=1, source_target_pairs={{0,8},{4,12},{8,0},{12,4},{1,9},{5,13},{9,1},{13,5},{2,10},{6,14},... | collective-permute-start | bytes 589832 | tf_op jit(solution)/shard_map/ppermute | solution.py:274
  30.2 3.0 %collective-permute-start.3 = (bf16[256,384]{1,0:T(8,128)(2,1)S(1)}, bf16[256,384]{1,0:T(8,128)(2,1)S(1)}, u32[]{:S(2)}, u32[]{:S(2)}) collective-permute-start(bf16[256,384]{1,0:T(8,128)(2,1)S(1)} %share_sum.1.refs_0_), channel_id=1, source_target_pairs={{0,2},{1,3},{2,0},{3,1},{4,6},{5,7},{6,4},{7,5},{8,10},{9,11},{10,... | collective-permute-start | bytes 589832 | tf_op jit(solution)/shard_map/ppermute | solution.py:274
  33.3 1.4 %collective-permute-done.10.refs_2_ = bf16[256,384]{1,0:T(8,128)(2,1)S(1)} collective-permute-done((bf16[256,384]{1,0:T(8,128)(2,1)S(1)}, bf16[256,384]{1,0:T(8,128)(2,1)S(1)}, u32[]{:S(2)}, u32[]{:S(2)}) %collective-permute-start.10) | collective-permute-done | bytes 196640 | tf_op jit(solution)/shard_map/ppermute | solution.py:274
  34.7 2.3 %collective-permute-start.15 = (bf16[256,384]{1,0:T(8,128)(2,1)S(1)}, bf16[256,384]{1,0:T(8,128)(2,1)S(1)}, u32[]{:S(2)}, u32[]{:S(2)}) collective-permute-start(bf16[256,384]{1,0:T(8,128)(2,1)S(1)} %collective-permute-done.10.refs_2_), channel_id=1, source_target_pairs={{0,3},{1,2},{2,1},{3,0},{4,7},{5,6},{6,5},{7,4},{8,11},{9,10},{10,... | collective-permute-start | bytes 589832 | tf_op jit(solution)/shard_map/ppermute | solution.py:274
  37.0 0.8 %collective-permute-done.5.refs_1_ = bf16[256,384]{1,0:T(8,128)(2,1)S(1)} collective-permute-done((bf16[256,384]{1,0:T(8,128)(2,1)S(1)}, bf16[256,384]{1,0:T(8,128)(2,1)S(1)}, u32[]{:S(2)}, u32[]{:S(2)}) %collective-permute-start.5) | collective-permute-done | bytes 196640 | tf_op jit(solution)/shard_map/ppermute | solution.py:274
  37.8 1.2 %collective-permute-start.6 = (bf16[256,384]{1,0:T(8,128)(2,1)S(1)}, bf16[256,384]{1,0:T(8,128)(2,1)S(1)}, u32[]{:S(2)}, u32[]{:S(2)}) collective-permute-start(bf16[256,384]{1,0:T(8,128)(2,1)S(1)} %collective-permute-done.5.refs_1_), channel_id=1, source_target_pairs={{0,8},{4,12},{8,0},{12,4},{1,9},{5,13},{9,1},{13,5},{2,10},{6,14},... | collective-permute-start | bytes 589832 | tf_op jit(solution)/shard_map/ppermute | solution.py:274
  39.0 8.5 %collective-permute-done.3.refs_0_ = bf16[256,384]{1,0:T(8,128)(2,1)S(1)} collective-permute-done((bf16[256,384]{1,0:T(8,128)(2,1)S(1)}, bf16[256,384]{1,0:T(8,128)(2,1)S(1)}, u32[]{:S(2)}, u32[]{:S(2)}) %collective-permute-start.3) | collective-permute-done | bytes 196640 | tf_op jit(solution)/shard_map/ppermute | solution.py:274
  47.5 0.5 collective-permute-start.14
  48.0 4.1 %collective-permute-start.4 = (bf16[256,384]{1,0:T(8,128)(2,1)S(1)}, bf16[256,384]{1,0:T(8,128)(2,1)S(1)}, u32[]{:S(2)}, u32[]{:S(2)}) collective-permute-start(bf16[256,384]{1,0:T(8,128)(2,1)S(1)} %collective-permute-done.3.refs_0_), channel_id=1, source_target_pairs={{0,1},{1,0},{2,3},{3,2},{4,5},{5,4},{6,7},{7,6},{8,9},{9,8},{10,11... | collective-permute-start | bytes 589832 | tf_op jit(solution)/shard_map/ppermute | solution.py:274
  52.1 0.1 copy.9.pairs_ref
  52.3 0.5 collective-permute-start.17
  52.9 1.2 %collective-permute-done.14.refs_0_ = bf16[256,384]{1,0:T(8,128)(2,1)S(1)} collective-permute-done((bf16[256,384]{1,0:T(8,128)(2,1)S(1)}, bf16[256,384]{1,0:T(8,128)(2,1)S(1)}, u32[]{:S(2)}, u32[]{:S(2)}) %collective-permute-start.14) | collective-permute-done | bytes 196640 | tf_op jit(solution)/shard_map/ppermute | solution.py:274
  54.1 3.0 %collective-permute-done.4.refs_1_ = bf16[256,384]{1,0:T(8,128)(2,1)S(1)} collective-permute-done((bf16[256,384]{1,0:T(8,128)(2,1)S(1)}, bf16[256,384]{1,0:T(8,128)(2,1)S(1)}, u32[]{:S(2)}, u32[]{:S(2)}) %collective-permute-start.4) | collective-permute-done | bytes 196640 | tf_op jit(solution)/shard_map/ppermute | solution.py:274
  57.1 3.2 %early_rows.2.refs_6_ = f32[6,256,384]{2,1,0:T(8,128)S(1)} custom-call(s32[3,2]{1,0:T(4,128)S(1)} %copy.9.pairs_ref, s32[16,1,256]{2,1,0:T(1,128)S(1)} %bitcast.4, bf16[256,384]{1,0:T(8,128)(2,1)S(1)} %share_sum.1.refs_0_, bf16[256,384]{1,0:T(8,128)(2,1)S(1)} %collective-permute-done.5.refs_1_, bf16[256,384]{1,0:T(8,128)(2,1)S(1)} %collective-permute-done.10.refs_2_, ...), custom_call_target="tpu_custom_call" | custom-call | flops 3623878656 | bytes 4718592 | tf_op jit(solution)/shard_map/early_rows/pallas_call | solution.py:193
  60.3 3.2 %early_rows.3.early_ref = f32[6,256,384]{2,1,0:T(8,128)S(1)} custom-call(s32[3,2]{1,0:T(4,128)S(1)} %copy.9.pairs_ref, s32[16,1,256]{2,1,0:T(1,128)S(1)} %bitcast.5, bf16[256,384]{1,0:T(8,128)(2,1)S(1)} %collective-permute-done.3.refs_0_, bf16[256,384]{1,0:T(8,128)(2,1)S(1)} %collective-permute-done.4.refs_1_, ...), custom_call_target="tpu_custom_call" | custom-call | flops 3623878656 | bytes 4718592 | tf_op jit(solution)/shard_map/early_rows/pallas_call | solution.py:193
  63.6 6.4 %cross.1 = bf16[3,2,768,768]{3,2,1,0:T(8,128)(2,1)} custom-call(s32[3,2]{1,0:T(4,128)S(1)} %copy.9.pairs_ref, s32[16,1,256]{2,1,0:T(1,128)S(1)} %bitcast.6, f32[1,128]{1,0:T(1,128)S(1)} %maximum_bitcast_fusion.weights_ref, f32[6,256,384]{2,1,0:T(8,128)S(1)} %early_rows.3.early_ref, bf16[256,384]{1,0:T(8,128)(2,1)S(1)} %collective-permute-done.14.refs_0_, ...), custom_call_target="tpu_custom_call" | custom-call | tf_op jit(solution)/shard_map/cross/pallas_call | solution.py:231
  (28 shorter events, 0.2 us)
Async XLA Ops:
  0.0 52.1 %copy-start.2 = (s32[3,2]{0,1:T(2,128)S(1)}, s32[3,2]{0,1:T(2,128)}, u32[]{:S(2)}) copy-start(s32[3,2]{0,1:T(2,128)} %param.11) | copy-start | bytes 76
  0.0 52.2 %copy-start.3 = (f32[64]{0:T(128)S(1)}, f32[64]{0:T(128)}, u32[]{:S(2)}) copy-start(f32[64]{0:T(128)} %param.9) | copy-start | bytes 772
  0.0 57.1 %copy-start.1 = (s32[4096]{0:T(1024)S(1)}, s32[4096]{0:T(1024)}, u32[]{:S(2)}) copy-start(s32[4096]{0:T(1024)} %param.10) | copy-start | bytes 49156
  6.6 11.2 %collective-permute-start = (bf16[256,384]{1,0:T(8,128)(2,1)}, bf16[256,384]{1,0:T(8,128)(2,1)S(1)}, u32[]{:S(2)}, u32[]{:S(2)}) collective-permute-start(bf16[256,384]{1,0:T(8,128)(2,1)} %get-tuple-element.12), channel_id=1, source_target_pairs={{0,3},{1,2},{2,1},{3,0},{4,7},{5,6},{6,5},{7,4},{8,11},{9,10},{10,... | collective-permute-start | bytes 589832 | tf_op jit(solution)/shard_map/ppermute | solution.py:274
  11.7 16.9 %collective-permute-start.1 = (bf16[256,384]{1,0:T(8,128)(2,1)}, bf16[256,384]{1,0:T(8,128)(2,1)S(1)}, u32[]{:S(2)}, u32[]{:S(2)}) collective-permute-start(bf16[256,384]{1,0:T(8,128)(2,1)} %get-tuple-element.13), channel_id=1, source_target_pairs={{0,2},{1,3},{2,0},{3,1},{4,6},{5,7},{6,4},{7,5},{8,10},{9,11},{10,... | collective-permute-start | bytes 589832 | tf_op jit(solution)/shard_map/ppermute | solution.py:274
  11.7 1.0 %copy-start = (bf16[1024,128]{1,0:T(8,128)(2,1)S(1)}, bf16[1024,128]{1,0:T(8,128)(2,1)}, u32[]{:S(2)}) copy-start(bf16[1024,128]{1,0:T(8,128)(2,1)} %get-tuple-element.10.my_loads_ref) | copy-start | bytes 786436
  15.5 13.1 %collective-permute-start.2 = (bf16[256,384]{1,0:T(8,128)(2,1)S(1)}, bf16[256,384]{1,0:T(8,128)(2,1)S(1)}, u32[]{:S(2)}, u32[]{:S(2)}) collective-permute-start(bf16[256,384]{1,0:T(8,128)(2,1)S(1)} %get-tuple-element.14), channel_id=1, source_target_pairs={{0,1},{1,0},{2,3},{3,2},{4,5},{5,4},{6,7},{7,6},{8,9},{9,8},{10,11... | collective-permute-start | bytes 589832 | tf_op jit(solution)/shard_map/ppermute | solution.py:274
  28.7 6.0 %collective-permute-start.10 = (bf16[256,384]{1,0:T(8,128)(2,1)S(1)}, bf16[256,384]{1,0:T(8,128)(2,1)S(1)}, u32[]{:S(2)}, u32[]{:S(2)}) collective-permute-start(bf16[256,384]{1,0:T(8,128)(2,1)S(1)} %share_sum.1.refs_0_), channel_id=1, source_target_pairs={{0,8},{4,12},{8,0},{12,4},{1,9},{5,13},{9,1},{13,5},{2,10},{6,14},... | collective-permute-start | bytes 589832 | tf_op jit(solution)/shard_map/ppermute | solution.py:274
  30.2 7.6 %collective-permute-start.5 = (bf16[256,384]{1,0:T(8,128)(2,1)S(1)}, bf16[256,384]{1,0:T(8,128)(2,1)S(1)}, u32[]{:S(2)}, u32[]{:S(2)}) collective-permute-start(bf16[256,384]{1,0:T(8,128)(2,1)S(1)} %share_sum.1.refs_0_), channel_id=1, source_target_pairs={{0,1},{1,0},{2,3},{3,2},{4,5},{5,4},{6,7},{7,6},{8,9},{9,8},{10,11... | collective-permute-start | bytes 589832 | tf_op jit(solution)/shard_map/ppermute | solution.py:274
  30.2 7.6 %collective-permute-start.11 = (bf16[256,384]{1,0:T(8,128)(2,1)S(1)}, bf16[256,384]{1,0:T(8,128)(2,1)S(1)}, u32[]{:S(2)}, u32[]{:S(2)}) collective-permute-start(bf16[256,384]{1,0:T(8,128)(2,1)S(1)} %share_sum.1.refs_0_), channel_id=1, source_target_pairs={{0,4},{4,0},{8,12},{12,8},{1,5},{5,1},{9,13},{13,9},{2,6},{6,2},{1... | collective-permute-start | bytes 589832 | tf_op jit(solution)/shard_map/ppermute | solution.py:274
  30.2 17.3 %collective-permute-start.3 = (bf16[256,384]{1,0:T(8,128)(2,1)S(1)}, bf16[256,384]{1,0:T(8,128)(2,1)S(1)}, u32[]{:S(2)}, u32[]{:S(2)}) collective-permute-start(bf16[256,384]{1,0:T(8,128)(2,1)S(1)} %share_sum.1.refs_0_), channel_id=1, source_target_pairs={{0,2},{1,3},{2,0},{3,1},{4,6},{5,7},{6,4},{7,5},{8,10},{9,11},{10,... | collective-permute-start | bytes 589832 | tf_op jit(solution)/shard_map/ppermute | solution.py:274
  34.7 13.3 %collective-permute-start.15 = (bf16[256,384]{1,0:T(8,128)(2,1)S(1)}, bf16[256,384]{1,0:T(8,128)(2,1)S(1)}, u32[]{:S(2)}, u32[]{:S(2)}) collective-permute-start(bf16[256,384]{1,0:T(8,128)(2,1)S(1)} %collective-permute-done.10.refs_2_), channel_id=1, source_target_pairs={{0,3},{1,2},{2,1},{3,0},{4,7},{5,6},{6,5},{7,4},{8,11},{9,10},{10,... | collective-permute-start | bytes 589832 | tf_op jit(solution)/shard_map/ppermute | solution.py:274
  37.0 15.3 %collective-permute-start.13 = (bf16[256,384]{1,0:T(8,128)(2,1)S(1)}, bf16[256,384]{1,0:T(8,128)(2,1)S(1)}, u32[]{:S(2)}, u32[]{:S(2)}) collective-permute-start(bf16[256,384]{1,0:T(8,128)(2,1)S(1)} %collective-permute-done.10.refs_2_), channel_id=1, source_target_pairs={{0,4},{4,0},{8,12},{12,8},{1,5},{5,1},{9,13},{13,9},{2,6},{6,2},{1... | collective-permute-start | bytes 589832 | tf_op jit(solution)/shard_map/ppermute | solution.py:274
  37.8 14.5 %collective-permute-start.12 = (bf16[256,384]{1,0:T(8,128)(2,1)S(1)}, bf16[256,384]{1,0:T(8,128)(2,1)S(1)}, u32[]{:S(2)}, u32[]{:S(2)}) collective-permute-start(bf16[256,384]{1,0:T(8,128)(2,1)S(1)} %collective-permute-done.5.refs_1_), channel_id=1, source_target_pairs={{0,4},{4,0},{8,12},{12,8},{1,5},{5,1},{9,13},{13,9},{2,6},{6,2},{1... | collective-permute-start | bytes 589832 | tf_op jit(solution)/shard_map/ppermute | solution.py:274
  37.8 15.0 %collective-permute-start.6 = (bf16[256,384]{1,0:T(8,128)(2,1)S(1)}, bf16[256,384]{1,0:T(8,128)(2,1)S(1)}, u32[]{:S(2)}, u32[]{:S(2)}) collective-permute-start(bf16[256,384]{1,0:T(8,128)(2,1)S(1)} %collective-permute-done.5.refs_1_), channel_id=1, source_target_pairs={{0,8},{4,12},{8,0},{12,4},{1,9},{5,13},{9,1},{13,5},{2,10},{6,14},... | collective-permute-start | bytes 589832 | tf_op jit(solution)/shard_map/ppermute | solution.py:274
  47.5 6.6 %collective-permute-start.14 = (bf16[256,384]{1,0:T(8,128)(2,1)S(1)}, bf16[256,384]{1,0:T(8,128)(2,1)S(1)}, u32[]{:S(2)}, u32[]{:S(2)}) collective-permute-start(bf16[256,384]{1,0:T(8,128)(2,1)S(1)} %collective-permute-done.3.refs_0_), channel_id=1, source_target_pairs={{0,8},{4,12},{8,0},{12,4},{1,9},{5,13},{9,1},{13,5},{2,10},{6,14},... | collective-permute-start | bytes 589832 | tf_op jit(solution)/shard_map/ppermute | solution.py:274
  48.0 9.1 %collective-permute-start.4 = (bf16[256,384]{1,0:T(8,128)(2,1)S(1)}, bf16[256,384]{1,0:T(8,128)(2,1)S(1)}, u32[]{:S(2)}, u32[]{:S(2)}) collective-permute-start(bf16[256,384]{1,0:T(8,128)(2,1)S(1)} %collective-permute-done.3.refs_0_), channel_id=1, source_target_pairs={{0,1},{1,0},{2,3},{3,2},{4,5},{5,4},{6,7},{7,6},{8,9},{9,8},{10,11... | collective-permute-start | bytes 589832 | tf_op jit(solution)/shard_map/ppermute | solution.py:274
  52.3 8.0 %collective-permute-start.7 = (bf16[256,384]{1,0:T(8,128)(2,1)S(1)}, bf16[256,384]{1,0:T(8,128)(2,1)S(1)}, u32[]{:S(2)}, u32[]{:S(2)}) collective-permute-start(bf16[256,384]{1,0:T(8,128)(2,1)S(1)} %collective-permute-done.3.refs_0_), channel_id=1, source_target_pairs={{0,4},{4,0},{8,12},{12,8},{1,5},{5,1},{9,13},{13,9},{2,6},{6,2},{1... | collective-permute-start | bytes 589832 | tf_op jit(solution)/shard_map/ppermute | solution.py:274
  52.3 11.2 %collective-permute-start.17 = (bf16[256,384]{1,0:T(8,128)(2,1)S(1)}, bf16[256,384]{1,0:T(8,128)(2,1)S(1)}, u32[]{:S(2)}, u32[]{:S(2)}) collective-permute-start(bf16[256,384]{1,0:T(8,128)(2,1)S(1)} %collective-permute-done.15.refs_1_), channel_id=1, source_target_pairs={{0,4},{4,0},{8,12},{12,8},{1,5},{5,1},{9,13},{13,9},{2,6},{6,2},{1... | collective-permute-start | bytes 589832 | tf_op jit(solution)/shard_map/ppermute | solution.py:274
  52.8 7.5 %collective-permute-start.9 = (bf16[256,384]{1,0:T(8,128)(2,1)S(1)}, bf16[256,384]{1,0:T(8,128)(2,1)S(1)}, u32[]{:S(2)}, u32[]{:S(2)}) collective-permute-start(bf16[256,384]{1,0:T(8,128)(2,1)S(1)} %collective-permute-done.6.refs_2_), channel_id=1, source_target_pairs={{0,4},{4,0},{8,12},{12,8},{1,5},{5,1},{9,13},{13,9},{2,6},{6,2},{1... | collective-permute-start | bytes 589832 | tf_op jit(solution)/shard_map/ppermute | solution.py:274
  54.1 9.5 %collective-permute-start.16 = (bf16[256,384]{1,0:T(8,128)(2,1)S(1)}, bf16[256,384]{1,0:T(8,128)(2,1)S(1)}, u32[]{:S(2)}, u32[]{:S(2)}) collective-permute-start(bf16[256,384]{1,0:T(8,128)(2,1)S(1)} %collective-permute-done.14.refs_0_), channel_id=1, source_target_pairs={{0,4},{4,0},{8,12},{12,8},{1,5},{5,1},{9,13},{13,9},{2,6},{6,2},{1... | collective-permute-start | bytes 589832 | tf_op jit(solution)/shard_map/ppermute | solution.py:274
  57.1 3.2 %collective-permute-start.8 = (bf16[256,384]{1,0:T(8,128)(2,1)S(1)}, bf16[256,384]{1,0:T(8,128)(2,1)S(1)}, u32[]{:S(2)}, u32[]{:S(2)}) collective-permute-start(bf16[256,384]{1,0:T(8,128)(2,1)S(1)} %collective-permute-done.4.refs_1_), channel_id=1, source_target_pairs={{0,4},{4,0},{8,12},{12,8},{1,5},{5,1},{9,13},{13,9},{2,6},{6,2},{1... | collective-permute-start | bytes 589832 | tf_op jit(solution)/shard_map/ppermute | solution.py:274

commit v3 on v2

--- a/solution.py
+++ b/solution.py
@@ -13,7 +13,7 @@
 F32 = jnp.float32
 BF16 = jnp.bfloat16
 VMEM_BYTES = 48 * 1024 * 1024
-FIRST_VMEM_BYTES = 125 * 512 * 1024
+FIRST_VMEM_BYTES = 124 * 512 * 1024
 
 
 def params(steps=1):
@@ -170,20 +170,20 @@
     n_patch = lax.axis_size("patch")
     place = (lax.axis_index("hot") ^ key[0]) * n_patch + (lax.axis_index("patch") ^ key[1])
     rows = position_ref.shape[2]
-    wanted = lax.broadcasted_iota(jnp.int32, (BLK, rows), 0) + block * BLK
-    return jnp.where(position_ref[place] == wanted, 1.0, 0.0).astype(BF16)
+    offset = position_ref[place] - block * BLK
+    return jnp.where(offset == lax.broadcasted_iota(jnp.int32, (BLK, rows), 0), 1.0, 0.0).astype(BF16)
 
 
 def early_kernel(keys, pairs_ref, position_ref, *refs):
-    pieces, befores, out_ref = refs[: len(keys)], refs[len(keys) : -1], refs[-1]
+    pieces, befores, (out_ref, joined_ref) = refs[: len(keys)], refs[len(keys) : -2], refs[-2:]
+    rows = pieces[0].shape[0]
+    for i, piece in enumerate(pieces):
+        joined_ref[i * rows : (i + 1) * rows, :] = piece[...]
     for s in range(out_ref.shape[0]):
         block = pairs_ref[s // 2, s % 2]
-        total = befores[0][s] if befores else None
-        for key, piece in zip(keys, pieces):
-            pick = pick_rows(position_ref, key, block)
-            term = jnp.dot(pick, piece[...], preferred_element_type=F32)
-            total = term if total is None else total + term
-        out_ref[s] = total
+        pick = jnp.concatenate([pick_rows(position_ref, key, block) for key in keys], axis=1)
+        total = jnp.dot(pick, joined_ref[...], preferred_element_type=F32)
+        out_ref[s] = total + befores[0][s] if befores else total
 
 
 def early_rows(pairs, position, keys, pieces, before=()):
@@ -195,6 +195,7 @@
         out_shape=jax.ShapeDtypeStruct((count, BLK, width), F32),
         in_specs=[pl.BlockSpec(memory_space=pltpu.SMEM)] + [vmem()] * (1 + len(pieces) + len(before)),
         out_specs=vmem(),
+        scratch_shapes=[pltpu.VMEM((len(keys) * rows, width), BF16)],
         compiler_params=pltpu.CompilerParams(vmem_limit_bytes=VMEM_BYTES),
         cost_estimate=cost(2 * flops, 8 * count * BLK * width),
         name="early_rows",
@@ -246,22 +247,6 @@
     )(pairs, position, weights, early, *pieces)
 
 
-def gather_plane(own, swap, n_patch, n_hot):
-    plane = {(0, 0): own}
-    bits = [1 << b for b in reversed(range((n_patch - 1).bit_length()))]
-    for bit in bits:
-        for _, k in list(plane):
-            plane[0, k ^ bit] = swap(plane[0, k], "patch", bit)
-    chip_bits = [2 << b for b in reversed(range((n_hot // 2 - 1).bit_length()))]
-    for bit in chip_bits:
-        for j, k in list(plane):
-            if k != n_patch - 1:
-                plane[j ^ bit, k] = swap(plane[j, k], "hot", bit)
-    for j in range(2, n_hot, 2):
-        plane[j, n_patch - 1] = swap(plane[j, 0], "patch", n_patch - 1)
-    return plane
-
-
 def shards(influence, loads, patch_order, spectral_weights, block_position, block_pairs):
     components, hot_rows, patch_cols = influence.shape
     n_patch, n_hot = lax.axis_size("patch"), lax.axis_size("hot")
@@ -282,15 +267,50 @@
     received = [swap(t, "patch", k) for k, t in zip(far + near, list(far_terms) + list(near_terms[:-1]))]
     own = share_sum(near_terms[-1], received)
 
-    plane = gather_plane(own, swap, n_patch, n_hot)
-    pieces = dict(plane)
-    pieces.update({(j + 1, k): swap(piece, "hot", 1) for (j, k), piece in plane.items()})
     position = block_position.reshape(n_hot * n_patch, 1, share_rows)
-    late = [key for key in pieces if key[0] >= 2 and key[1] in far]
-    first = [key for key in pieces if (key[0] < 2 and key[1] not in far) or key[1] == 0]
-    second = [key for key in pieces if key not in late and key not in first]
-    early = early_rows(block_pairs, position, first, [pieces[key] for key in first])
-    early = early_rows(block_pairs, position, second, [pieces[key] for key in second], [early])
+    top = n_patch // 2
+    patch_bits = [1 << b for b in reversed(range((n_patch - 1).bit_length()))]
+    chip_bits = [2 << b for b in reversed(range((n_hot // 2 - 1).bit_length()))]
+    tie = lambda value, *after: lax.optimization_barrier((value, *after))[0]
+
+    plane, pieces = {(0, 0): own}, {}
+
+    def along(keys, axis, bits):
+        for bit in bits:
+            for j, k in list(keys):
+                key = (j ^ bit, k) if axis == "hot" else (j, k ^ bit)
+                plane[key] = swap(plane[j, k], axis, bit)
+                keys = keys + [key]
+        return keys
+
+    def cores(keys):
+        for j, k in keys:
+            pieces[j, k] = plane[j, k]
+            pieces[j + 1, k] = swap(plane[j, k], "hot", 1)
+        return [(j + c, k) for j, k in keys for c in (0, 1)]
+
+    def picked(keys, *before):
+        return early_rows(block_pairs, position, keys, [pieces[key] for key in keys], before)
+
+    head = cores([(0, 0)])
+    along([(0, 0)], "patch", patch_bits[:1])
+    near_keys = along([(0, 0)], "patch", patch_bits[1:])
+    chip_keys = along([(0, 0)], "hot", chip_bits)
+    for key in near_keys[1:] + chip_keys[1:]:
+        plane[key] = tie(plane[key], plane[0, top])
+    far_keys = along([(0, top)], "patch", patch_bits[1:])
+    for j, _ in chip_keys[1:]:
+        plane[j, n_patch - 1] = swap(plane[j, 0], "patch", n_patch - 1)
+    early = picked(head + cores(near_keys[1:] + chip_keys[1:] + [(0, top)]))
+    later = []
+    for key in near_keys[1:] + far_keys[:-1]:
+        later += along([key], "hot", chip_bits)[1:]
+    middle = [key for key in later if key[1] < top]
+    early = picked(cores(far_keys[1:] + middle), early)
+    last = [key for key in plane if key not in pieces]
+    for key in last:
+        plane[key] = tie(plane[key], early)
+    late = cores(last)
     return cross(
         block_pairs, position, weights, early, late, [pieces[key] for key in late], components
     )

time: 70.2 us -> 65.6 us (0.934)
  the two profiles are of different devices: /device:TPU:0 before, /device:TPU:25 now
where the time goes in v3:
time: 65.6 us; the launch traced here: 65.5 us
  starting transfers between devices  22.6 us (34%)
  Pallas kernels  22.3 us (34%)
  waiting for transfers between devices  19.4 us (30%)
  local copies, waits for them, and re-layouts  1.06 us (2%)
    ppermute x18, starting transfers between devices, swap(): return lax.ppermute(array, axis, [(i, i ^ k) for i in range(size)])  22.6 us
    ppermute x18, waiting for transfers between devices, swap(): return lax.ppermute(array, axis, [(i, i ^ k) for i in range(size)])  19.4 us
    pallas_call x1, Pallas kernels, first_products(): pl.pallas_call(functools.partial(first_kernel, which), out_shape=[share]...  6.53 us
    pallas_call x2, Pallas kernels, early_rows(): pl.pallas_call(functools.partial(early_kernel, keys), out_shape=jax.Shape...  6.41 us
    pallas_call x1, Pallas kernels, cross(): pl.pallas_call(functools.partial(cross_kernel, components, keys), out_sha...  6.36 us
    pallas_call x1, Pallas kernels, more_products(): pl.pallas_call(functools.partial(more_kernel, which), out_shape=[jax.Shap...  2.87 us
  transfers between devices with their start and end apart: 18, of which 6 were waited for; matrix products, arithmetic and copies ran while one was open for 0% of the time, Pallas kernels for 14%

profile of v3, /device:TPU:25, one launch (start us, length us, event | category | flops | bytes accessed | tf_op | source)
XLA Modules:
  0.0 65.5 jit_solution(8143549837348836826)
XLA Ops:
  0.0 6.5 %first_products.1 = (bf16[256,384]{1,0:T(8,128)(2,1)}, bf16[256,384]{1,0:T(8,128)(2,1)}, bf16[1024,128]{1,0:T(8,128)(2,1)}) custom-call(s32[4,8,128]{2,1,0:T(8,128)} %bitcast.7, bf16[4096,128]{1,0:T(8,128)(2,1)} %loads_ref.1, bf16[3,1024,1024]{2,1,0:T(8,128)(2,1)} %influence_ref.3), custom_call_target="tpu_custom_call" | custom-call | tf_op jit(solution)/shard_map/first_products/pallas_call | solution.py:117
  6.6 1.3 %collective-permute-start.1 = (bf16[256,384]{1,0:T(8,128)(2,1)}, bf16[256,384]{1,0:T(8,128)(2,1)S(1)}, u32[]{:S(2)}, u32[]{:S(2)}) collective-permute-start(bf16[256,384]{1,0:T(8,128)(2,1)} %get-tuple-element.17), channel_id=1, source_target_pairs={{0,2},{1,3},{2,0},{3,1},{4,6},{5,7},{6,4},{7,5},{8,10},{9,11},{10,... | collective-permute-start | bytes 589832 | tf_op jit(solution)/shard_map/ppermute | solution.py:259
  8.0 0.9 %copy-done = bf16[1024,128]{1,0:T(8,128)(2,1)S(1)} copy-done((bf16[1024,128]{1,0:T(8,128)(2,1)S(1)}, bf16[1024,128]{1,0:T(8,128)(2,1)}, u32[]{:S(2)}) %copy-start) | copy-done | bytes 262168
  8.9 2.9 %more_products.1 = (bf16[256,384]{1,0:T(8,128)(2,1)S(1)}, f32[256,384]{1,0:T(8,128)S(1)}) custom-call(bf16[1024,128]{1,0:T(8,128)(2,1)S(1)} %copy-done, bf16[3,1024,1024]{2,1,0:T(8,128)(2,1)} %influence_ref.3), custom_call_target="tpu_custom_call" | custom-call | flops 805306368 | bytes 12582912 | tf_op jit(solution)/shard_map/more_products/pallas_call | solution.py:141
  11.8 2.3 %collective-permute-start.2 = (bf16[256,384]{1,0:T(8,128)(2,1)S(1)}, bf16[256,384]{1,0:T(8,128)(2,1)S(1)}, u32[]{:S(2)}, u32[]{:S(2)}) collective-permute-start(bf16[256,384]{1,0:T(8,128)(2,1)S(1)} %get-tuple-element.18), channel_id=1, source_target_pairs={{0,1},{1,0},{2,3},{3,2},{4,5},{5,4},{6,7},{7,6},{8,9},{9,8},{10,11... | collective-permute-start | bytes 589832 | tf_op jit(solution)/shard_map/ppermute | solution.py:259
  14.1 0.4 collective-permute-done.refs_0_
  14.5 10.6 %collective-permute-done.1.refs_1_ = bf16[256,384]{1,0:T(8,128)(2,1)S(1)} collective-permute-done((bf16[256,384]{1,0:T(8,128)(2,1)}, bf16[256,384]{1,0:T(8,128)(2,1)S(1)}, u32[]{:S(2)}, u32[]{:S(2)}) %collective-permute-start.1) | collective-permute-done | bytes 196640 | tf_op jit(solution)/shard_map/ppermute | solution.py:259
  25.3 1.5 %collective-permute-start.3 = (bf16[256,384]{1,0:T(8,128)(2,1)S(1)}, bf16[256,384]{1,0:T(8,128)(2,1)S(1)}, u32[]{:S(2)}, u32[]{:S(2)}) collective-permute-start(bf16[256,384]{1,0:T(8,128)(2,1)S(1)} %share_sum.1.refs_0_), channel_id=1, source_target_pairs={{0,2},{1,3},{2,0},{3,1},{4,6},{5,7},{6,4},{7,5},{8,10},{9,11},{10,... | collective-permute-start | bytes 589832 | tf_op jit(solution)/shard_map/ppermute | solution.py:259
  26.8 1.2 %collective-permute-start.11 = (bf16[256,384]{1,0:T(8,128)(2,1)S(1)}, bf16[256,384]{1,0:T(8,128)(2,1)S(1)}, u32[]{:S(2)}, u32[]{:S(2)}) collective-permute-start(bf16[256,384]{1,0:T(8,128)(2,1)S(1)} %share_sum.1.refs_0_), channel_id=1, source_target_pairs={{0,8},{4,12},{8,0},{12,4},{1,9},{5,13},{9,1},{13,5},{2,10},{6,14},... | collective-permute-start | bytes 589832 | tf_op jit(solution)/shard_map/ppermute | solution.py:259
  28.0 2.2 %collective-permute-start.9 = (bf16[256,384]{1,0:T(8,128)(2,1)S(1)}, bf16[256,384]{1,0:T(8,128)(2,1)S(1)}, u32[]{:S(2)}, u32[]{:S(2)}) collective-permute-start(bf16[256,384]{1,0:T(8,128)(2,1)S(1)} %share_sum.1.refs_0_), channel_id=1, source_target_pairs={{0,4},{4,0},{8,12},{12,8},{1,5},{5,1},{9,13},{13,9},{2,6},{6,2},{1... | collective-permute-start | bytes 589832 | tf_op jit(solution)/shard_map/ppermute | solution.py:259
  30.2 3.9 %collective-permute-done.6.refs_2_ = bf16[256,384]{1,0:T(8,128)(2,1)S(1)} collective-permute-done((bf16[256,384]{1,0:T(8,128)(2,1)S(1)}, bf16[256,384]{1,0:T(8,128)(2,1)S(1)}, u32[]{:S(2)}, u32[]{:S(2)}) %collective-permute-start.6) | collective-permute-done | bytes 196640 | tf_op jit(solution)/shard_map/ppermute | solution.py:259
  34.1 3.7 %collective-permute-start.10 = (bf16[256,384]{1,0:T(8,128)(2,1)S(1)}, bf16[256,384]{1,0:T(8,128)(2,1)S(1)}, u32[]{:S(2)}, u32[]{:S(2)}) collective-permute-start(bf16[256,384]{1,0:T(8,128)(2,1)S(1)} %collective-permute-done.6.refs_2_), channel_id=1, source_target_pairs={{0,4},{4,0},{8,12},{12,8},{1,5},{5,1},{9,13},{13,9},{2,6},{6,2},{1... | collective-permute-start | bytes 589832 | tf_op jit(solution)/shard_map/ppermute | solution.py:259
  37.8 1.2 %collective-permute-start.7 = (bf16[256,384]{1,0:T(8,128)(2,1)S(1)}, bf16[256,384]{1,0:T(8,128)(2,1)S(1)}, u32[]{:S(2)}, u32[]{:S(2)}) collective-permute-start(bf16[256,384]{1,0:T(8,128)(2,1)S(1)} %collective-permute-done.6.refs_2_), channel_id=1, source_target_pairs={{0,8},{4,12},{8,0},{12,4},{1,9},{5,13},{9,1},{13,5},{2,10},{6,14},... | collective-permute-start | bytes 589832 | tf_op jit(solution)/shard_map/ppermute | solution.py:259
  39.0 0.3 collective-permute-start.12
  39.7 1.5 %collective-permute-start.14 = (bf16[256,384]{1,0:T(8,128)(2,1)S(1)}, bf16[256,384]{1,0:T(8,128)(2,1)S(1)}, u32[]{:S(2)}, u32[]{:S(2)}) collective-permute-start(bf16[256,384]{1,0:T(8,128)(2,1)S(1)} %collective-permute-done.11.refs_4_), channel_id=1, source_target_pairs={{0,3},{1,2},{2,1},{3,0},{4,7},{5,6},{6,5},{7,4},{8,11},{9,10},{10,... | collective-permute-start | bytes 589832 | tf_op jit(solution)/shard_map/ppermute | solution.py:259
  41.1 3.2 %collective-permute-done.7.refs_2_ = bf16[256,384]{1,0:T(8,128)(2,1)S(1)} collective-permute-done((bf16[256,384]{1,0:T(8,128)(2,1)S(1)}, bf16[256,384]{1,0:T(8,128)(2,1)S(1)}, u32[]{:S(2)}, u32[]{:S(2)}) %collective-permute-start.7) | collective-permute-done | bytes 196640 | tf_op jit(solution)/shard_map/ppermute | solution.py:259
  44.4 1.2 %collective-permute-start.16 = (bf16[256,384]{1,0:T(8,128)(2,1)S(1)}, bf16[256,384]{1,0:T(8,128)(2,1)S(1)}, u32[]{:S(2)}, u32[]{:S(2)}) collective-permute-start(bf16[256,384]{1,0:T(8,128)(2,1)S(1)} %collective-permute-done.3.refs_6_), channel_id=1, source_target_pairs={{0,8},{4,12},{8,0},{12,4},{1,9},{5,13},{9,1},{13,5},{2,10},{6,14},... | collective-permute-start | bytes 589832 | tf_op jit(solution)/shard_map/ppermute | solution.py:259
  45.6 1.1 %collective-permute-start.8 = (bf16[256,384]{1,0:T(8,128)(2,1)S(1)}, bf16[256,384]{1,0:T(8,128)(2,1)S(1)}, u32[]{:S(2)}, u32[]{:S(2)}) collective-permute-start(bf16[256,384]{1,0:T(8,128)(2,1)S(1)} %collective-permute-done.7.refs_2_), channel_id=1, source_target_pairs={{0,4},{4,0},{8,12},{12,8},{1,5},{5,1},{9,13},{13,9},{2,6},{6,2},{1... | collective-permute-start | bytes 589832 | tf_op jit(solution)/shard_map/ppermute | solution.py:259
  46.7 4.2 %collective-permute-start.5 = (bf16[256,384]{1,0:T(8,128)(2,1)S(1)}, bf16[256,384]{1,0:T(8,128)(2,1)S(1)}, u32[]{:S(2)}, u32[]{:S(2)}) collective-permute-start(bf16[256,384]{1,0:T(8,128)(2,1)S(1)} %collective-permute-done.4.refs_0_), channel_id=1, source_target_pairs={{0,4},{4,0},{8,12},{12,8},{1,5},{5,1},{9,13},{13,9},{2,6},{6,2},{1... | collective-permute-start | bytes 589832 | tf_op jit(solution)/shard_map/ppermute | solution.py:259
  50.9 4.0 %early_rows.2.refs_4_ = f32[6,256,384]{2,1,0:T(8,128)S(1)} custom-call(s32[3,2]{1,0:T(4,128)S(1)} %copy.9.pairs_ref, s32[16,1,256]{2,1,0:T(1,128)S(1)} %bitcast.4, bf16[256,384]{1,0:T(8,128)(2,1)S(1)} %share_sum.1.refs_0_, bf16[256,384]{1,0:T(8,128)(2,1)S(1)} %collective-permute-done.9.refs_1_, bf16[256,384]{1,0:T(8,128)(2,1)S(1)} %collective-permute-done.6.refs_2_, ...), custom_call_target="tpu_custom_call" | custom-call | flops 4831838208 | bytes 4718592 | tf_op jit(solution)/shard_map/early_rows/pallas_call | solution.py:193
  54.9 2.4 %early_rows.3.early_ref = f32[6,256,384]{2,1,0:T(8,128)S(1)} custom-call(s32[3,2]{1,0:T(4,128)S(1)} %copy.9.pairs_ref, s32[16,1,256]{2,1,0:T(1,128)S(1)} %bitcast.5, bf16[256,384]{1,0:T(8,128)(2,1)S(1)} %collective-permute-done.4.refs_0_, bf16[256,384]{1,0:T(8,128)(2,1)S(1)} %collective-permute-done.5.refs_1_, ...), custom_call_target="tpu_custom_call" | custom-call | flops 2415919104 | bytes 4718592 | tf_op jit(solution)/shard_map/early_rows/pallas_call | solution.py:193
  57.4 0.5 collective-permute-start.17
  58.0 0.9 %collective-permute-done.15.refs_1_ = bf16[256,384]{1,0:T(8,128)(2,1)S(1)} collective-permute-done((bf16[256,384]{1,0:T(8,128)(2,1)S(1)}, bf16[256,384]{1,0:T(8,128)(2,1)S(1)}, u32[]{:S(2)}, u32[]{:S(2)}) %collective-permute-start.15) | collective-permute-done | bytes 196640 | tf_op jit(solution)/shard_map/ppermute | solution.py:259
  59.1 6.4 %cross.1 = bf16[3,2,768,768]{3,2,1,0:T(8,128)(2,1)} custom-call(s32[3,2]{1,0:T(4,128)S(1)} %copy.9.pairs_ref, s32[16,1,256]{2,1,0:T(1,128)S(1)} %bitcast.6, f32[1,128]{1,0:T(1,128)S(1)} %maximum_bitcast_fusion.weights_ref, f32[6,256,384]{2,1,0:T(8,128)S(1)} %early_rows.3.early_ref, bf16[256,384]{1,0:T(8,128)(2,1)S(1)} %collective-permute-done.14.refs_0_, ...), custom_call_target="tpu_custom_call" | custom-call | tf_op jit(solution)/shard_map/cross/pallas_call | solution.py:232
  (28 shorter events, 1.0 us)
Async XLA Ops:
  0.0 39.6 %copy-start.2 = (s32[3,2]{0,1:T(2,128)S(1)}, s32[3,2]{0,1:T(2,128)}, u32[]{:S(2)}) copy-start(s32[3,2]{0,1:T(2,128)} %param.11) | copy-start | bytes 76
  0.0 50.9 %copy-start.1 = (s32[4096]{0:T(1024)S(1)}, s32[4096]{0:T(1024)}, u32[]{:S(2)}) copy-start(s32[4096]{0:T(1024)} %param.10) | copy-start | bytes 49156
  6.5 7.9 %collective-permute-start = (bf16[256,384]{1,0:T(8,128)(2,1)}, bf16[256,384]{1,0:T(8,128)(2,1)S(1)}, u32[]{:S(2)}, u32[]{:S(2)}) collective-permute-start(bf16[256,384]{1,0:T(8,128)(2,1)} %get-tuple-element.16), channel_id=1, source_target_pairs={{0,3},{1,2},{2,1},{3,0},{4,7},{5,6},{6,5},{7,4},{8,11},{9,10},{10,... | collective-permute-start | bytes 589832 | tf_op jit(solution)/shard_map/ppermute | solution.py:259
  6.6 18.5 %collective-permute-start.1 = (bf16[256,384]{1,0:T(8,128)(2,1)}, bf16[256,384]{1,0:T(8,128)(2,1)S(1)}, u32[]{:S(2)}, u32[]{:S(2)}) collective-permute-start(bf16[256,384]{1,0:T(8,128)(2,1)} %get-tuple-element.17), channel_id=1, source_target_pairs={{0,2},{1,3},{2,0},{3,1},{4,6},{5,7},{6,4},{7,5},{8,10},{9,11},{10,... | collective-permute-start | bytes 589832 | tf_op jit(solution)/shard_map/ppermute | solution.py:259
  8.0 0.9 %copy-start = (bf16[1024,128]{1,0:T(8,128)(2,1)S(1)}, bf16[1024,128]{1,0:T(8,128)(2,1)}, u32[]{:S(2)}) copy-start(bf16[1024,128]{1,0:T(8,128)(2,1)} %get-tuple-element.14.my_loads_ref) | copy-start | bytes 786436
  11.8 13.3 %collective-permute-start.2 = (bf16[256,384]{1,0:T(8,128)(2,1)S(1)}, bf16[256,384]{1,0:T(8,128)(2,1)S(1)}, u32[]{:S(2)}, u32[]{:S(2)}) collective-permute-start(bf16[256,384]{1,0:T(8,128)(2,1)S(1)} %get-tuple-element.18), channel_id=1, source_target_pairs={{0,1},{1,0},{2,3},{3,2},{4,5},{5,4},{6,7},{7,6},{8,9},{9,8},{10,11... | collective-permute-start | bytes 589832 | tf_op jit(solution)/shard_map/ppermute | solution.py:259
  25.2 8.9 %collective-permute-start.6 = (bf16[256,384]{1,0:T(8,128)(2,1)S(1)}, bf16[256,384]{1,0:T(8,128)(2,1)S(1)}, u32[]{:S(2)}, u32[]{:S(2)}) collective-permute-start(bf16[256,384]{1,0:T(8,128)(2,1)S(1)} %share_sum.1.refs_0_), channel_id=1, source_target_pairs={{0,1},{1,0},{2,3},{3,2},{4,5},{5,4},{6,7},{7,6},{8,9},{9,8},{10,11... | collective-permute-start | bytes 589832 | tf_op jit(solution)/shard_map/ppermute | solution.py:259
  25.3 8.9 %collective-permute-start.3 = (bf16[256,384]{1,0:T(8,128)(2,1)S(1)}, bf16[256,384]{1,0:T(8,128)(2,1)S(1)}, u32[]{:S(2)}, u32[]{:S(2)}) collective-permute-start(bf16[256,384]{1,0:T(8,128)(2,1)S(1)} %share_sum.1.refs_0_), channel_id=1, source_target_pairs={{0,2},{1,3},{2,0},{3,1},{4,6},{5,7},{6,4},{7,5},{8,10},{9,11},{10,... | collective-permute-start | bytes 589832 | tf_op jit(solution)/shard_map/ppermute | solution.py:259
  26.8 12.2 %collective-permute-start.11 = (bf16[256,384]{1,0:T(8,128)(2,1)S(1)}, bf16[256,384]{1,0:T(8,128)(2,1)S(1)}, u32[]{:S(2)}, u32[]{:S(2)}) collective-permute-start(bf16[256,384]{1,0:T(8,128)(2,1)S(1)} %share_sum.1.refs_0_), channel_id=1, source_target_pairs={{0,8},{4,12},{8,0},{12,4},{1,9},{5,13},{9,1},{13,5},{2,10},{6,14},... | collective-permute-start | bytes 589832 | tf_op jit(solution)/shard_map/ppermute | solution.py:259
  28.0 11.3 %collective-permute-start.9 = (bf16[256,384]{1,0:T(8,128)(2,1)S(1)}, bf16[256,384]{1,0:T(8,128)(2,1)S(1)}, u32[]{:S(2)}, u32[]{:S(2)}) collective-permute-start(bf16[256,384]{1,0:T(8,128)(2,1)S(1)} %share_sum.1.refs_0_), channel_id=1, source_target_pairs={{0,4},{4,0},{8,12},{12,8},{1,5},{5,1},{9,13},{13,9},{2,6},{6,2},{1... | collective-permute-start | bytes 589832 | tf_op jit(solution)/shard_map/ppermute | solution.py:259
  34.1 5.5 %collective-permute-start.10 = (bf16[256,384]{1,0:T(8,128)(2,1)S(1)}, bf16[256,384]{1,0:T(8,128)(2,1)S(1)}, u32[]{:S(2)}, u32[]{:S(2)}) collective-permute-start(bf16[256,384]{1,0:T(8,128)(2,1)S(1)} %collective-permute-done.6.refs_2_), channel_id=1, source_target_pairs={{0,4},{4,0},{8,12},{12,8},{1,5},{5,1},{9,13},{13,9},{2,6},{6,2},{1... | collective-permute-start | bytes 589832 | tf_op jit(solution)/shard_map/ppermute | solution.py:259
  37.8 6.5 %collective-permute-start.7 = (bf16[256,384]{1,0:T(8,128)(2,1)S(1)}, bf16[256,384]{1,0:T(8,128)(2,1)S(1)}, u32[]{:S(2)}, u32[]{:S(2)}) collective-permute-start(bf16[256,384]{1,0:T(8,128)(2,1)S(1)} %collective-permute-done.6.refs_2_), channel_id=1, source_target_pairs={{0,8},{4,12},{8,0},{12,4},{1,9},{5,13},{9,1},{13,5},{2,10},{6,14},... | collective-permute-start | bytes 589832 | tf_op jit(solution)/shard_map/ppermute | solution.py:259
  39.0 6.5 %collective-permute-start.12 = (bf16[256,384]{1,0:T(8,128)(2,1)S(1)}, bf16[256,384]{1,0:T(8,128)(2,1)S(1)}, u32[]{:S(2)}, u32[]{:S(2)}) collective-permute-start(bf16[256,384]{1,0:T(8,128)(2,1)S(1)} %collective-permute-done.11.refs_4_), channel_id=1, source_target_pairs={{0,4},{4,0},{8,12},{12,8},{1,5},{5,1},{9,13},{13,9},{2,6},{6,2},{1... | collective-permute-start | bytes 589832 | tf_op jit(solution)/shard_map/ppermute | solution.py:259
  39.3 7.3 %collective-permute-start.4 = (bf16[256,384]{1,0:T(8,128)(2,1)S(1)}, bf16[256,384]{1,0:T(8,128)(2,1)S(1)}, u32[]{:S(2)}, u32[]{:S(2)}) collective-permute-start(bf16[256,384]{1,0:T(8,128)(2,1)S(1)} %collective-permute-done.3.refs_6_), channel_id=1, source_target_pairs={{0,1},{1,0},{2,3},{3,2},{4,5},{5,4},{6,7},{7,6},{8,9},{9,8},{10,11... | collective-permute-start | bytes 589832 | tf_op jit(solution)/shard_map/ppermute | solution.py:259
  39.3 11.5 %collective-permute-start.13 = (bf16[256,384]{1,0:T(8,128)(2,1)S(1)}, bf16[256,384]{1,0:T(8,128)(2,1)S(1)}, u32[]{:S(2)}, u32[]{:S(2)}) collective-permute-start(bf16[256,384]{1,0:T(8,128)(2,1)S(1)} %collective-permute-done.3.refs_6_), channel_id=1, source_target_pairs={{0,4},{4,0},{8,12},{12,8},{1,5},{5,1},{9,13},{13,9},{2,6},{6,2},{1... | collective-permute-start | bytes 589832 | tf_op jit(solution)/shard_map/ppermute | solution.py:259
  39.7 17.7 %collective-permute-start.14 = (bf16[256,384]{1,0:T(8,128)(2,1)S(1)}, bf16[256,384]{1,0:T(8,128)(2,1)S(1)}, u32[]{:S(2)}, u32[]{:S(2)}) collective-permute-start(bf16[256,384]{1,0:T(8,128)(2,1)S(1)} %collective-permute-done.11.refs_4_), channel_id=1, source_target_pairs={{0,3},{1,2},{2,1},{3,0},{4,7},{5,6},{6,5},{7,4},{8,11},{9,10},{10,... | collective-permute-start | bytes 589832 | tf_op jit(solution)/shard_map/ppermute | solution.py:259
  44.4 13.0 %collective-permute-start.16 = (bf16[256,384]{1,0:T(8,128)(2,1)S(1)}, bf16[256,384]{1,0:T(8,128)(2,1)S(1)}, u32[]{:S(2)}, u32[]{:S(2)}) collective-permute-start(bf16[256,384]{1,0:T(8,128)(2,1)S(1)} %collective-permute-done.3.refs_6_), channel_id=1, source_target_pairs={{0,8},{4,12},{8,0},{12,4},{1,9},{5,13},{9,1},{13,5},{2,10},{6,14},... | collective-permute-start | bytes 589832 | tf_op jit(solution)/shard_map/ppermute | solution.py:259
  45.6 9.3 %collective-permute-start.8 = (bf16[256,384]{1,0:T(8,128)(2,1)S(1)}, bf16[256,384]{1,0:T(8,128)(2,1)S(1)}, u32[]{:S(2)}, u32[]{:S(2)}) collective-permute-start(bf16[256,384]{1,0:T(8,128)(2,1)S(1)} %collective-permute-done.7.refs_2_), channel_id=1, source_target_pairs={{0,4},{4,0},{8,12},{12,8},{1,5},{5,1},{9,13},{13,9},{2,6},{6,2},{1... | collective-permute-start | bytes 589832 | tf_op jit(solution)/shard_map/ppermute | solution.py:259
  46.7 8.3 %collective-permute-start.5 = (bf16[256,384]{1,0:T(8,128)(2,1)S(1)}, bf16[256,384]{1,0:T(8,128)(2,1)S(1)}, u32[]{:S(2)}, u32[]{:S(2)}) collective-permute-start(bf16[256,384]{1,0:T(8,128)(2,1)S(1)} %collective-permute-done.4.refs_0_), channel_id=1, source_target_pairs={{0,4},{4,0},{8,12},{12,8},{1,5},{5,1},{9,13},{13,9},{2,6},{6,2},{1... | collective-permute-start | bytes 589832 | tf_op jit(solution)/shard_map/ppermute | solution.py:259
  54.9 3.0 %copy-start.3 = (f32[64]{0:T(128)S(1)}, f32[64]{0:T(128)}, u32[]{:S(2)}) copy-start(f32[64]{0:T(128)} %param.9) | copy-start | bytes 772
  57.3 1.5 %collective-permute-start.15 = (bf16[256,384]{1,0:T(8,128)(2,1)S(1)}, bf16[256,384]{1,0:T(8,128)(2,1)S(1)}, u32[]{:S(2)}, u32[]{:S(2)}) collective-permute-start(bf16[256,384]{1,0:T(8,128)(2,1)S(1)} %collective-permute-done.14.refs_0_), channel_id=1, source_target_pairs={{0,4},{4,0},{8,12},{12,8},{1,5},{5,1},{9,13},{13,9},{2,6},{6,2},{1... | collective-permute-start | bytes 589832 | tf_op jit(solution)/shard_map/ppermute | solution.py:259
  57.4 1.7 %collective-permute-start.17 = (bf16[256,384]{1,0:T(8,128)(2,1)S(1)}, bf16[256,384]{1,0:T(8,128)(2,1)S(1)}, u32[]{:S(2)}, u32[]{:S(2)}) collective-permute-start(bf16[256,384]{1,0:T(8,128)(2,1)S(1)} %collective-permute-done.16.refs_2_), channel_id=1, source_target_pairs={{0,4},{4,0},{8,12},{12,8},{1,5},{5,1},{9,13},{13,9},{2,6},{6,2},{1... | collective-permute-start | bytes 589832 | tf_op jit(solution)/shard_map/ppermute | solution.py:259

commit v4 on v3

--- a/solution.py
+++ b/solution.py
@@ -71,21 +71,22 @@
         copy.start()
     order_copy.wait()
     lane = lax.broadcasted_iota(jnp.int32, (LANES, LANES), 1)
-    for g in range(own_order.shape[0]):
-        rows = slice(g * LANES, (g + 1) * LANES)
-        wanted = jnp.transpose(jnp.broadcast_to(own_order[g : g + 1, :], (LANES, LANES)))
-        column_ref[rows, :] = wanted
-        wanted = jnp.where(wanted >= half, wanted - half, wanted) - lane
-        for j in range(half // LANES):
-            pick_ref[rows, j * LANES : (j + 1) * LANES] = jnp.where(
-                wanted == j * LANES, 1.0, 0.0
-            ).astype(BF16)
     low_copy.wait()
     high_copy.wait()
-    both = jnp.dot(pick_ref[...], table[...], preferred_element_type=F32)
-    my_loads_ref[...] = jnp.where(
-        column_ref[...] >= half, both[:, columns:], both[:, :columns]
-    ).astype(BF16)
+    for g in range(own_order.shape[0] * LANES // 512):
+        wanteds = []
+        for h in range(512 // LANES):
+            i = g * (512 // LANES) + h
+            wanteds.append(jnp.transpose(jnp.broadcast_to(own_order[i : i + 1, :], (LANES, LANES))))
+        wanted = jnp.concatenate(wanteds, axis=0)
+        low = jnp.where(wanted >= half, wanted - half, wanted) - lax.broadcasted_iota(jnp.int32, wanted.shape, 1)
+        pick = jnp.concatenate(
+            [jnp.where(low == j * LANES, 1.0, 0.0).astype(BF16) for j in range(half // LANES)], axis=1
+        )
+        both = jnp.dot(pick, table[...], preferred_element_type=F32)
+        my_loads_ref[g * 512 : (g + 1) * 512, :] = jnp.where(
+            wanted >= half, both[:, columns:], both[:, :columns]
+        ).astype(BF16)
     for copy in copies:
         copy.wait()
     products(held[...], my_loads_ref[...], out_refs)
@@ -260,12 +261,14 @@
 
     far = list(range(n_patch - 1, n_patch // 2 - 1, -1))
     near = list(range(n_patch // 2 - 1, -1, -1))
-    far_terms, my_loads = first_products(order, loads, influence, share_rows, far)
-    near_terms = more_products(
-        my_loads, influence, share_rows, near, [BF16] * (len(near) - 1) + [F32]
-    )
-    received = [swap(t, "patch", k) for k, t in zip(far + near, list(far_terms) + list(near_terms[:-1]))]
-    own = share_sum(near_terms[-1], received)
+    first_terms, my_loads = first_products(order, loads, influence, share_rows, far[:1])
+    rest = far[1:] + near
+    more_terms = more_products(
+        my_loads, influence, share_rows, rest, [BF16] * (len(rest) - 1) + [F32]
+    )
+    terms = list(first_terms) + list(more_terms)
+    received = [swap(t, "patch", k) for k, t in zip(far + near[:-1], terms)]
+    own = share_sum(terms[-1], received)
 
     position = block_position.reshape(n_hot * n_patch, 1, share_rows)
     top = n_patch // 2

time: 65.6 us -> 62.9 us (0.959)
  Pallas kernels: 22.3 us -> 20.4 us
  waiting for transfers between devices: 19.4 us -> 18.5 us
    pallas_call x1, Pallas kernels: 6.53 us -> 3.81 us  [first_products(): pl.pallas_call(functools.partial(first_kernel, which), out_shape=[share]...]
    pallas_call x1, Pallas kernels: 2.87 us -> 3.76 us  [more_products(): pl.pallas_call(functools.partial(more_kernel, which), out_shape=[jax.Shap...]
    ppermute x18, waiting for transfers between devices: 19.4 us -> 18.5 us  [swap(): return lax.ppermute(array, axis, [(i, i ^ k) for i in range(size)])]
  transfers between devices with their start and end apart: 18 -> 18, of which waited for: 6 -> 5; matrix products, arithmetic and copies ran while one was open for 0% -> 0% of each run, Pallas kernels for 14% -> 16%
where the time goes in v4:
time: 62.9 us; the launch traced here: 62.8 us
  starting transfers between devices  22.6 us (36%)
  Pallas kernels  20.4 us (32%)
  waiting for transfers between devices  18.5 us (29%)
  local copies, waits for them, and re-layouts  1.05 us (2%)
    ppermute x18, starting transfers between devices, swap(): return lax.ppermute(array, axis, [(i, i ^ k) for i in range(size)])  22.6 us
    ppermute x18, waiting for transfers between devices, swap(): return lax.ppermute(array, axis, [(i, i ^ k) for i in range(size)])  18.5 us
    pallas_call x2, Pallas kernels, early_rows(): pl.pallas_call(functools.partial(early_kernel, keys), out_shape=jax.Shape...  6.41 us
    pallas_call x1, Pallas kernels, cross(): pl.pallas_call(functools.partial(cross_kernel, components, keys), out_sha...  6.35 us
    pallas_call x1, Pallas kernels, first_products(): pl.pallas_call(functools.partial(first_kernel, which), out_shape=[share]...  3.81 us
    pallas_call x1, Pallas kernels, more_products(): pl.pallas_call(functools.partial(more_kernel, which), out_shape=[jax.Shap...  3.76 us
  transfers between devices with their start and end apart: 18, of which 5 were waited for; matrix products, arithmetic and copies ran while one was open for 0% of the time, Pallas kernels for 16%

profile of v4, /device:TPU:25, one launch (start us, length us, event | category | flops | bytes accessed | tf_op | source)
XLA Modules:
  0.0 62.8 jit_solution(4671538600553486155)
XLA Ops:
  0.0 3.8 %first_products.1 = (bf16[256,384]{1,0:T(8,128)(2,1)}, bf16[1024,128]{1,0:T(8,128)(2,1)}) custom-call(s32[4,8,128]{2,1,0:T(8,128)} %bitcast.7, bf16[4096,128]{1,0:T(8,128)(2,1)} %loads_ref.1, bf16[3,1024,1024]{2,1,0:T(8,128)(2,1)} %influence_ref.3), custom_call_target="tpu_custom_call" | custom-call | tf_op jit(solution)/shard_map/first_products/pallas_call | solution.py:118
  3.9 0.9 %copy-done = bf16[1024,128]{1,0:T(8,128)(2,1)S(1)} copy-done((bf16[1024,128]{1,0:T(8,128)(2,1)S(1)}, bf16[1024,128]{1,0:T(8,128)(2,1)}, u32[]{:S(2)}) %copy-start) | copy-done | bytes 262168
  4.9 3.8 %more_products.1 = (bf16[256,384]{1,0:T(8,128)(2,1)S(1)}, bf16[256,384]{1,0:T(8,128)(2,1)S(1)}, f32[256,384]{1,0:T(8,128)S(1)}) custom-call(bf16[1024,128]{1,0:T(8,128)(2,1)S(1)} %copy-done, bf16[3,1024,1024]{2,1,0:T(8,128)(2,1)} %influence_ref.3), custom_call_target="tpu_custom_call" | custom-call | flops 805306368 | bytes 18874368 | tf_op jit(solution)/shard_map/more_products/pallas_call | solution.py:142
  8.6 1.4 %collective-permute-start.1 = (bf16[256,384]{1,0:T(8,128)(2,1)S(1)}, bf16[256,384]{1,0:T(8,128)(2,1)S(1)}, u32[]{:S(2)}, u32[]{:S(2)}) collective-permute-start(bf16[256,384]{1,0:T(8,128)(2,1)S(1)} %get-tuple-element.17), channel_id=1, source_target_pairs={{0,2},{1,3},{2,0},{3,1},{4,6},{5,7},{6,4},{7,5},{8,10},{9,11},{10,... | collective-permute-start | bytes 589832 | tf_op jit(solution)/shard_map/ppermute | solution.py:260
  10.0 2.2 %collective-permute-start.2 = (bf16[256,384]{1,0:T(8,128)(2,1)S(1)}, bf16[256,384]{1,0:T(8,128)(2,1)S(1)}, u32[]{:S(2)}, u32[]{:S(2)}) collective-permute-start(bf16[256,384]{1,0:T(8,128)(2,1)S(1)} %get-tuple-element.18), channel_id=1, source_target_pairs={{0,1},{1,0},{2,3},{3,2},{4,5},{5,4},{6,7},{7,6},{8,9},{9,8},{10,11... | collective-permute-start | bytes 589832 | tf_op jit(solution)/shard_map/ppermute | solution.py:260
  12.2 10.2 %collective-permute-done.1.refs_1_ = bf16[256,384]{1,0:T(8,128)(2,1)S(1)} collective-permute-done((bf16[256,384]{1,0:T(8,128)(2,1)S(1)}, bf16[256,384]{1,0:T(8,128)(2,1)S(1)}, u32[]{:S(2)}, u32[]{:S(2)}) %collective-permute-start.1) | collective-permute-done | bytes 196640 | tf_op jit(solution)/shard_map/ppermute | solution.py:260
  22.6 1.5 %collective-permute-start.3 = (bf16[256,384]{1,0:T(8,128)(2,1)S(1)}, bf16[256,384]{1,0:T(8,128)(2,1)S(1)}, u32[]{:S(2)}, u32[]{:S(2)}) collective-permute-start(bf16[256,384]{1,0:T(8,128)(2,1)S(1)} %share_sum.1.refs_0_), channel_id=1, source_target_pairs={{0,2},{1,3},{2,0},{3,1},{4,6},{5,7},{6,4},{7,5},{8,10},{9,11},{10,... | collective-permute-start | bytes 589832 | tf_op jit(solution)/shard_map/ppermute | solution.py:260
  24.1 1.2 %collective-permute-start.11 = (bf16[256,384]{1,0:T(8,128)(2,1)S(1)}, bf16[256,384]{1,0:T(8,128)(2,1)S(1)}, u32[]{:S(2)}, u32[]{:S(2)}) collective-permute-start(bf16[256,384]{1,0:T(8,128)(2,1)S(1)} %share_sum.1.refs_0_), channel_id=1, source_target_pairs={{0,8},{4,12},{8,0},{12,4},{1,9},{5,13},{9,1},{13,5},{2,10},{6,14},... | collective-permute-start | bytes 589832 | tf_op jit(solution)/shard_map/ppermute | solution.py:260
  25.3 2.2 %collective-permute-start.9 = (bf16[256,384]{1,0:T(8,128)(2,1)S(1)}, bf16[256,384]{1,0:T(8,128)(2,1)S(1)}, u32[]{:S(2)}, u32[]{:S(2)}) collective-permute-start(bf16[256,384]{1,0:T(8,128)(2,1)S(1)} %share_sum.1.refs_0_), channel_id=1, source_target_pairs={{0,4},{4,0},{8,12},{12,8},{1,5},{5,1},{9,13},{13,9},{2,6},{6,2},{1... | collective-permute-start | bytes 589832 | tf_op jit(solution)/shard_map/ppermute | solution.py:260
  27.5 3.9 %collective-permute-done.6.refs_2_ = bf16[256,384]{1,0:T(8,128)(2,1)S(1)} collective-permute-done((bf16[256,384]{1,0:T(8,128)(2,1)S(1)}, bf16[256,384]{1,0:T(8,128)(2,1)S(1)}, u32[]{:S(2)}, u32[]{:S(2)}) %collective-permute-start.6) | collective-permute-done | bytes 196640 | tf_op jit(solution)/shard_map/ppermute | solution.py:260
  31.4 3.7 %collective-permute-start.10 = (bf16[256,384]{1,0:T(8,128)(2,1)S(1)}, bf16[256,384]{1,0:T(8,128)(2,1)S(1)}, u32[]{:S(2)}, u32[]{:S(2)}) collective-permute-start(bf16[256,384]{1,0:T(8,128)(2,1)S(1)} %collective-permute-done.6.refs_2_), channel_id=1, source_target_pairs={{0,4},{4,0},{8,12},{12,8},{1,5},{5,1},{9,13},{13,9},{2,6},{6,2},{1... | collective-permute-start | bytes 589832 | tf_op jit(solution)/shard_map/ppermute | solution.py:260
  35.1 1.2 %collective-permute-start.7 = (bf16[256,384]{1,0:T(8,128)(2,1)S(1)}, bf16[256,384]{1,0:T(8,128)(2,1)S(1)}, u32[]{:S(2)}, u32[]{:S(2)}) collective-permute-start(bf16[256,384]{1,0:T(8,128)(2,1)S(1)} %collective-permute-done.6.refs_2_), channel_id=1, source_target_pairs={{0,8},{4,12},{8,0},{12,4},{1,9},{5,13},{9,1},{13,5},{2,10},{6,14},... | collective-permute-start | bytes 589832 | tf_op jit(solution)/shard_map/ppermute | solution.py:260
  36.3 0.3 collective-permute-start.12
  36.9 1.5 %collective-permute-start.14 = (bf16[256,384]{1,0:T(8,128)(2,1)S(1)}, bf16[256,384]{1,0:T(8,128)(2,1)S(1)}, u32[]{:S(2)}, u32[]{:S(2)}) collective-permute-start(bf16[256,384]{1,0:T(8,128)(2,1)S(1)} %collective-permute-done.11.refs_4_), channel_id=1, source_target_pairs={{0,3},{1,2},{2,1},{3,0},{4,7},{5,6},{6,5},{7,4},{8,11},{9,10},{10,... | collective-permute-start | bytes 589832 | tf_op jit(solution)/shard_map/ppermute | solution.py:260
  38.4 3.2 %collective-permute-done.7.refs_2_ = bf16[256,384]{1,0:T(8,128)(2,1)S(1)} collective-permute-done((bf16[256,384]{1,0:T(8,128)(2,1)S(1)}, bf16[256,384]{1,0:T(8,128)(2,1)S(1)}, u32[]{:S(2)}, u32[]{:S(2)}) %collective-permute-start.7) | collective-permute-done | bytes 196640 | tf_op jit(solution)/shard_map/ppermute | solution.py:260
  41.6 1.2 %collective-permute-start.16 = (bf16[256,384]{1,0:T(8,128)(2,1)S(1)}, bf16[256,384]{1,0:T(8,128)(2,1)S(1)}, u32[]{:S(2)}, u32[]{:S(2)}) collective-permute-start(bf16[256,384]{1,0:T(8,128)(2,1)S(1)} %collective-permute-done.3.refs_6_), channel_id=1, source_target_pairs={{0,8},{4,12},{8,0},{12,4},{1,9},{5,13},{9,1},{13,5},{2,10},{6,14},... | collective-permute-start | bytes 589832 | tf_op jit(solution)/shard_map/ppermute | solution.py:260
  42.9 1.1 %collective-permute-start.8 = (bf16[256,384]{1,0:T(8,128)(2,1)S(1)}, bf16[256,384]{1,0:T(8,128)(2,1)S(1)}, u32[]{:S(2)}, u32[]{:S(2)}) collective-permute-start(bf16[256,384]{1,0:T(8,128)(2,1)S(1)} %collective-permute-done.7.refs_2_), channel_id=1, source_target_pairs={{0,4},{4,0},{8,12},{12,8},{1,5},{5,1},{9,13},{13,9},{2,6},{6,2},{1... | collective-permute-start | bytes 589832 | tf_op jit(solution)/shard_map/ppermute | solution.py:260
  43.9 4.2 %collective-permute-start.5 = (bf16[256,384]{1,0:T(8,128)(2,1)S(1)}, bf16[256,384]{1,0:T(8,128)(2,1)S(1)}, u32[]{:S(2)}, u32[]{:S(2)}) collective-permute-start(bf16[256,384]{1,0:T(8,128)(2,1)S(1)} %collective-permute-done.4.refs_0_), channel_id=1, source_target_pairs={{0,4},{4,0},{8,12},{12,8},{1,5},{5,1},{9,13},{13,9},{2,6},{6,2},{1... | collective-permute-start | bytes 589832 | tf_op jit(solution)/shard_map/ppermute | solution.py:260
  48.1 4.0 %early_rows.2.refs_4_ = f32[6,256,384]{2,1,0:T(8,128)S(1)} custom-call(s32[3,2]{1,0:T(4,128)S(1)} %copy.9.pairs_ref, s32[16,1,256]{2,1,0:T(1,128)S(1)} %bitcast.4, bf16[256,384]{1,0:T(8,128)(2,1)S(1)} %share_sum.1.refs_0_, bf16[256,384]{1,0:T(8,128)(2,1)S(1)} %collective-permute-done.9.refs_1_, bf16[256,384]{1,0:T(8,128)(2,1)S(1)} %collective-permute-done.6.refs_2_, ...), custom_call_target="tpu_custom_call" | custom-call | flops 4831838208 | bytes 4718592 | tf_op jit(solution)/shard_map/early_rows/pallas_call | solution.py:194
  52.2 2.4 %early_rows.3.early_ref = f32[6,256,384]{2,1,0:T(8,128)S(1)} custom-call(s32[3,2]{1,0:T(4,128)S(1)} %copy.9.pairs_ref, s32[16,1,256]{2,1,0:T(1,128)S(1)} %bitcast.5, bf16[256,384]{1,0:T(8,128)(2,1)S(1)} %collective-permute-done.4.refs_0_, bf16[256,384]{1,0:T(8,128)(2,1)S(1)} %collective-permute-done.5.refs_1_, ...), custom_call_target="tpu_custom_call" | custom-call | flops 2415919104 | bytes 4718592 | tf_op jit(solution)/shard_map/early_rows/pallas_call | solution.py:194
  54.7 0.5 collective-permute-start.17
  55.3 0.9 %collective-permute-done.15.refs_1_ = bf16[256,384]{1,0:T(8,128)(2,1)S(1)} collective-permute-done((bf16[256,384]{1,0:T(8,128)(2,1)S(1)}, bf16[256,384]{1,0:T(8,128)(2,1)S(1)}, u32[]{:S(2)}, u32[]{:S(2)}) %collective-permute-start.15) | collective-permute-done | bytes 196640 | tf_op jit(solution)/shard_map/ppermute | solution.py:260
  56.1 0.3 collective-permute-done.17.refs_3_
  56.4 6.4 %cross.1 = bf16[3,2,768,768]{3,2,1,0:T(8,128)(2,1)} custom-call(s32[3,2]{1,0:T(4,128)S(1)} %copy.9.pairs_ref, s32[16,1,256]{2,1,0:T(1,128)S(1)} %bitcast.6, f32[1,128]{1,0:T(1,128)S(1)} %maximum_bitcast_fusion.weights_ref, f32[6,256,384]{2,1,0:T(8,128)S(1)} %early_rows.3.early_ref, bf16[256,384]{1,0:T(8,128)(2,1)S(1)} %collective-permute-done.14.refs_0_, ...), custom_call_target="tpu_custom_call" | custom-call | tf_op jit(solution)/shard_map/cross/pallas_call | solution.py:233
  (28 shorter events, 0.8 us)
Async XLA Ops:
  0.0 36.8 %copy-start.2 = (s32[3,2]{0,1:T(2,128)S(1)}, s32[3,2]{0,1:T(2,128)}, u32[]{:S(2)}) copy-start(s32[3,2]{0,1:T(2,128)} %param.11) | copy-start | bytes 76
  0.0 48.1 %copy-start.1 = (s32[4096]{0:T(1024)S(1)}, s32[4096]{0:T(1024)}, u32[]{:S(2)}) copy-start(s32[4096]{0:T(1024)} %param.10) | copy-start | bytes 49156
  3.8 8.4 %collective-permute-start = (bf16[256,384]{1,0:T(8,128)(2,1)}, bf16[256,384]{1,0:T(8,128)(2,1)S(1)}, u32[]{:S(2)}, u32[]{:S(2)}) collective-permute-start(bf16[256,384]{1,0:T(8,128)(2,1)} %get-tuple-element.16), channel_id=1, source_target_pairs={{0,3},{1,2},{2,1},{3,0},{4,7},{5,6},{6,5},{7,4},{8,11},{9,10},{10,... | collective-permute-start | bytes 589832 | tf_op jit(solution)/shard_map/ppermute | solution.py:260
  3.9 1.0 %copy-start = (bf16[1024,128]{1,0:T(8,128)(2,1)S(1)}, bf16[1024,128]{1,0:T(8,128)(2,1)}, u32[]{:S(2)}) copy-start(bf16[1024,128]{1,0:T(8,128)(2,1)} %get-tuple-element.14.my_loads_ref) | copy-start | bytes 786436
  8.6 13.8 %collective-permute-start.1 = (bf16[256,384]{1,0:T(8,128)(2,1)S(1)}, bf16[256,384]{1,0:T(8,128)(2,1)S(1)}, u32[]{:S(2)}, u32[]{:S(2)}) collective-permute-start(bf16[256,384]{1,0:T(8,128)(2,1)S(1)} %get-tuple-element.17), channel_id=1, source_target_pairs={{0,2},{1,3},{2,0},{3,1},{4,6},{5,7},{6,4},{7,5},{8,10},{9,11},{10,... | collective-permute-start | bytes 589832 | tf_op jit(solution)/shard_map/ppermute | solution.py:260
  10.0 12.4 %collective-permute-start.2 = (bf16[256,384]{1,0:T(8,128)(2,1)S(1)}, bf16[256,384]{1,0:T(8,128)(2,1)S(1)}, u32[]{:S(2)}, u32[]{:S(2)}) collective-permute-start(bf16[256,384]{1,0:T(8,128)(2,1)S(1)} %get-tuple-element.18), channel_id=1, source_target_pairs={{0,1},{1,0},{2,3},{3,2},{4,5},{5,4},{6,7},{7,6},{8,9},{9,8},{10,11... | collective-permute-start | bytes 589832 | tf_op jit(solution)/shard_map/ppermute | solution.py:260
  22.5 8.9 %collective-permute-start.6 = (bf16[256,384]{1,0:T(8,128)(2,1)S(1)}, bf16[256,384]{1,0:T(8,128)(2,1)S(1)}, u32[]{:S(2)}, u32[]{:S(2)}) collective-permute-start(bf16[256,384]{1,0:T(8,128)(2,1)S(1)} %share_sum.1.refs_0_), channel_id=1, source_target_pairs={{0,1},{1,0},{2,3},{3,2},{4,5},{5,4},{6,7},{7,6},{8,9},{9,8},{10,11... | collective-permute-start | bytes 589832 | tf_op jit(solution)/shard_map/ppermute | solution.py:260
  22.6 8.9 %collective-permute-start.3 = (bf16[256,384]{1,0:T(8,128)(2,1)S(1)}, bf16[256,384]{1,0:T(8,128)(2,1)S(1)}, u32[]{:S(2)}, u32[]{:S(2)}) collective-permute-start(bf16[256,384]{1,0:T(8,128)(2,1)S(1)} %share_sum.1.refs_0_), channel_id=1, source_target_pairs={{0,2},{1,3},{2,0},{3,1},{4,6},{5,7},{6,4},{7,5},{8,10},{9,11},{10,... | collective-permute-start | bytes 589832 | tf_op jit(solution)/shard_map/ppermute | solution.py:260
  24.1 12.2 %collective-permute-start.11 = (bf16[256,384]{1,0:T(8,128)(2,1)S(1)}, bf16[256,384]{1,0:T(8,128)(2,1)S(1)}, u32[]{:S(2)}, u32[]{:S(2)}) collective-permute-start(bf16[256,384]{1,0:T(8,128)(2,1)S(1)} %share_sum.1.refs_0_), channel_id=1, source_target_pairs={{0,8},{4,12},{8,0},{12,4},{1,9},{5,13},{9,1},{13,5},{2,10},{6,14},... | collective-permute-start | bytes 589832 | tf_op jit(solution)/shard_map/ppermute | solution.py:260
  25.3 11.3 %collective-permute-start.9 = (bf16[256,384]{1,0:T(8,128)(2,1)S(1)}, bf16[256,384]{1,0:T(8,128)(2,1)S(1)}, u32[]{:S(2)}, u32[]{:S(2)}) collective-permute-start(bf16[256,384]{1,0:T(8,128)(2,1)S(1)} %share_sum.1.refs_0_), channel_id=1, source_target_pairs={{0,4},{4,0},{8,12},{12,8},{1,5},{5,1},{9,13},{13,9},{2,6},{6,2},{1... | collective-permute-start | bytes 589832 | tf_op jit(solution)/shard_map/ppermute | solution.py:260
  31.4 5.5 %collective-permute-start.10 = (bf16[256,384]{1,0:T(8,128)(2,1)S(1)}, bf16[256,384]{1,0:T(8,128)(2,1)S(1)}, u32[]{:S(2)}, u32[]{:S(2)}) collective-permute-start(bf16[256,384]{1,0:T(8,128)(2,1)S(1)} %collective-permute-done.6.refs_2_), channel_id=1, source_target_pairs={{0,4},{4,0},{8,12},{12,8},{1,5},{5,1},{9,13},{13,9},{2,6},{6,2},{1... | collective-permute-start | bytes 589832 | tf_op jit(solution)/shard_map/ppermute | solution.py:260
  35.1 6.5 %collective-permute-start.7 = (bf16[256,384]{1,0:T(8,128)(2,1)S(1)}, bf16[256,384]{1,0:T(8,128)(2,1)S(1)}, u32[]{:S(2)}, u32[]{:S(2)}) collective-permute-start(bf16[256,384]{1,0:T(8,128)(2,1)S(1)} %collective-permute-done.6.refs_2_), channel_id=1, source_target_pairs={{0,8},{4,12},{8,0},{12,4},{1,9},{5,13},{9,1},{13,5},{2,10},{6,14},... | collective-permute-start | bytes 589832 | tf_op jit(solution)/shard_map/ppermute | solution.py:260
  36.3 6.5 %collective-permute-start.12 = (bf16[256,384]{1,0:T(8,128)(2,1)S(1)}, bf16[256,384]{1,0:T(8,128)(2,1)S(1)}, u32[]{:S(2)}, u32[]{:S(2)}) collective-permute-start(bf16[256,384]{1,0:T(8,128)(2,1)S(1)} %collective-permute-done.11.refs_4_), channel_id=1, source_target_pairs={{0,4},{4,0},{8,12},{12,8},{1,5},{5,1},{9,13},{13,9},{2,6},{6,2},{1... | collective-permute-start | bytes 589832 | tf_op jit(solution)/shard_map/ppermute | solution.py:260
  36.6 7.3 %collective-permute-start.4 = (bf16[256,384]{1,0:T(8,128)(2,1)S(1)}, bf16[256,384]{1,0:T(8,128)(2,1)S(1)}, u32[]{:S(2)}, u32[]{:S(2)}) collective-permute-start(bf16[256,384]{1,0:T(8,128)(2,1)S(1)} %collective-permute-done.3.refs_6_), channel_id=1, source_target_pairs={{0,1},{1,0},{2,3},{3,2},{4,5},{5,4},{6,7},{7,6},{8,9},{9,8},{10,11... | collective-permute-start | bytes 589832 | tf_op jit(solution)/shard_map/ppermute | solution.py:260
  36.6 11.5 %collective-permute-start.13 = (bf16[256,384]{1,0:T(8,128)(2,1)S(1)}, bf16[256,384]{1,0:T(8,128)(2,1)S(1)}, u32[]{:S(2)}, u32[]{:S(2)}) collective-permute-start(bf16[256,384]{1,0:T(8,128)(2,1)S(1)} %collective-permute-done.3.refs_6_), channel_id=1, source_target_pairs={{0,4},{4,0},{8,12},{12,8},{1,5},{5,1},{9,13},{13,9},{2,6},{6,2},{1... | collective-permute-start | bytes 589832 | tf_op jit(solution)/shard_map/ppermute | solution.py:260
  36.9 17.7 %collective-permute-start.14 = (bf16[256,384]{1,0:T(8,128)(2,1)S(1)}, bf16[256,384]{1,0:T(8,128)(2,1)S(1)}, u32[]{:S(2)}, u32[]{:S(2)}) collective-permute-start(bf16[256,384]{1,0:T(8,128)(2,1)S(1)} %collective-permute-done.11.refs_4_), channel_id=1, source_target_pairs={{0,3},{1,2},{2,1},{3,0},{4,7},{5,6},{6,5},{7,4},{8,11},{9,10},{10,... | collective-permute-start | bytes 589832 | tf_op jit(solution)/shard_map/ppermute | solution.py:260
  41.6 13.0 %collective-permute-start.16 = (bf16[256,384]{1,0:T(8,128)(2,1)S(1)}, bf16[256,384]{1,0:T(8,128)(2,1)S(1)}, u32[]{:S(2)}, u32[]{:S(2)}) collective-permute-start(bf16[256,384]{1,0:T(8,128)(2,1)S(1)} %collective-permute-done.3.refs_6_), channel_id=1, source_target_pairs={{0,8},{4,12},{8,0},{12,4},{1,9},{5,13},{9,1},{13,5},{2,10},{6,14},... | collective-permute-start | bytes 589832 | tf_op jit(solution)/shard_map/ppermute | solution.py:260
  42.9 9.3 %collective-permute-start.8 = (bf16[256,384]{1,0:T(8,128)(2,1)S(1)}, bf16[256,384]{1,0:T(8,128)(2,1)S(1)}, u32[]{:S(2)}, u32[]{:S(2)}) collective-permute-start(bf16[256,384]{1,0:T(8,128)(2,1)S(1)} %collective-permute-done.7.refs_2_), channel_id=1, source_target_pairs={{0,4},{4,0},{8,12},{12,8},{1,5},{5,1},{9,13},{13,9},{2,6},{6,2},{1... | collective-permute-start | bytes 589832 | tf_op jit(solution)/shard_map/ppermute | solution.py:260
  43.9 8.3 %collective-permute-start.5 = (bf16[256,384]{1,0:T(8,128)(2,1)S(1)}, bf16[256,384]{1,0:T(8,128)(2,1)S(1)}, u32[]{:S(2)}, u32[]{:S(2)}) collective-permute-start(bf16[256,384]{1,0:T(8,128)(2,1)S(1)} %collective-permute-done.4.refs_0_), channel_id=1, source_target_pairs={{0,4},{4,0},{8,12},{12,8},{1,5},{5,1},{9,13},{13,9},{2,6},{6,2},{1... | collective-permute-start | bytes 589832 | tf_op jit(solution)/shard_map/ppermute | solution.py:260
  52.2 3.0 %copy-start.3 = (f32[64]{0:T(128)S(1)}, f32[64]{0:T(128)}, u32[]{:S(2)}) copy-start(f32[64]{0:T(128)} %param.9) | copy-start | bytes 772
  54.6 1.5 %collective-permute-start.15 = (bf16[256,384]{1,0:T(8,128)(2,1)S(1)}, bf16[256,384]{1,0:T(8,128)(2,1)S(1)}, u32[]{:S(2)}, u32[]{:S(2)}) collective-permute-start(bf16[256,384]{1,0:T(8,128)(2,1)S(1)} %collective-permute-done.14.refs_0_), channel_id=1, source_target_pairs={{0,4},{4,0},{8,12},{12,8},{1,5},{5,1},{9,13},{13,9},{2,6},{6,2},{1... | collective-permute-start | bytes 589832 | tf_op jit(solution)/shard_map/ppermute | solution.py:260
  54.7 1.7 %collective-permute-start.17 = (bf16[256,384]{1,0:T(8,128)(2,1)S(1)}, bf16[256,384]{1,0:T(8,128)(2,1)S(1)}, u32[]{:S(2)}, u32[]{:S(2)}) collective-permute-start(bf16[256,384]{1,0:T(8,128)(2,1)S(1)} %collective-permute-done.16.refs_2_), channel_id=1, source_target_pairs={{0,4},{4,0},{8,12},{12,8},{1,5},{5,1},{9,13},{13,9},{2,6},{6,2},{1... | collective-permute-start | bytes 589832 | tf_op jit(solution)/shard_map/ppermute | solution.py:260

commit v5 on v4

v5 whole, which is shorter than its diff:
```python
import functools
import math

import jax
import jax.numpy as jnp
from jax import lax
from jax.experimental import pallas as pl
from jax.experimental.pallas import tpu as pltpu
from jax.sharding import PartitionSpec as P

BLK = 256
LANES = 128
F32 = jnp.float32
BF16 = jnp.bfloat16
VMEM_BYTES = 48 * 1024 * 1024
FIRST_VMEM_BYTES = 124 * 512 * 1024


def params(steps=1):
    return pltpu.CompilerParams(
        dimension_semantics=("arbitrary",) * steps, vmem_limit_bytes=VMEM_BYTES
    )


def cost(flops, bytes_accessed):
    return pl.CostEstimate(flops=flops, bytes_accessed=bytes_accessed, transcendentals=0)


def products(influence, my_loads, cuts, out_refs):
    components = influence.shape[1]
    columns = my_loads.shape[1]
    for (i, top, rows, kind), out_ref in zip(cuts, out_refs):
        for c in range(components):
            part = jnp.dot(influence[i, c, top : top + rows], my_loads, preferred_element_type=F32)
            out_ref[:, c * columns : (c + 1) * columns] = part.astype(kind)


def share_copies(influence_ref, held_ref, sems, which):
    rows = held_ref.shape[2]
    here = lax.axis_index("patch")
    return [
        pltpu.make_async_copy(
            influence_ref.at[:, pl.ds(pl.multiple_of((here ^ k) * rows, rows), rows), :],
            held_ref.at[i],
            sems.at[i],
        )
        for i, k in enumerate(which)
    ]


def first_kernel(which, cuts, order_ref, loads_ref, influence_ref, *refs):
    out_refs, (my_loads_ref, own_order, column_ref, table, pick_ref, held, sems) = refs[:-7], refs[-7:]
    columns = loads_ref.shape[1]
    half = loads_ref.shape[0] // 2
    order_copy = pltpu.make_async_copy(order_ref.at[lax.axis_index("patch")], own_order, sems.at[0])
    low_copy = pltpu.make_async_copy(
        loads_ref.at[pl.ds(0, half)], table.at[:, pl.ds(0, columns)], sems.at[1]
    )
    high_copy = pltpu.make_async_copy(
        loads_ref.at[pl.ds(half, half)], table.at[:, pl.ds(columns, columns)], sems.at[2]
    )
    copies = share_copies(influence_ref, held, sems.at[pl.ds(3, len(which))], which)
    order_copy.start()
    low_copy.start()
    high_copy.start()
    for copy in copies:
        copy.start()
    order_copy.wait()
    lane = lax.broadcasted_iota(jnp.int32, (LANES, LANES), 1)
    low_copy.wait()
    high_copy.wait()
    for g in range(own_order.shape[0] * LANES // 512):
        wanteds = []
        for h in range(512 // LANES):
            i = g * (512 // LANES) + h
            wanteds.append(jnp.transpose(jnp.broadcast_to(own_order[i : i + 1, :], (LANES, LANES))))
        wanted = jnp.concatenate(wanteds, axis=0)
        low = jnp.where(wanted >= half, wanted - half, wanted) - lax.broadcasted_iota(jnp.int32, wanted.shape, 1)
        pick = jnp.concatenate(
            [jnp.where(low == j * LANES, 1.0, 0.0).astype(BF16) for j in range(half // LANES)], axis=1
        )
        both = jnp.dot(pick, table[...], preferred_element_type=F32)
        my_loads_ref[g * 512 : (g + 1) * 512, :] = jnp.where(
            wanted >= half, both[:, columns:], both[:, :columns]
        ).astype(BF16)
    for copy in copies:
        copy.wait()
    products(held[...], my_loads_ref[...], cuts, out_refs)


def more_kernel(which, cuts, my_loads_ref, influence_ref, *refs):
    out_refs, (held, sems) = refs[:-2], refs[-2:]
    copies = share_copies(influence_ref, held, sems, which)
    for copy in copies:
        copy.start()
    for copy in copies:
        copy.wait()
    products(held[...], my_loads_ref[...], cuts, out_refs)


def vmem():
    return pl.BlockSpec(memory_space=pltpu.VMEM)


def hbm():
    return pl.BlockSpec(memory_space=pltpu.HBM)


def first_products(order, loads, influence, share_rows, which, cuts):
    components, _, patch_cols = influence.shape
    patches, columns = loads.shape
    cut_shapes = [jax.ShapeDtypeStruct((cut[2], components * columns), cut[3]) for cut in cuts]
    held = (len(which), components, share_rows, patch_cols)
    out = pl.pallas_call(
        functools.partial(first_kernel, which, cuts),
        out_shape=cut_shapes + [jax.ShapeDtypeStruct((patch_cols, columns), BF16)],
        in_specs=[hbm()] * 3,
        out_specs=[vmem()] * (len(cuts) + 1),
        scratch_shapes=[
            pltpu.VMEM(order.shape[1:], jnp.int32),
            pltpu.VMEM((patch_cols, columns), jnp.int32),
            pltpu.VMEM((patches // 2, 2 * columns), BF16),
            pltpu.VMEM((patch_cols, patches // 2), BF16),
            pltpu.VMEM(held, BF16),
            pltpu.SemaphoreType.DMA((3 + len(which),)),
        ],
        compiler_params=pltpu.CompilerParams(vmem_limit_bytes=FIRST_VMEM_BYTES),
        name="first_products",
    )(order, loads, influence)
    return out[:-1], out[-1]


def more_products(my_loads, influence, share_rows, which, cuts):
    components, _, patch_cols = influence.shape
    columns = my_loads.shape[1]
    cut_shapes = [jax.ShapeDtypeStruct((cut[2], components * columns), cut[3]) for cut in cuts]
    held = (len(which), components, share_rows, patch_cols)
    return pl.pallas_call(
        functools.partial(more_kernel, which, cuts),
        out_shape=cut_shapes,
        in_specs=[vmem(), hbm()],
        out_specs=[vmem()] * len(cuts),
        scratch_shapes=[pltpu.VMEM(held, BF16), pltpu.SemaphoreType.DMA((len(which),))],
        compiler_params=pltpu.CompilerParams(vmem_limit_bytes=VMEM_BYTES),
        cost_estimate=cost(2 * columns * math.prod(held), 2 * math.prod(held)),
        name="more_products",
    )(my_loads, influence)


def sum_kernel(kind, own_ref, *refs):
    total = own_ref[...]
    for ref in refs[:-1]:
        total = total + ref[...].astype(F32)
    refs[-1][...] = total.astype(kind)


def total_kernel(near, own_ref, *refs):
    out_ref, half = refs[-1], refs[-2].shape[0]
    for top, terms in ((0, refs[near:-2]), (half, refs[-2:-1])):
        rows = slice(top, top + half)
        total = own_ref[rows, :]
        for ref in refs[:near]:
            total = total + ref[rows, :].astype(F32)
        for ref in terms:
            total = total + ref[...].astype(F32)
        out_ref[rows, :] = total.astype(BF16)


def summed(kernel, own, others, name):
    return pl.pallas_call(
        kernel,
        out_shape=jax.ShapeDtypeStruct(own.shape, BF16),
        in_specs=[vmem()] * (1 + len(others)),
        out_specs=vmem(),
        compiler_params=pltpu.CompilerParams(vmem_limit_bytes=VMEM_BYTES),
        name=name,
    )(own, *others)


def pick_rows(position_ref, key, block):
    n_patch = lax.axis_size("patch")
    place = (lax.axis_index("hot") ^ key[0]) * n_patch + (lax.axis_index("patch") ^ key[1])
    rows = position_ref.shape[2]
    offset = position_ref[place] - block * BLK
    return jnp.where(offset == lax.broadcasted_iota(jnp.int32, (BLK, rows), 0), 1.0, 0.0).astype(BF16)


def pick_group(position_ref, groups, block):
    picks = [pick_rows(position_ref, key, block) for keys in groups for key in keys]
    return jnp.concatenate(picks, axis=1)


def join_kernel(*refs):
    rows = refs[0].shape[0]
    for i, ref in enumerate(refs[:-1]):
        refs[-1][i * rows : (i + 1) * rows, :] = ref[...]


def join(pieces):
    rows, width = pieces[0].shape
    return pl.pallas_call(
        join_kernel,
        out_shape=jax.ShapeDtypeStruct((len(pieces) * rows, width), BF16),
        in_specs=[vmem()] * len(pieces),
        out_specs=vmem(),
        compiler_params=pltpu.CompilerParams(vmem_limit_bytes=VMEM_BYTES),
        name="join",
    )(*pieces)


def early_kernel(groups, pairs_ref, position_ref, *refs):
    count = len(groups)
    pieces, befores, (out_ref, joined_ref) = refs[:count], refs[count:-2], refs[-2:]
    rows = pieces[0].shape[0]
    for i, piece in enumerate(pieces):
        joined_ref[i * rows : (i + 1) * rows, :] = piece[...]
    for s in range(out_ref.shape[0]):
        pick = pick_group(position_ref, groups, pairs_ref[s // 2, s % 2])
        total = jnp.dot(pick, joined_ref[...], preferred_element_type=F32)
        out_ref[s] = total + befores[0][s] if befores else total


def early_rows(pairs, position, groups, pieces, before=()):
    count = pairs.shape[0] * 2
    rows, width = pieces[0].shape
    flops = 2 * count * BLK * rows * width * len(groups)
    return pl.pallas_call(
        functools.partial(early_kernel, groups),
        out_shape=jax.ShapeDtypeStruct((count, BLK, width), F32),
        in_specs=[pl.BlockSpec(memory_space=pltpu.SMEM)] + [vmem()] * (1 + len(pieces) + len(before)),
        out_specs=vmem(),
        scratch_shapes=[pltpu.VMEM((len(groups) * rows, width), BF16)],
        compiler_params=pltpu.CompilerParams(vmem_limit_bytes=VMEM_BYTES),
        cost_estimate=cost(2 * flops, 8 * count * BLK * width),
        name="early_rows",
    )(pairs, position, *pieces, *before)


def cross_kernel(components, groups, pairs_ref, position_ref, weights_ref, early_ref, *refs):
    pieces, (out_ref, left_ref, right_ref, joined_ref) = refs[:-4], refs[-4:]
    q = pl.program_id(0)
    columns = weights_ref.shape[1]
    rows = pieces[0].shape[0]

    @pl.when(q == 0)
    def _():
        for i, piece in enumerate(pieces):
            joined_ref[i * rows : (i + 1) * rows, :] = piece[...]

    for side, rows_ref in ((0, left_ref), (1, right_ref)):
        pick = pick_group(position_ref, groups, pairs_ref[q, side])
        total = jnp.dot(pick, joined_ref[...], preferred_element_type=F32) + early_ref[2 * q + side]
        for c in range(components):
            rows_ref[pl.ds(c, BLK, stride=components), :] = total[:, c * columns : (c + 1) * columns]
    scaled = (left_ref[...] * weights_ref[...]).astype(BF16)
    right = right_ref[...]
    lane = lax.broadcasted_iota(jnp.int32, right.shape, 1)
    turned = pltpu.roll(right, columns // 2, 1)
    turned = jnp.where(lane < columns // 2, -turned, turned)
    for part, other in ((0, right), (1, turned)):
        out_ref[0, part] = lax.dot_general(
            scaled, other.astype(BF16), (((1,), (1,)), ((), ())), preferred_element_type=F32
        ).astype(BF16)


def cross(pairs, position, weights, early, groups, pieces, components):
    count = pairs.shape[0]
    columns = weights.shape[1]
    rows = BLK * components
    return pl.pallas_call(
        functools.partial(cross_kernel, components, groups),
        out_shape=jax.ShapeDtypeStruct((count, 2, rows, rows), BF16),
        grid=(count,),
        in_specs=[pl.BlockSpec(memory_space=pltpu.SMEM)] + [vmem()] * (3 + len(pieces)),
        out_specs=pl.BlockSpec((1, 2, rows, rows), lambda i: (i, 0, 0, 0)),
        scratch_shapes=[
            pltpu.VMEM((rows, columns), F32),
            pltpu.VMEM((rows, columns), F32),
            pltpu.VMEM((len(pieces) * pieces[0].shape[0], components * columns), BF16),
        ],
        compiler_params=params(),
        name="cross",
    )(pairs, position, weights, early, *pieces)


def shards(influence, loads, patch_order, spectral_weights, block_position, block_pairs):
    components, hot_rows, patch_cols = influence.shape
    n_patch, n_hot = lax.axis_size("patch"), lax.axis_size("hot")
    share_rows = hot_rows // n_patch
    weights = jnp.concatenate([spectral_weights, spectral_weights])[None, :]
    order = patch_order.reshape(n_patch, patch_cols // LANES, LANES)

    def swap(array, axis, k):
        size = lax.axis_size(axis)
        return lax.ppermute(array, axis, [(i, i ^ k) for i in range(size)])

    far = list(range(n_patch - 1, n_patch // 2 - 1, -1))
    near = list(range(n_patch // 2 - 1, -1, -1))
    tie = lambda value, *after: lax.optimization_barrier((value, *after))[0]

    top = n_patch // 2
    half = share_rows // 2

    def halves(i, kind):
        return [(i, 0, half, BF16), (i, half, half, kind)]

    first_terms, my_loads = first_products(
        order, loads, influence, share_rows, far[:1], halves(0, BF16 if n_patch > 2 else F32)
    )
    rest = far[1:] + near
    cuts = []
    for i, k in enumerate(rest):
        if k >= top:
            cuts += halves(i, BF16 if k > top else F32)
        else:
            cuts.append((i, 0, share_rows, BF16 if k else F32))
    terms = list(first_terms) + list(more_products(my_loads, influence, share_rows, rest, cuts))
    straight = dict(zip(far, terms[0 : 2 * len(far) : 2]))
    lower = dict(zip(far, terms[1 : 2 * len(far) : 2]))
    carried = [swap(lower[k], "patch", k ^ top) for k in far if k != top]
    from_far = [swap(straight[k], "patch", k) for k in far]
    from_near = [
        swap(tie(term, *carried), "patch", k) for k, term in zip(near[:-1], terms[2 * len(far) :])
    ]
    passed = swap(
        summed(functools.partial(sum_kernel, BF16), tie(lower[top], *from_far[:-1]), carried, "pass_sum"), "patch", top
    )
    own = summed(
        functools.partial(total_kernel, len(from_near)), terms[-1], from_near + from_far + [passed], "share_sum"
    )

    position = block_position.reshape(n_hot * n_patch, 1, share_rows)
    patch_bits = [1 << b for b in reversed(range((n_patch - 1).bit_length()))]
    chip_bits = [2 << b for b in reversed(range((n_hot // 2 - 1).bit_length()))]

    plane = {(0, 0): own}

    def along(keys, axis, bits):
        for bit in bits:
            for j, k in list(keys):
                key = (j ^ bit, k) if axis == "hot" else (j, k ^ bit)
                plane[key] = swap(plane[j, k], axis, bit)
                keys = keys + [key]
        return keys

    def cores(keys, *after):
        mine = join([plane[key] for key in keys])
        other = swap(tie(mine, *after), "hot", 1)
        return [keys, [(j + 1, k) for j, k in keys]], [mine, other]

    def picked(group, *before):
        return early_rows(block_pairs, position, *group, before)

    along([(0, 0)], "patch", patch_bits[:1])
    near_keys = along([(0, 0)], "patch", patch_bits[1:])
    chip_keys = along([(0, 0)], "hot", chip_bits)
    head = cores([(0, 0)])
    early = picked(head)
    for key in near_keys[1:] + chip_keys[1:]:
        plane[key] = tie(plane[key], plane[0, top])
    far_keys = along([(0, top)], "patch", patch_bits[1:])
    for j, _ in chip_keys[1:]:
        start = tie(plane[j, 0], plane[0, top])
        plane[j, n_patch - 1] = swap(start, "patch", n_patch - 1)
    middle = []
    for key in near_keys[1:]:
        middle += along([key], "hot", chip_bits)[1:]
    for key in far_keys[:-1]:
        along([key], "hot", chip_bits)
    early = picked(cores(near_keys[1:] + chip_keys[1:] + [(0, top)], head[1][1]), early)
    before = early
    early = picked(cores(middle + far_keys[1:]), early)
    done = chip_keys + near_keys + [(0, top)] + middle + far_keys
    last = [key for key in plane if key not in done]
    for key in last:
        plane[key] = tie(plane[key], before)
    groups, pieces = cores(last)
    return cross(block_pairs, position, weights, early, groups, pieces, components)


def solution(mesh):
    placed = (
        P(None, "hot", "patch"),
        P("grp", None),
        P(),
        P("grp"),
        P(),
        P(("hot", "patch"), None),
    )
    return jax.shard_map(
        shards,
        mesh=mesh,
        in_specs=placed,
        out_specs=P(("grp", "hot", "patch"), None, None, None),
        check_vma=False,
    )
```

time: 62.9 us -> 58 us (0.922)
  the two profiles are of different devices: /device:TPU:25 before, /device:TPU:0 now
where the time goes in v5:
time: 58 us; the launch traced here: 57.8 us
  Pallas kernels  21.5 us (37%)
  starting transfers between devices  18.7 us (32%)
  waiting for transfers between devices  16.3 us (28%)
  local copies, waits for them, and re-layouts  1.06 us (2%)
    ppermute x16, starting transfers between devices, swap(): return lax.ppermute(array, axis, [(i, i ^ k) for i in range(size)])  18.7 us
    ppermute x16, waiting for transfers between devices, swap(): return lax.ppermute(array, axis, [(i, i ^ k) for i in range(size)])  16.3 us
    pallas_call x3, Pallas kernels, early_rows(): pl.pallas_call(functools.partial(early_kernel, groups), out_shape=jax.Sha...  7.19 us
    pallas_call x1, Pallas kernels, cross(): pl.pallas_call(functools.partial(cross_kernel, components, groups), out_s...  6.48 us
    pallas_call x1, Pallas kernels, first_products(): pl.pallas_call(functools.partial(first_kernel, which, cuts), out_shape=cu...  3.84 us
    pallas_call x1, Pallas kernels, more_products(): pl.pallas_call(functools.partial(more_kernel, which, cuts), out_shape=cut...  3.76 us
  transfers between devices with their start and end apart: 16, of which 7 were waited for; matrix products, arithmetic and copies ran while one was open for 0% of the time, Pallas kernels for 19%

profile of v5, /device:TPU:0, one launch (start us, length us, event | category | flops | bytes accessed | tf_op | source)
XLA Modules:
  0.0 57.8 jit_solution(16304165196309337896)
XLA Ops:
  0.0 3.8 %first_products.1 = (bf16[128,384]{1,0:T(8,128)(2,1)}, bf16[128,384]{1,0:T(8,128)(2,1)}, bf16[1024,128]{1,0:T(8,128)(2,1)}) custom-call(s32[4,8,128]{2,1,0:T(8,128)} %bitcast.8, bf16[4096,128]{1,0:T(8,128)(2,1)} %loads_ref.1, bf16[3,1024,1024]{2,1,0:T(8,128)(2,1)} %influence_ref.3), custom_call_target="tpu_custom_call" | custom-call | tf_op jit(solution)/shard_map/first_products/pallas_call | solution.py:114
  3.9 3.1 %collective-permute-start = (bf16[128,384]{1,0:T(8,128)(2,1)}, bf16[128,384]{1,0:T(8,128)(2,1)S(1)}, u32[]{:S(2)}, u32[]{:S(2)}) collective-permute-start(bf16[128,384]{1,0:T(8,128)(2,1)} %get-tuple-element.23), channel_id=1, source_target_pairs={{0,1},{1,0},{2,3},{3,2},{4,5},{5,4},{6,7},{7,6},{8,9},{9,8},{10,11... | collective-permute-start | bytes 294920 | tf_op jit(solution)/shard_map/ppermute | solution.py:295
  6.9 2.5 %collective-permute-start.2 = (bf16[128,384]{1,0:T(8,128)(2,1)}, bf16[128,384]{1,0:T(8,128)(2,1)S(1)}, u32[]{:S(2)}, u32[]{:S(2)}) collective-permute-start(bf16[128,384]{1,0:T(8,128)(2,1)} %get-tuple-element.25), channel_id=1, source_target_pairs={{0,3},{1,2},{2,1},{3,0},{4,7},{5,6},{6,5},{7,4},{8,11},{9,10},{10,... | collective-permute-start | bytes 294920 | tf_op jit(solution)/shard_map/ppermute | solution.py:295
  9.4 0.9 %copy-done = bf16[1024,128]{1,0:T(8,128)(2,1)S(1)} copy-done((bf16[1024,128]{1,0:T(8,128)(2,1)S(1)}, bf16[1024,128]{1,0:T(8,128)(2,1)}, u32[]{:S(2)}) %copy-start) | copy-done | bytes 262168
  10.4 3.8 %more_products.1 = (bf16[128,384]{1,0:T(8,128)(2,1)S(1)}, f32[128,384]{1,0:T(8,128)S(1)}, bf16[256,384]{1,0:T(8,128)(2,1)S(1)}, f32[256,384]{1,0:T(8,128)S(1)}) custom-call(bf16[1024,128]{1,0:T(8,128)(2,1)S(1)} %copy-done, bf16[3,1024,1024]{2,1,0:T(8,128)(2,1)} %influence_ref.3), custom_call_target="tpu_custom_call" | custom-call | flops 603979776 | bytes 4718592 | tf_op jit(solution)/shard_map/more_products/pallas_call | solution.py:138
  14.2 0.7 %collective-permute-start.1 = (bf16[256,384]{1,0:T(8,128)(2,1)S(1)}, bf16[256,384]{1,0:T(8,128)(2,1)S(1)}, u32[]{:S(2)}, u32[]{:S(2)}) collective-permute-start(bf16[256,384]{1,0:T(8,128)(2,1)S(1)} %get-tuple-element.24), channel_id=1, source_target_pairs={{0,1},{1,0},{2,3},{3,2},{4,5},{5,4},{6,7},{7,6},{8,9},{9,8},{10,11... | collective-permute-start | bytes 589832 | tf_op jit(solution)/shard_map/ppermute | solution.py:295
  14.9 1.2 %collective-permute-start.3 = (bf16[128,384]{1,0:T(8,128)(2,1)S(1)}, bf16[128,384]{1,0:T(8,128)(2,1)S(1)}, u32[]{:S(2)}, u32[]{:S(2)}) collective-permute-start(bf16[128,384]{1,0:T(8,128)(2,1)S(1)} %get-tuple-element.26), channel_id=1, source_target_pairs={{0,2},{1,3},{2,0},{3,1},{4,6},{5,7},{6,4},{7,5},{8,10},{9,11},{10,... | collective-permute-start | bytes 294920 | tf_op jit(solution)/shard_map/ppermute | solution.py:295
  16.2 1.8 %collective-permute-start.4 = (bf16[128,384]{1,0:T(8,128)(2,1)S(1)}, bf16[128,384]{1,0:T(8,128)(2,1)S(1)}, u32[]{:S(2)}, u32[]{:S(2)}) collective-permute-start(bf16[128,384]{1,0:T(8,128)(2,1)S(1)} %pass_sum.1), channel_id=1, source_target_pairs={{0,2},{1,3},{2,0},{3,1},{4,6},{5,7},{6,4},{7,5},{8,10},{9,11},{10,... | collective-permute-start | bytes 294920 | tf_op jit(solution)/shard_map/ppermute | solution.py:295
  17.9 6.9 %collective-permute-done.3.refs_2_ = bf16[128,384]{1,0:T(8,128)(2,1)S(1)} collective-permute-done((bf16[128,384]{1,0:T(8,128)(2,1)S(1)}, bf16[128,384]{1,0:T(8,128)(2,1)S(1)}, u32[]{:S(2)}, u32[]{:S(2)}) %collective-permute-start.3) | collective-permute-done | bytes 98336 | tf_op jit(solution)/shard_map/ppermute | solution.py:295
  24.8 1.1 %collective-permute-done.4.refs_3_ = bf16[128,384]{1,0:T(8,128)(2,1)S(1)} collective-permute-done((bf16[128,384]{1,0:T(8,128)(2,1)S(1)}, bf16[128,384]{1,0:T(8,128)(2,1)S(1)}, u32[]{:S(2)}, u32[]{:S(2)}) %collective-permute-start.4) | collective-permute-done | bytes 98336 | tf_op jit(solution)/shard_map/ppermute | solution.py:295
  26.0 1.6 %collective-permute-start.10 = (bf16[256,384]{1,0:T(8,128)(2,1)S(1)}, bf16[256,384]{1,0:T(8,128)(2,1)S(1)}, u32[]{:S(2)}, u32[]{:S(2)}) collective-permute-start(bf16[256,384]{1,0:T(8,128)(2,1)S(1)} %share_sum.1.refs_0_), channel_id=1, source_target_pairs={{0,8},{4,12},{8,0},{12,4},{1,9},{5,13},{9,1},{13,5},{2,10},{6,14},... | collective-permute-start | bytes 589832 | tf_op jit(solution)/shard_map/ppermute | solution.py:295
  27.9 2.0 %collective-permute-start.5 = (bf16[256,384]{1,0:T(8,128)(2,1)S(1)}, bf16[256,384]{1,0:T(8,128)(2,1)S(1)}, u32[]{:S(2)}, u32[]{:S(2)}) collective-permute-start(bf16[256,384]{1,0:T(8,128)(2,1)S(1)} %share_sum.1.refs_0_), channel_id=1, source_target_pairs={{0,1},{1,0},{2,3},{3,2},{4,5},{5,4},{6,7},{7,6},{8,9},{9,8},{10,11... | collective-permute-start | bytes 589832 | tf_op jit(solution)/shard_map/ppermute | solution.py:295
  30.0 1.7 %collective-permute-done.10.refs_1_ = bf16[256,384]{1,0:T(8,128)(2,1)S(1)} collective-permute-done((bf16[256,384]{1,0:T(8,128)(2,1)S(1)}, bf16[256,384]{1,0:T(8,128)(2,1)S(1)}, u32[]{:S(2)}, u32[]{:S(2)}) %collective-permute-start.10) | collective-permute-done | bytes 196640 | tf_op jit(solution)/shard_map/ppermute | solution.py:295
  31.7 4.0 %collective-permute-done.6.refs_2_ = bf16[256,384]{1,0:T(8,128)(2,1)S(1)} collective-permute-done((bf16[256,384]{1,0:T(8,128)(2,1)S(1)}, bf16[256,384]{1,0:T(8,128)(2,1)S(1)}, u32[]{:S(2)}, u32[]{:S(2)}) %collective-permute-start.6) | collective-permute-done | bytes 196640 | tf_op jit(solution)/shard_map/ppermute | solution.py:295
  35.8 1.2 %collective-permute-start.8 = (bf16[256,384]{1,0:T(8,128)(2,1)S(1)}, bf16[256,384]{1,0:T(8,128)(2,1)S(1)}, u32[]{:S(2)}, u32[]{:S(2)}) collective-permute-start(bf16[256,384]{1,0:T(8,128)(2,1)S(1)} %collective-permute-done.6.refs_2_), channel_id=1, source_target_pairs={{0,1},{1,0},{2,3},{3,2},{4,5},{5,4},{6,7},{7,6},{8,9},{9,8},{10,11... | collective-permute-start | bytes 589832 | tf_op jit(solution)/shard_map/ppermute | solution.py:295
  37.1 0.5 collective-permute-start.7
  37.7 1.5 %collective-permute-start.13 = (bf16[256,384]{1,0:T(8,128)(2,1)S(1)}, bf16[256,384]{1,0:T(8,128)(2,1)S(1)}, u32[]{:S(2)}, u32[]{:S(2)}) collective-permute-start(bf16[256,384]{1,0:T(8,128)(2,1)S(1)} %collective-permute-done.10.refs_1_), channel_id=1, source_target_pairs={{0,3},{1,2},{2,1},{3,0},{4,7},{5,6},{6,5},{7,4},{8,11},{9,10},{10,... | collective-permute-start | bytes 589832 | tf_op jit(solution)/shard_map/ppermute | solution.py:295
  39.2 1.5 %collective-permute-start.14 = (bf16[256,384]{1,0:T(8,128)(2,1)S(1)}, bf16[256,384]{1,0:T(8,128)(2,1)S(1)}, u32[]{:S(2)}, u32[]{:S(2)}) collective-permute-start(bf16[256,384]{1,0:T(8,128)(2,1)S(1)} %collective-permute-done.6.refs_2_), channel_id=1, source_target_pairs={{0,8},{4,12},{8,0},{12,4},{1,9},{5,13},{9,1},{13,5},{2,10},{6,14},... | collective-permute-start | bytes 589832 | tf_op jit(solution)/shard_map/ppermute | solution.py:295
  40.7 1.6 %early_rows.3.refs_2_ = f32[6,256,384]{2,1,0:T(8,128)S(1)} custom-call(s32[3,2]{1,0:T(4,128)S(1)} %copy.10.pairs_ref, s32[16,1,256]{2,1,0:T(1,128)S(1)} %bitcast.4, bf16[256,384]{1,0:T(8,128)(2,1)S(1)} %join.6.refs_0_, bf16[256,384]{1,0:T(8,128)(2,1)S(1)} %collective-permute-done.11.refs_1_), custom_call_target="tpu_custom_call" | custom-call | flops 1207959552 | bytes 4718592 | tf_op jit(solution)/shard_map/early_rows/pallas_call | solution.py:227
  42.3 0.9 %collective-permute-done.8.refs_1_ = bf16[256,384]{1,0:T(8,128)(2,1)S(1)} collective-permute-done((bf16[256,384]{1,0:T(8,128)(2,1)S(1)}, bf16[256,384]{1,0:T(8,128)(2,1)S(1)}, u32[]{:S(2)}, u32[]{:S(2)}) %collective-permute-start.8) | collective-permute-done | bytes 196640 | tf_op jit(solution)/shard_map/ppermute | solution.py:295
  43.2 1.7 %collective-permute-done.7.refs_0_ = bf16[256,384]{1,0:T(8,128)(2,1)S(1)} collective-permute-done((bf16[256,384]{1,0:T(8,128)(2,1)S(1)}, bf16[256,384]{1,0:T(8,128)(2,1)S(1)}, u32[]{:S(2)}, u32[]{:S(2)}) %collective-permute-start.7) | collective-permute-done | bytes 196640 | tf_op jit(solution)/shard_map/ppermute | solution.py:295
  45.0 3.2 %early_rows.4.refs_2_ = f32[6,256,384]{2,1,0:T(8,128)S(1)} custom-call(s32[3,2]{1,0:T(4,128)S(1)} %copy.10.pairs_ref, s32[16,1,256]{2,1,0:T(1,128)S(1)} %bitcast.5, bf16[768,384]{1,0:T(8,128)(2,1)S(1)} %join.5.refs_0_, bf16[768,384]{1,0:T(8,128)(2,1)S(1)} %collective-permute-done.12.refs_1_, f32[6,256,384]{2,1,0:T(8,128)S(1)} %early_rows.3.refs_2_), custom_call_target="tpu_custom_call" | custom-call | flops 3623878656 | bytes 4718592 | tf_op jit(solution)/shard_map/early_rows/pallas_call | solution.py:227
  48.9 2.4 %early_rows.5.early_ref = f32[6,256,384]{2,1,0:T(8,128)S(1)} custom-call(s32[3,2]{1,0:T(4,128)S(1)} %copy.10.pairs_ref, s32[16,1,256]{2,1,0:T(1,128)S(1)} %bitcast.6, bf16[512,384]{1,0:T(8,128)(2,1)S(1)} %join.4.refs_0_, bf16[512,384]{1,0:T(8,128)(2,1)S(1)} %collective-permute-done.9.refs_1_, f32[6,256,384]{2,1,0:T(8,128)S(1)} %early_rows.4.refs_2_), custom_call_target="tpu_custom_call" | custom-call | flops 2415919104 | bytes 4718592 | tf_op jit(solution)/shard_map/early_rows/pallas_call | solution.py:227
  51.3 6.5 %cross.1 = bf16[3,2,768,768]{3,2,1,0:T(8,128)(2,1)} custom-call(s32[3,2]{1,0:T(4,128)S(1)} %copy.10.pairs_ref, s32[16,1,256]{2,1,0:T(1,128)S(1)} %bitcast.7, f32[1,128]{1,0:T(1,128)S(1)} %maximum_bitcast_fusion.weights_ref, f32[6,256,384]{2,1,0:T(8,128)S(1)} %early_rows.5.early_ref, bf16[512,384]{1,0:T(8,128)(2,1)S(1)} %join.7.refs_0_, ...), custom_call_target="tpu_custom_call" | custom-call | tf_op jit(solution)/shard_map/cross/pallas_call | solution.py:270
  (30 shorter events, 1.5 us)
Async XLA Ops:
  3.9 10.3 %collective-permute-start = (bf16[128,384]{1,0:T(8,128)(2,1)}, bf16[128,384]{1,0:T(8,128)(2,1)S(1)}, u32[]{:S(2)}, u32[]{:S(2)}) collective-permute-start(bf16[128,384]{1,0:T(8,128)(2,1)} %get-tuple-element.23), channel_id=1, source_target_pairs={{0,1},{1,0},{2,3},{3,2},{4,5},{5,4},{6,7},{7,6},{8,9},{9,8},{10,11... | collective-permute-start | bytes 294920 | tf_op jit(solution)/shard_map/ppermute | solution.py:295
  6.9 9.2 %collective-permute-start.2 = (bf16[128,384]{1,0:T(8,128)(2,1)}, bf16[128,384]{1,0:T(8,128)(2,1)S(1)}, u32[]{:S(2)}, u32[]{:S(2)}) collective-permute-start(bf16[128,384]{1,0:T(8,128)(2,1)} %get-tuple-element.25), channel_id=1, source_target_pairs={{0,3},{1,2},{2,1},{3,0},{4,7},{5,6},{6,5},{7,4},{8,11},{9,10},{10,... | collective-permute-start | bytes 294920 | tf_op jit(solution)/shard_map/ppermute | solution.py:295
  9.4 0.9 %copy-start = (bf16[1024,128]{1,0:T(8,128)(2,1)S(1)}, bf16[1024,128]{1,0:T(8,128)(2,1)}, u32[]{:S(2)}) copy-start(bf16[1024,128]{1,0:T(8,128)(2,1)} %get-tuple-element.20.my_loads_ref) | copy-start | bytes 786436
  14.1 23.5 %copy-start.2 = (s32[3,2]{0,1:T(2,128)S(1)}, s32[3,2]{0,1:T(2,128)}, u32[]{:S(2)}) copy-start(s32[3,2]{0,1:T(2,128)} %param.11) | copy-start | bytes 76
  14.1 26.6 %copy-start.1 = (s32[4096]{0:T(1024)S(1)}, s32[4096]{0:T(1024)}, u32[]{:S(2)}) copy-start(s32[4096]{0:T(1024)} %param.10) | copy-start | bytes 49156
  14.2 11.7 %collective-permute-start.1 = (bf16[256,384]{1,0:T(8,128)(2,1)S(1)}, bf16[256,384]{1,0:T(8,128)(2,1)S(1)}, u32[]{:S(2)}, u32[]{:S(2)}) collective-permute-start(bf16[256,384]{1,0:T(8,128)(2,1)S(1)} %get-tuple-element.24), channel_id=1, source_target_pairs={{0,1},{1,0},{2,3},{3,2},{4,5},{5,4},{6,7},{7,6},{8,9},{9,8},{10,11... | collective-permute-start | bytes 589832 | tf_op jit(solution)/shard_map/ppermute | solution.py:295
  14.9 9.9 %collective-permute-start.3 = (bf16[128,384]{1,0:T(8,128)(2,1)S(1)}, bf16[128,384]{1,0:T(8,128)(2,1)S(1)}, u32[]{:S(2)}, u32[]{:S(2)}) collective-permute-start(bf16[128,384]{1,0:T(8,128)(2,1)S(1)} %get-tuple-element.26), channel_id=1, source_target_pairs={{0,2},{1,3},{2,0},{3,1},{4,6},{5,7},{6,4},{7,5},{8,10},{9,11},{10,... | collective-permute-start | bytes 294920 | tf_op jit(solution)/shard_map/ppermute | solution.py:295
  16.2 9.7 %collective-permute-start.4 = (bf16[128,384]{1,0:T(8,128)(2,1)S(1)}, bf16[128,384]{1,0:T(8,128)(2,1)S(1)}, u32[]{:S(2)}, u32[]{:S(2)}) collective-permute-start(bf16[128,384]{1,0:T(8,128)(2,1)S(1)} %pass_sum.1), channel_id=1, source_target_pairs={{0,2},{1,3},{2,0},{3,1},{4,6},{5,7},{6,4},{7,5},{8,10},{9,11},{10,... | collective-permute-start | bytes 294920 | tf_op jit(solution)/shard_map/ppermute | solution.py:295
  26.0 5.7 %collective-permute-start.10 = (bf16[256,384]{1,0:T(8,128)(2,1)S(1)}, bf16[256,384]{1,0:T(8,128)(2,1)S(1)}, u32[]{:S(2)}, u32[]{:S(2)}) collective-permute-start(bf16[256,384]{1,0:T(8,128)(2,1)S(1)} %share_sum.1.refs_0_), channel_id=1, source_target_pairs={{0,8},{4,12},{8,0},{12,4},{1,9},{5,13},{9,1},{13,5},{2,10},{6,14},... | collective-permute-start | bytes 589832 | tf_op jit(solution)/shard_map/ppermute | solution.py:295
  27.6 8.1 %collective-permute-start.6 = (bf16[256,384]{1,0:T(8,128)(2,1)S(1)}, bf16[256,384]{1,0:T(8,128)(2,1)S(1)}, u32[]{:S(2)}, u32[]{:S(2)}) collective-permute-start(bf16[256,384]{1,0:T(8,128)(2,1)S(1)} %share_sum.1.refs_0_), channel_id=1, source_target_pairs={{0,2},{1,3},{2,0},{3,1},{4,6},{5,7},{6,4},{7,5},{8,10},{9,11},{10,... | collective-permute-start | bytes 589832 | tf_op jit(solution)/shard_map/ppermute | solution.py:295
  27.9 7.8 %collective-permute-start.5 = (bf16[256,384]{1,0:T(8,128)(2,1)S(1)}, bf16[256,384]{1,0:T(8,128)(2,1)S(1)}, u32[]{:S(2)}, u32[]{:S(2)}) collective-permute-start(bf16[256,384]{1,0:T(8,128)(2,1)S(1)} %share_sum.1.refs_0_), channel_id=1, source_target_pairs={{0,1},{1,0},{2,3},{3,2},{4,5},{5,4},{6,7},{7,6},{8,9},{9,8},{10,11... | collective-permute-start | bytes 589832 | tf_op jit(solution)/shard_map/ppermute | solution.py:295
  29.9 5.9 %collective-permute-start.11 = (bf16[256,384]{1,0:T(8,128)(2,1)S(1)}, bf16[256,384]{1,0:T(8,128)(2,1)S(1)}, u32[]{:S(2)}, u32[]{:S(2)}) collective-permute-start(bf16[256,384]{1,0:T(8,128)(2,1)S(1)} %join.6.refs_0_), channel_id=1, source_target_pairs={{0,4},{4,0},{8,12},{12,8},{1,5},{5,1},{9,13},{13,9},{2,6},{6,2},{1... | collective-permute-start | bytes 589832 | tf_op jit(solution)/shard_map/ppermute | solution.py:295
  35.8 9.2 %collective-permute-start.12 = (bf16[768,384]{1,0:T(8,128)(2,1)S(1)}, bf16[768,384]{1,0:T(8,128)(2,1)S(1)}, u32[]{:S(2)}, u32[]{:S(2)}) collective-permute-start(bf16[768,384]{1,0:T(8,128)(2,1)S(1)} %join.5.refs_0_), channel_id=1, source_target_pairs={{0,4},{4,0},{8,12},{12,8},{1,5},{5,1},{9,13},{13,9},{2,6},{6,2},{1... | collective-permute-start | bytes 1769480 | tf_op jit(solution)/shard_map/ppermute | solution.py:295
  35.8 7.3 %collective-permute-start.8 = (bf16[256,384]{1,0:T(8,128)(2,1)S(1)}, bf16[256,384]{1,0:T(8,128)(2,1)S(1)}, u32[]{:S(2)}, u32[]{:S(2)}) collective-permute-start(bf16[256,384]{1,0:T(8,128)(2,1)S(1)} %collective-permute-done.6.refs_2_), channel_id=1, source_target_pairs={{0,1},{1,0},{2,3},{3,2},{4,5},{5,4},{6,7},{7,6},{8,9},{9,8},{10,11... | collective-permute-start | bytes 589832 | tf_op jit(solution)/shard_map/ppermute | solution.py:295
  37.1 7.7 %collective-permute-start.7 = (bf16[256,384]{1,0:T(8,128)(2,1)S(1)}, bf16[256,384]{1,0:T(8,128)(2,1)S(1)}, u32[]{:S(2)}, u32[]{:S(2)}) collective-permute-start(bf16[256,384]{1,0:T(8,128)(2,1)S(1)} %collective-permute-done.5.refs_0_), channel_id=1, source_target_pairs={{0,8},{4,12},{8,0},{12,4},{1,9},{5,13},{9,1},{13,5},{2,10},{6,14},... | collective-permute-start | bytes 589832 | tf_op jit(solution)/shard_map/ppermute | solution.py:295
  37.7 10.6 %collective-permute-start.13 = (bf16[256,384]{1,0:T(8,128)(2,1)S(1)}, bf16[256,384]{1,0:T(8,128)(2,1)S(1)}, u32[]{:S(2)}, u32[]{:S(2)}) collective-permute-start(bf16[256,384]{1,0:T(8,128)(2,1)S(1)} %collective-permute-done.10.refs_1_), channel_id=1, source_target_pairs={{0,3},{1,2},{2,1},{3,0},{4,7},{5,6},{6,5},{7,4},{8,11},{9,10},{10,... | collective-permute-start | bytes 589832 | tf_op jit(solution)/shard_map/ppermute | solution.py:295
  39.2 9.0 %collective-permute-start.14 = (bf16[256,384]{1,0:T(8,128)(2,1)S(1)}, bf16[256,384]{1,0:T(8,128)(2,1)S(1)}, u32[]{:S(2)}, u32[]{:S(2)}) collective-permute-start(bf16[256,384]{1,0:T(8,128)(2,1)S(1)} %collective-permute-done.6.refs_2_), channel_id=1, source_target_pairs={{0,8},{4,12},{8,0},{12,4},{1,9},{5,13},{9,1},{13,5},{2,10},{6,14},... | collective-permute-start | bytes 589832 | tf_op jit(solution)/shard_map/ppermute | solution.py:295
  44.9 3.9 %copy-start.3 = (f32[64]{0:T(128)S(1)}, f32[64]{0:T(128)}, u32[]{:S(2)}) copy-start(f32[64]{0:T(128)} %param.9) | copy-start | bytes 772
  44.9 4.0 %collective-permute-start.9 = (bf16[512,384]{1,0:T(8,128)(2,1)S(1)}, bf16[512,384]{1,0:T(8,128)(2,1)S(1)}, u32[]{:S(2)}, u32[]{:S(2)}) collective-permute-start(bf16[512,384]{1,0:T(8,128)(2,1)S(1)} %join.4.refs_0_), channel_id=1, source_target_pairs={{0,4},{4,0},{8,12},{12,8},{1,5},{5,1},{9,13},{13,9},{2,6},{6,2},{1... | collective-permute-start | bytes 1179656 | tf_op jit(solution)/shard_map/ppermute | solution.py:295
  48.3 3.0 %collective-permute-start.15 = (bf16[512,384]{1,0:T(8,128)(2,1)S(1)}, bf16[512,384]{1,0:T(8,128)(2,1)S(1)}, u32[]{:S(2)}, u32[]{:S(2)}) collective-permute-start(bf16[512,384]{1,0:T(8,128)(2,1)S(1)} %join.7.refs_0_), channel_id=1, source_target_pairs={{0,4},{4,0},{8,12},{12,8},{1,5},{5,1},{9,13},{13,9},{2,6},{6,2},{1... | collective-permute-start | bytes 1179656 | tf_op jit(solution)/shard_map/ppermute | solution.py:295

commit v6 on v5

--- a/solution.py
+++ b/solution.py
@@ -237,48 +237,54 @@
 
 
 def cross_kernel(components, groups, pairs_ref, position_ref, weights_ref, early_ref, *refs):
-    pieces, (out_ref, left_ref, right_ref, joined_ref) = refs[:-4], refs[-4:]
-    q = pl.program_id(0)
+    pieces, (out_ref, left_ref, right_ref, joined_ref, done_ref, sems) = refs[:-6], refs[-6:]
     columns = weights_ref.shape[1]
     rows = pieces[0].shape[0]
-
-    @pl.when(q == 0)
-    def _():
-        for i, piece in enumerate(pieces):
-            joined_ref[i * rows : (i + 1) * rows, :] = piece[...]
-
-    for side, rows_ref in ((0, left_ref), (1, right_ref)):
-        pick = pick_group(position_ref, groups, pairs_ref[q, side])
-        total = jnp.dot(pick, joined_ref[...], preferred_element_type=F32) + early_ref[2 * q + side]
-        for c in range(components):
-            rows_ref[pl.ds(c, BLK, stride=components), :] = total[:, c * columns : (c + 1) * columns]
-    scaled = (left_ref[...] * weights_ref[...]).astype(BF16)
-    right = right_ref[...]
-    lane = lax.broadcasted_iota(jnp.int32, right.shape, 1)
-    turned = pltpu.roll(right, columns // 2, 1)
-    turned = jnp.where(lane < columns // 2, -turned, turned)
-    for part, other in ((0, right), (1, turned)):
-        out_ref[0, part] = lax.dot_general(
-            scaled, other.astype(BF16), (((1,), (1,)), ((), ())), preferred_element_type=F32
-        ).astype(BF16)
+    for i, piece in enumerate(pieces):
+        joined_ref[i * rows : (i + 1) * rows, :] = piece[...]
+    copies = []
+    for q in range(out_ref.shape[0]):
+        for side, rows_ref in ((0, left_ref), (1, right_ref)):
+            pick = pick_group(position_ref, groups, pairs_ref[q, side])
+            total = jnp.dot(pick, joined_ref[...], preferred_element_type=F32) + early_ref[2 * q + side]
+            for c in range(components):
+                rows_ref[q, pl.ds(c, BLK, stride=components), :] = total[:, c * columns : (c + 1) * columns]
+        scaled = (left_ref[q] * weights_ref[...]).astype(BF16)
+        right = right_ref[q]
+        lane = lax.broadcasted_iota(jnp.int32, right.shape, 1)
+        turned = pltpu.roll(right, columns // 2, 1)
+        turned = jnp.where(lane < columns // 2, -turned, turned)
+        for part, other in ((0, right), (1, turned)):
+            other = other.astype(BF16)
+            for top in range(0, scaled.shape[0], BLK):
+                done_ref[q, part, top : top + BLK, :] = lax.dot_general(
+                    scaled[top : top + BLK], other, (((1,), (1,)), ((), ())), preferred_element_type=F32
+                ).astype(BF16)
+            copy = pltpu.make_async_copy(done_ref.at[q, part], out_ref.at[q, part], sems.at[q, part])
+            copy.start()
+            copies.append(copy)
+    for copy in copies:
+        copy.wait()
 
 
 def cross(pairs, position, weights, early, groups, pieces, components):
     count = pairs.shape[0]
     columns = weights.shape[1]
     rows = BLK * components
+    out = jax.ShapeDtypeStruct((count, 2, rows, rows), BF16)
     return pl.pallas_call(
         functools.partial(cross_kernel, components, groups),
-        out_shape=jax.ShapeDtypeStruct((count, 2, rows, rows), BF16),
-        grid=(count,),
+        out_shape=out,
         in_specs=[pl.BlockSpec(memory_space=pltpu.SMEM)] + [vmem()] * (3 + len(pieces)),
-        out_specs=pl.BlockSpec((1, 2, rows, rows), lambda i: (i, 0, 0, 0)),
+        out_specs=hbm(),
         scratch_shapes=[
-            pltpu.VMEM((rows, columns), F32),
-            pltpu.VMEM((rows, columns), F32),
+            pltpu.VMEM((count, rows, columns), F32),
+            pltpu.VMEM((count, rows, columns), F32),
             pltpu.VMEM((len(pieces) * pieces[0].shape[0], components * columns), BF16),
+            pltpu.VMEM(out.shape, BF16),
+            pltpu.SemaphoreType.DMA((count, 2)),
         ],
-        compiler_params=params(),
+        compiler_params=pltpu.CompilerParams(vmem_limit_bytes=VMEM_BYTES),
         name="cross",
     )(pairs, position, weights, early, *pieces)
 

time: 58 us -> 57.3 us (0.988)
  Pallas kernels: 21.5 us -> 20.8 us
    pallas_call x1, Pallas kernels: 6.48 us -> 5.8 us  [cross(): pl.pallas_call(functools.partial(cross_kernel, components, groups), out_s...]
where the time goes in v6:
time: 57.3 us; the launch traced here: 57.1 us
  Pallas kernels  20.8 us (36%)
  starting transfers between devices  18.7 us (33%)
  waiting for transfers between devices  16.3 us (28%)
  local copies, waits for them, and re-layouts  1.06 us (2%)
    ppermute x16, starting transfers between devices, swap(): return lax.ppermute(array, axis, [(i, i ^ k) for i in range(size)])  18.7 us
    ppermute x16, waiting for transfers between devices, swap(): return lax.ppermute(array, axis, [(i, i ^ k) for i in range(size)])  16.3 us
    pallas_call x3, Pallas kernels, early_rows(): pl.pallas_call(functools.partial(early_kernel, groups), out_shape=jax.Sha...  7.19 us
    pallas_call x1, Pallas kernels, cross(): pl.pallas_call(functools.partial(cross_kernel, components, groups), out_s...  5.8 us
    pallas_call x1, Pallas kernels, first_products(): pl.pallas_call(functools.partial(first_kernel, which, cuts), out_shape=cu...  3.84 us
    pallas_call x1, Pallas kernels, more_products(): pl.pallas_call(functools.partial(more_kernel, which, cuts), out_shape=cut...  3.76 us
  transfers between devices with their start and end apart: 16, of which 7 were waited for; matrix products, arithmetic and copies ran while one was open for 0% of the time, Pallas kernels for 19%

profile of v6, /device:TPU:0, one launch (start us, length us, event | category | flops | bytes accessed | tf_op | source)
XLA Modules:
  0.0 57.1 jit_solution(11345848291489943305)
XLA Ops:
  0.0 3.8 %first_products.1 = (bf16[128,384]{1,0:T(8,128)(2,1)}, bf16[128,384]{1,0:T(8,128)(2,1)}, bf16[1024,128]{1,0:T(8,128)(2,1)}) custom-call(s32[4,8,128]{2,1,0:T(8,128)} %bitcast.8, bf16[4096,128]{1,0:T(8,128)(2,1)} %loads_ref.1, bf16[3,1024,1024]{2,1,0:T(8,128)(2,1)} %influence_ref.3), custom_call_target="tpu_custom_call" | custom-call | tf_op jit(solution)/shard_map/first_products/pallas_call | solution.py:114
  3.9 3.1 %collective-permute-start = (bf16[128,384]{1,0:T(8,128)(2,1)}, bf16[128,384]{1,0:T(8,128)(2,1)S(1)}, u32[]{:S(2)}, u32[]{:S(2)}) collective-permute-start(bf16[128,384]{1,0:T(8,128)(2,1)} %get-tuple-element.23), channel_id=1, source_target_pairs={{0,1},{1,0},{2,3},{3,2},{4,5},{5,4},{6,7},{7,6},{8,9},{9,8},{10,11... | collective-permute-start | bytes 294920 | tf_op jit(solution)/shard_map/ppermute | solution.py:301
  6.9 2.5 %collective-permute-start.2 = (bf16[128,384]{1,0:T(8,128)(2,1)}, bf16[128,384]{1,0:T(8,128)(2,1)S(1)}, u32[]{:S(2)}, u32[]{:S(2)}) collective-permute-start(bf16[128,384]{1,0:T(8,128)(2,1)} %get-tuple-element.25), channel_id=1, source_target_pairs={{0,3},{1,2},{2,1},{3,0},{4,7},{5,6},{6,5},{7,4},{8,11},{9,10},{10,... | collective-permute-start | bytes 294920 | tf_op jit(solution)/shard_map/ppermute | solution.py:301
  9.4 0.9 %copy-done = bf16[1024,128]{1,0:T(8,128)(2,1)S(1)} copy-done((bf16[1024,128]{1,0:T(8,128)(2,1)S(1)}, bf16[1024,128]{1,0:T(8,128)(2,1)}, u32[]{:S(2)}) %copy-start) | copy-done | bytes 262168
  10.4 3.8 %more_products.1 = (bf16[128,384]{1,0:T(8,128)(2,1)S(1)}, f32[128,384]{1,0:T(8,128)S(1)}, bf16[256,384]{1,0:T(8,128)(2,1)S(1)}, f32[256,384]{1,0:T(8,128)S(1)}) custom-call(bf16[1024,128]{1,0:T(8,128)(2,1)S(1)} %copy-done, bf16[3,1024,1024]{2,1,0:T(8,128)(2,1)} %influence_ref.3), custom_call_target="tpu_custom_call" | custom-call | flops 603979776 | bytes 4718592 | tf_op jit(solution)/shard_map/more_products/pallas_call | solution.py:138
  14.2 0.7 %collective-permute-start.1 = (bf16[256,384]{1,0:T(8,128)(2,1)S(1)}, bf16[256,384]{1,0:T(8,128)(2,1)S(1)}, u32[]{:S(2)}, u32[]{:S(2)}) collective-permute-start(bf16[256,384]{1,0:T(8,128)(2,1)S(1)} %get-tuple-element.24), channel_id=1, source_target_pairs={{0,1},{1,0},{2,3},{3,2},{4,5},{5,4},{6,7},{7,6},{8,9},{9,8},{10,11... | collective-permute-start | bytes 589832 | tf_op jit(solution)/shard_map/ppermute | solution.py:301
  14.9 1.2 %collective-permute-start.3 = (bf16[128,384]{1,0:T(8,128)(2,1)S(1)}, bf16[128,384]{1,0:T(8,128)(2,1)S(1)}, u32[]{:S(2)}, u32[]{:S(2)}) collective-permute-start(bf16[128,384]{1,0:T(8,128)(2,1)S(1)} %get-tuple-element.26), channel_id=1, source_target_pairs={{0,2},{1,3},{2,0},{3,1},{4,6},{5,7},{6,4},{7,5},{8,10},{9,11},{10,... | collective-permute-start | bytes 294920 | tf_op jit(solution)/shard_map/ppermute | solution.py:301
  16.2 1.8 %collective-permute-start.4 = (bf16[128,384]{1,0:T(8,128)(2,1)S(1)}, bf16[128,384]{1,0:T(8,128)(2,1)S(1)}, u32[]{:S(2)}, u32[]{:S(2)}) collective-permute-start(bf16[128,384]{1,0:T(8,128)(2,1)S(1)} %pass_sum.1), channel_id=1, source_target_pairs={{0,2},{1,3},{2,0},{3,1},{4,6},{5,7},{6,4},{7,5},{8,10},{9,11},{10,... | collective-permute-start | bytes 294920 | tf_op jit(solution)/shard_map/ppermute | solution.py:301
  17.9 6.9 %collective-permute-done.3.refs_2_ = bf16[128,384]{1,0:T(8,128)(2,1)S(1)} collective-permute-done((bf16[128,384]{1,0:T(8,128)(2,1)S(1)}, bf16[128,384]{1,0:T(8,128)(2,1)S(1)}, u32[]{:S(2)}, u32[]{:S(2)}) %collective-permute-start.3) | collective-permute-done | bytes 98336 | tf_op jit(solution)/shard_map/ppermute | solution.py:301
  24.8 1.1 %collective-permute-done.4.refs_3_ = bf16[128,384]{1,0:T(8,128)(2,1)S(1)} collective-permute-done((bf16[128,384]{1,0:T(8,128)(2,1)S(1)}, bf16[128,384]{1,0:T(8,128)(2,1)S(1)}, u32[]{:S(2)}, u32[]{:S(2)}) %collective-permute-start.4) | collective-permute-done | bytes 98336 | tf_op jit(solution)/shard_map/ppermute | solution.py:301
  26.0 1.6 %collective-permute-start.10 = (bf16[256,384]{1,0:T(8,128)(2,1)S(1)}, bf16[256,384]{1,0:T(8,128)(2,1)S(1)}, u32[]{:S(2)}, u32[]{:S(2)}) collective-permute-start(bf16[256,384]{1,0:T(8,128)(2,1)S(1)} %share_sum.1.refs_0_), channel_id=1, source_target_pairs={{0,8},{4,12},{8,0},{12,4},{1,9},{5,13},{9,1},{13,5},{2,10},{6,14},... | collective-permute-start | bytes 589832 | tf_op jit(solution)/shard_map/ppermute | solution.py:301
  27.9 2.0 %collective-permute-start.5 = (bf16[256,384]{1,0:T(8,128)(2,1)S(1)}, bf16[256,384]{1,0:T(8,128)(2,1)S(1)}, u32[]{:S(2)}, u32[]{:S(2)}) collective-permute-start(bf16[256,384]{1,0:T(8,128)(2,1)S(1)} %share_sum.1.refs_0_), channel_id=1, source_target_pairs={{0,1},{1,0},{2,3},{3,2},{4,5},{5,4},{6,7},{7,6},{8,9},{9,8},{10,11... | collective-permute-start | bytes 589832 | tf_op jit(solution)/shard_map/ppermute | solution.py:301
  30.0 1.7 %collective-permute-done.10.refs_1_ = bf16[256,384]{1,0:T(8,128)(2,1)S(1)} collective-permute-done((bf16[256,384]{1,0:T(8,128)(2,1)S(1)}, bf16[256,384]{1,0:T(8,128)(2,1)S(1)}, u32[]{:S(2)}, u32[]{:S(2)}) %collective-permute-start.10) | collective-permute-done | bytes 196640 | tf_op jit(solution)/shard_map/ppermute | solution.py:301
  31.7 4.0 %collective-permute-done.6.refs_2_ = bf16[256,384]{1,0:T(8,128)(2,1)S(1)} collective-permute-done((bf16[256,384]{1,0:T(8,128)(2,1)S(1)}, bf16[256,384]{1,0:T(8,128)(2,1)S(1)}, u32[]{:S(2)}, u32[]{:S(2)}) %collective-permute-start.6) | collective-permute-done | bytes 196640 | tf_op jit(solution)/shard_map/ppermute | solution.py:301
  35.8 1.2 %collective-permute-start.8 = (bf16[256,384]{1,0:T(8,128)(2,1)S(1)}, bf16[256,384]{1,0:T(8,128)(2,1)S(1)}, u32[]{:S(2)}, u32[]{:S(2)}) collective-permute-start(bf16[256,384]{1,0:T(8,128)(2,1)S(1)} %collective-permute-done.6.refs_2_), channel_id=1, source_target_pairs={{0,1},{1,0},{2,3},{3,2},{4,5},{5,4},{6,7},{7,6},{8,9},{9,8},{10,11... | collective-permute-start | bytes 589832 | tf_op jit(solution)/shard_map/ppermute | solution.py:301
  37.1 0.5 collective-permute-start.7
  37.7 1.5 %collective-permute-start.13 = (bf16[256,384]{1,0:T(8,128)(2,1)S(1)}, bf16[256,384]{1,0:T(8,128)(2,1)S(1)}, u32[]{:S(2)}, u32[]{:S(2)}) collective-permute-start(bf16[256,384]{1,0:T(8,128)(2,1)S(1)} %collective-permute-done.10.refs_1_), channel_id=1, source_target_pairs={{0,3},{1,2},{2,1},{3,0},{4,7},{5,6},{6,5},{7,4},{8,11},{9,10},{10,... | collective-permute-start | bytes 589832 | tf_op jit(solution)/shard_map/ppermute | solution.py:301
  39.2 1.5 %collective-permute-start.14 = (bf16[256,384]{1,0:T(8,128)(2,1)S(1)}, bf16[256,384]{1,0:T(8,128)(2,1)S(1)}, u32[]{:S(2)}, u32[]{:S(2)}) collective-permute-start(bf16[256,384]{1,0:T(8,128)(2,1)S(1)} %collective-permute-done.6.refs_2_), channel_id=1, source_target_pairs={{0,8},{4,12},{8,0},{12,4},{1,9},{5,13},{9,1},{13,5},{2,10},{6,14},... | collective-permute-start | bytes 589832 | tf_op jit(solution)/shard_map/ppermute | solution.py:301
  40.7 1.6 %early_rows.3.refs_2_ = f32[6,256,384]{2,1,0:T(8,128)S(1)} custom-call(s32[3,2]{1,0:T(4,128)S(1)} %copy.10.pairs_ref, s32[16,1,256]{2,1,0:T(1,128)S(1)} %bitcast.4, bf16[256,384]{1,0:T(8,128)(2,1)S(1)} %join.6.refs_0_, bf16[256,384]{1,0:T(8,128)(2,1)S(1)} %collective-permute-done.11.refs_1_), custom_call_target="tpu_custom_call" | custom-call | flops 1207959552 | bytes 4718592 | tf_op jit(solution)/shard_map/early_rows/pallas_call | solution.py:227
  42.3 0.9 %collective-permute-done.8.refs_1_ = bf16[256,384]{1,0:T(8,128)(2,1)S(1)} collective-permute-done((bf16[256,384]{1,0:T(8,128)(2,1)S(1)}, bf16[256,384]{1,0:T(8,128)(2,1)S(1)}, u32[]{:S(2)}, u32[]{:S(2)}) %collective-permute-start.8) | collective-permute-done | bytes 196640 | tf_op jit(solution)/shard_map/ppermute | solution.py:301
  43.2 1.7 %collective-permute-done.7.refs_0_ = bf16[256,384]{1,0:T(8,128)(2,1)S(1)} collective-permute-done((bf16[256,384]{1,0:T(8,128)(2,1)S(1)}, bf16[256,384]{1,0:T(8,128)(2,1)S(1)}, u32[]{:S(2)}, u32[]{:S(2)}) %collective-permute-start.7) | collective-permute-done | bytes 196640 | tf_op jit(solution)/shard_map/ppermute | solution.py:301
  45.0 3.2 %early_rows.4.refs_2_ = f32[6,256,384]{2,1,0:T(8,128)S(1)} custom-call(s32[3,2]{1,0:T(4,128)S(1)} %copy.10.pairs_ref, s32[16,1,256]{2,1,0:T(1,128)S(1)} %bitcast.5, bf16[768,384]{1,0:T(8,128)(2,1)S(1)} %join.5.refs_0_, bf16[768,384]{1,0:T(8,128)(2,1)S(1)} %collective-permute-done.12.refs_1_, f32[6,256,384]{2,1,0:T(8,128)S(1)} %early_rows.3.refs_2_), custom_call_target="tpu_custom_call" | custom-call | flops 3623878656 | bytes 4718592 | tf_op jit(solution)/shard_map/early_rows/pallas_call | solution.py:227
  48.9 2.4 %early_rows.5.early_ref = f32[6,256,384]{2,1,0:T(8,128)S(1)} custom-call(s32[3,2]{1,0:T(4,128)S(1)} %copy.10.pairs_ref, s32[16,1,256]{2,1,0:T(1,128)S(1)} %bitcast.6, bf16[512,384]{1,0:T(8,128)(2,1)S(1)} %join.4.refs_0_, bf16[512,384]{1,0:T(8,128)(2,1)S(1)} %collective-permute-done.9.refs_1_, f32[6,256,384]{2,1,0:T(8,128)S(1)} %early_rows.4.refs_2_), custom_call_target="tpu_custom_call" | custom-call | flops 2415919104 | bytes 4718592 | tf_op jit(solution)/shard_map/early_rows/pallas_call | solution.py:227
  51.3 5.8 %cross.1 = bf16[3,2,768,768]{3,2,1,0:T(8,128)(2,1)} custom-call(s32[3,2]{1,0:T(4,128)S(1)} %copy.10.pairs_ref, s32[16,1,256]{2,1,0:T(1,128)S(1)} %bitcast.7, f32[1,128]{1,0:T(1,128)S(1)} %maximum_bitcast_fusion.weights_ref, f32[6,256,384]{2,1,0:T(8,128)S(1)} %early_rows.5.early_ref, bf16[512,384]{1,0:T(8,128)(2,1)S(1)} %join.7.refs_0_, ...), custom_call_target="tpu_custom_call" | custom-call | tf_op jit(solution)/shard_map/cross/pallas_call | solution.py:275
  (30 shorter events, 1.5 us)
Async XLA Ops:
  3.9 10.3 %collective-permute-start = (bf16[128,384]{1,0:T(8,128)(2,1)}, bf16[128,384]{1,0:T(8,128)(2,1)S(1)}, u32[]{:S(2)}, u32[]{:S(2)}) collective-permute-start(bf16[128,384]{1,0:T(8,128)(2,1)} %get-tuple-element.23), channel_id=1, source_target_pairs={{0,1},{1,0},{2,3},{3,2},{4,5},{5,4},{6,7},{7,6},{8,9},{9,8},{10,11... | collective-permute-start | bytes 294920 | tf_op jit(solution)/shard_map/ppermute | solution.py:301
  6.9 9.2 %collective-permute-start.2 = (bf16[128,384]{1,0:T(8,128)(2,1)}, bf16[128,384]{1,0:T(8,128)(2,1)S(1)}, u32[]{:S(2)}, u32[]{:S(2)}) collective-permute-start(bf16[128,384]{1,0:T(8,128)(2,1)} %get-tuple-element.25), channel_id=1, source_target_pairs={{0,3},{1,2},{2,1},{3,0},{4,7},{5,6},{6,5},{7,4},{8,11},{9,10},{10,... | collective-permute-start | bytes 294920 | tf_op jit(solution)/shard_map/ppermute | solution.py:301
  9.4 0.9 %copy-start = (bf16[1024,128]{1,0:T(8,128)(2,1)S(1)}, bf16[1024,128]{1,0:T(8,128)(2,1)}, u32[]{:S(2)}) copy-start(bf16[1024,128]{1,0:T(8,128)(2,1)} %get-tuple-element.20.my_loads_ref) | copy-start | bytes 786436
  14.1 23.5 %copy-start.2 = (s32[3,2]{0,1:T(2,128)S(1)}, s32[3,2]{0,1:T(2,128)}, u32[]{:S(2)}) copy-start(s32[3,2]{0,1:T(2,128)} %param.11) | copy-start | bytes 76
  14.1 26.6 %copy-start.1 = (s32[4096]{0:T(1024)S(1)}, s32[4096]{0:T(1024)}, u32[]{:S(2)}) copy-start(s32[4096]{0:T(1024)} %param.10) | copy-start | bytes 49156
  14.2 11.7 %collective-permute-start.1 = (bf16[256,384]{1,0:T(8,128)(2,1)S(1)}, bf16[256,384]{1,0:T(8,128)(2,1)S(1)}, u32[]{:S(2)}, u32[]{:S(2)}) collective-permute-start(bf16[256,384]{1,0:T(8,128)(2,1)S(1)} %get-tuple-element.24), channel_id=1, source_target_pairs={{0,1},{1,0},{2,3},{3,2},{4,5},{5,4},{6,7},{7,6},{8,9},{9,8},{10,11... | collective-permute-start | bytes 589832 | tf_op jit(solution)/shard_map/ppermute | solution.py:301
  14.9 9.9 %collective-permute-start.3 = (bf16[128,384]{1,0:T(8,128)(2,1)S(1)}, bf16[128,384]{1,0:T(8,128)(2,1)S(1)}, u32[]{:S(2)}, u32[]{:S(2)}) collective-permute-start(bf16[128,384]{1,0:T(8,128)(2,1)S(1)} %get-tuple-element.26), channel_id=1, source_target_pairs={{0,2},{1,3},{2,0},{3,1},{4,6},{5,7},{6,4},{7,5},{8,10},{9,11},{10,... | collective-permute-start | bytes 294920 | tf_op jit(solution)/shard_map/ppermute | solution.py:301
  16.2 9.7 %collective-permute-start.4 = (bf16[128,384]{1,0:T(8,128)(2,1)S(1)}, bf16[128,384]{1,0:T(8,128)(2,1)S(1)}, u32[]{:S(2)}, u32[]{:S(2)}) collective-permute-start(bf16[128,384]{1,0:T(8,128)(2,1)S(1)} %pass_sum.1), channel_id=1, source_target_pairs={{0,2},{1,3},{2,0},{3,1},{4,6},{5,7},{6,4},{7,5},{8,10},{9,11},{10,... | collective-permute-start | bytes 294920 | tf_op jit(solution)/shard_map/ppermute | solution.py:301
  26.0 5.7 %collective-permute-start.10 = (bf16[256,384]{1,0:T(8,128)(2,1)S(1)}, bf16[256,384]{1,0:T(8,128)(2,1)S(1)}, u32[]{:S(2)}, u32[]{:S(2)}) collective-permute-start(bf16[256,384]{1,0:T(8,128)(2,1)S(1)} %share_sum.1.refs_0_), channel_id=1, source_target_pairs={{0,8},{4,12},{8,0},{12,4},{1,9},{5,13},{9,1},{13,5},{2,10},{6,14},... | collective-permute-start | bytes 589832 | tf_op jit(solution)/shard_map/ppermute | solution.py:301
  27.6 8.1 %collective-permute-start.6 = (bf16[256,384]{1,0:T(8,128)(2,1)S(1)}, bf16[256,384]{1,0:T(8,128)(2,1)S(1)}, u32[]{:S(2)}, u32[]{:S(2)}) collective-permute-start(bf16[256,384]{1,0:T(8,128)(2,1)S(1)} %share_sum.1.refs_0_), channel_id=1, source_target_pairs={{0,2},{1,3},{2,0},{3,1},{4,6},{5,7},{6,4},{7,5},{8,10},{9,11},{10,... | collective-permute-start | bytes 589832 | tf_op jit(solution)/shard_map/ppermute | solution.py:301
  27.9 7.8 %collective-permute-start.5 = (bf16[256,384]{1,0:T(8,128)(2,1)S(1)}, bf16[256,384]{1,0:T(8,128)(2,1)S(1)}, u32[]{:S(2)}, u32[]{:S(2)}) collective-permute-start(bf16[256,384]{1,0:T(8,128)(2,1)S(1)} %share_sum.1.refs_0_), channel_id=1, source_target_pairs={{0,1},{1,0},{2,3},{3,2},{4,5},{5,4},{6,7},{7,6},{8,9},{9,8},{10,11... | collective-permute-start | bytes 589832 | tf_op jit(solution)/shard_map/ppermute | solution.py:301
  29.9 5.9 %collective-permute-start.11 = (bf16[256,384]{1,0:T(8,128)(2,1)S(1)}, bf16[256,384]{1,0:T(8,128)(2,1)S(1)}, u32[]{:S(2)}, u32[]{:S(2)}) collective-permute-start(bf16[256,384]{1,0:T(8,128)(2,1)S(1)} %join.6.refs_0_), channel_id=1, source_target_pairs={{0,4},{4,0},{8,12},{12,8},{1,5},{5,1},{9,13},{13,9},{2,6},{6,2},{1... | collective-permute-start | bytes 589832 | tf_op jit(solution)/shard_map/ppermute | solution.py:301
  35.8 9.2 %collective-permute-start.12 = (bf16[768,384]{1,0:T(8,128)(2,1)S(1)}, bf16[768,384]{1,0:T(8,128)(2,1)S(1)}, u32[]{:S(2)}, u32[]{:S(2)}) collective-permute-start(bf16[768,384]{1,0:T(8,128)(2,1)S(1)} %join.5.refs_0_), channel_id=1, source_target_pairs={{0,4},{4,0},{8,12},{12,8},{1,5},{5,1},{9,13},{13,9},{2,6},{6,2},{1... | collective-permute-start | bytes 1769480 | tf_op jit(solution)/shard_map/ppermute | solution.py:301
  35.8 7.3 %collective-permute-start.8 = (bf16[256,384]{1,0:T(8,128)(2,1)S(1)}, bf16[256,384]{1,0:T(8,128)(2,1)S(1)}, u32[]{:S(2)}, u32[]{:S(2)}) collective-permute-start(bf16[256,384]{1,0:T(8,128)(2,1)S(1)} %collective-permute-done.6.refs_2_), channel_id=1, source_target_pairs={{0,1},{1,0},{2,3},{3,2},{4,5},{5,4},{6,7},{7,6},{8,9},{9,8},{10,11... | collective-permute-start | bytes 589832 | tf_op jit(solution)/shard_map/ppermute | solution.py:301
  37.1 7.7 %collective-permute-start.7 = (bf16[256,384]{1,0:T(8,128)(2,1)S(1)}, bf16[256,384]{1,0:T(8,128)(2,1)S(1)}, u32[]{:S(2)}, u32[]{:S(2)}) collective-permute-start(bf16[256,384]{1,0:T(8,128)(2,1)S(1)} %collective-permute-done.5.refs_0_), channel_id=1, source_target_pairs={{0,8},{4,12},{8,0},{12,4},{1,9},{5,13},{9,1},{13,5},{2,10},{6,14},... | collective-permute-start | bytes 589832 | tf_op jit(solution)/shard_map/ppermute | solution.py:301
  37.7 10.6 %collective-permute-start.13 = (bf16[256,384]{1,0:T(8,128)(2,1)S(1)}, bf16[256,384]{1,0:T(8,128)(2,1)S(1)}, u32[]{:S(2)}, u32[]{:S(2)}) collective-permute-start(bf16[256,384]{1,0:T(8,128)(2,1)S(1)} %collective-permute-done.10.refs_1_), channel_id=1, source_target_pairs={{0,3},{1,2},{2,1},{3,0},{4,7},{5,6},{6,5},{7,4},{8,11},{9,10},{10,... | collective-permute-start | bytes 589832 | tf_op jit(solution)/shard_map/ppermute | solution.py:301
  39.2 9.0 %collective-permute-start.14 = (bf16[256,384]{1,0:T(8,128)(2,1)S(1)}, bf16[256,384]{1,0:T(8,128)(2,1)S(1)}, u32[]{:S(2)}, u32[]{:S(2)}) collective-permute-start(bf16[256,384]{1,0:T(8,128)(2,1)S(1)} %collective-permute-done.6.refs_2_), channel_id=1, source_target_pairs={{0,8},{4,12},{8,0},{12,4},{1,9},{5,13},{9,1},{13,5},{2,10},{6,14},... | collective-permute-start | bytes 589832 | tf_op jit(solution)/shard_map/ppermute | solution.py:301
  44.9 3.9 %copy-start.3 = (f32[64]{0:T(128)S(1)}, f32[64]{0:T(128)}, u32[]{:S(2)}) copy-start(f32[64]{0:T(128)} %param.9) | copy-start | bytes 772
  44.9 4.0 %collective-permute-start.9 = (bf16[512,384]{1,0:T(8,128)(2,1)S(1)}, bf16[512,384]{1,0:T(8,128)(2,1)S(1)}, u32[]{:S(2)}, u32[]{:S(2)}) collective-permute-start(bf16[512,384]{1,0:T(8,128)(2,1)S(1)} %join.4.refs_0_), channel_id=1, source_target_pairs={{0,4},{4,0},{8,12},{12,8},{1,5},{5,1},{9,13},{13,9},{2,6},{6,2},{1... | collective-permute-start | bytes 1179656 | tf_op jit(solution)/shard_map/ppermute | solution.py:301
  48.3 3.0 %collective-permute-start.15 = (bf16[512,384]{1,0:T(8,128)(2,1)S(1)}, bf16[512,384]{1,0:T(8,128)(2,1)S(1)}, u32[]{:S(2)}, u32[]{:S(2)}) collective-permute-start(bf16[512,384]{1,0:T(8,128)(2,1)S(1)} %join.7.refs_0_), channel_id=1, source_target_pairs={{0,4},{4,0},{8,12},{12,8},{1,5},{5,1},{9,13},{13,9},{2,6},{6,2},{1... | collective-permute-start | bytes 1179656 | tf_op jit(solution)/shard_map/ppermute | solution.py:301

commit v7 on v6

--- a/solution.py
+++ b/solution.py
@@ -155,9 +155,11 @@
 
 
 def total_kernel(near, own_ref, *refs):
-    out_ref, half = refs[-1], refs[-2].shape[0]
-    for top, terms in ((0, refs[near:-2]), (half, refs[-2:-1])):
-        rows = slice(top, top + half)
+    out_ref = refs[-1]
+    rest = refs[-2].shape[0]
+    half = out_ref.shape[0] - rest
+    for top, held, terms in ((0, half, refs[near:-2]), (half, rest, refs[-2:-1])):
+        rows = slice(top, top + held)
         total = own_ref[rows, :]
         for ref in refs[:near]:
             total = total + ref[rows, :].astype(F32)
@@ -305,10 +307,10 @@
     tie = lambda value, *after: lax.optimization_barrier((value, *after))[0]
 
     top = n_patch // 2
-    half = share_rows // 2
+    half = share_rows // 4
 
     def halves(i, kind):
-        return [(i, 0, half, BF16), (i, half, half, kind)]
+        return [(i, 0, half, BF16), (i, half, share_rows - half, kind)]
 
     first_terms, my_loads = first_products(
         order, loads, influence, share_rows, far[:1], halves(0, BF16 if n_patch > 2 else F32)

time: 57.3 us -> 57.3 us (level)
  transfers between devices with their start and end apart: 16 -> 16, of which waited for: 7 -> 6; matrix products, arithmetic and copies ran while one was open for 0% -> 0% of each run, Pallas kernels for 19% -> 19%
where the time goes in v7:
time: 57.3 us; the launch traced here: 57.2 us
  Pallas kernels  20.9 us (36%)
  starting transfers between devices  18.2 us (32%)
  waiting for transfers between devices  16.8 us (29%)
  local copies, waits for them, and re-layouts  1.06 us (2%)
    ppermute x16, starting transfers between devices, swap(): return lax.ppermute(array, axis, [(i, i ^ k) for i in range(size)])  18.2 us
    ppermute x16, waiting for transfers between devices, swap(): return lax.ppermute(array, axis, [(i, i ^ k) for i in range(size)])  16.8 us
    pallas_call x3, Pallas kernels, early_rows(): pl.pallas_call(functools.partial(early_kernel, groups), out_shape=jax.Sha...  7.2 us
    pallas_call x1, Pallas kernels, cross(): pl.pallas_call(functools.partial(cross_kernel, components, groups), out_s...  5.8 us
    pallas_call x1, Pallas kernels, first_products(): pl.pallas_call(functools.partial(first_kernel, which, cuts), out_shape=cu...  3.87 us
    pallas_call x1, Pallas kernels, more_products(): pl.pallas_call(functools.partial(more_kernel, which, cuts), out_shape=cut...  3.77 us
  transfers between devices with their start and end apart: 16, of which 6 were waited for; matrix products, arithmetic and copies ran while one was open for 0% of the time, Pallas kernels for 19%

profile of v7, /device:TPU:0, one launch (start us, length us, event | category | flops | bytes accessed | tf_op | source)
XLA Modules:
  0.0 57.2 jit_solution(4521731162169908271)
XLA Ops:
  0.0 3.9 %first_products.1 = (bf16[64,384]{1,0:T(8,128)(2,1)}, bf16[192,384]{1,0:T(8,128)(2,1)}, bf16[1024,128]{1,0:T(8,128)(2,1)}) custom-call(s32[4,8,128]{2,1,0:T(8,128)} %bitcast.8, bf16[4096,128]{1,0:T(8,128)(2,1)} %loads_ref.1, bf16[3,1024,1024]{2,1,0:T(8,128)(2,1)} %influence_ref.3), custom_call_target="tpu_custom_call" | custom-call | tf_op jit(solution)/shard_map/first_products/pallas_call | solution.py:114
  3.9 3.1 %collective-permute-start = (bf16[192,384]{1,0:T(8,128)(2,1)}, bf16[192,384]{1,0:T(8,128)(2,1)S(1)}, u32[]{:S(2)}, u32[]{:S(2)}) collective-permute-start(bf16[192,384]{1,0:T(8,128)(2,1)} %get-tuple-element.23), channel_id=1, source_target_pairs={{0,1},{1,0},{2,3},{3,2},{4,5},{5,4},{6,7},{7,6},{8,9},{9,8},{10,11... | collective-permute-start | bytes 442376 | tf_op jit(solution)/shard_map/ppermute | solution.py:303
  7.0 2.5 %collective-permute-start.2 = (bf16[64,384]{1,0:T(8,128)(2,1)}, bf16[64,384]{1,0:T(8,128)(2,1)S(1)}, u32[]{:S(2)}, u32[]{:S(2)}) collective-permute-start(bf16[64,384]{1,0:T(8,128)(2,1)} %get-tuple-element.25), channel_id=1, source_target_pairs={{0,3},{1,2},{2,1},{3,0},{4,7},{5,6},{6,5},{7,4},{8,11},{9,10},{10,... | collective-permute-start | bytes 147464 | tf_op jit(solution)/shard_map/ppermute | solution.py:303
  9.4 0.9 %copy-done = bf16[1024,128]{1,0:T(8,128)(2,1)S(1)} copy-done((bf16[1024,128]{1,0:T(8,128)(2,1)S(1)}, bf16[1024,128]{1,0:T(8,128)(2,1)}, u32[]{:S(2)}) %copy-start) | copy-done | bytes 262168
  10.4 3.8 %more_products.1 = (bf16[64,384]{1,0:T(8,128)(2,1)S(1)}, f32[192,384]{1,0:T(8,128)S(1)}, bf16[256,384]{1,0:T(8,128)(2,1)S(1)}, f32[256,384]{1,0:T(8,128)S(1)}) custom-call(bf16[1024,128]{1,0:T(8,128)(2,1)S(1)} %copy-done, bf16[3,1024,1024]{2,1,0:T(8,128)(2,1)} %influence_ref.3), custom_call_target="tpu_custom_call" | custom-call | flops 603979776 | bytes 4718592 | tf_op jit(solution)/shard_map/more_products/pallas_call | solution.py:138
  14.2 0.7 %collective-permute-start.1 = (bf16[256,384]{1,0:T(8,128)(2,1)S(1)}, bf16[256,384]{1,0:T(8,128)(2,1)S(1)}, u32[]{:S(2)}, u32[]{:S(2)}) collective-permute-start(bf16[256,384]{1,0:T(8,128)(2,1)S(1)} %get-tuple-element.24), channel_id=1, source_target_pairs={{0,1},{1,0},{2,3},{3,2},{4,5},{5,4},{6,7},{7,6},{8,9},{9,8},{10,11... | collective-permute-start | bytes 589832 | tf_op jit(solution)/shard_map/ppermute | solution.py:303
  15.0 1.5 %collective-permute-start.4 = (bf16[192,384]{1,0:T(8,128)(2,1)S(1)}, bf16[192,384]{1,0:T(8,128)(2,1)S(1)}, u32[]{:S(2)}, u32[]{:S(2)}) collective-permute-start(bf16[192,384]{1,0:T(8,128)(2,1)S(1)} %pass_sum.1), channel_id=1, source_target_pairs={{0,2},{1,3},{2,0},{3,1},{4,6},{5,7},{6,4},{7,5},{8,10},{9,11},{10,... | collective-permute-start | bytes 442376 | tf_op jit(solution)/shard_map/ppermute | solution.py:303
  16.5 1.5 %collective-permute-start.3 = (bf16[64,384]{1,0:T(8,128)(2,1)S(1)}, bf16[64,384]{1,0:T(8,128)(2,1)S(1)}, u32[]{:S(2)}, u32[]{:S(2)}) collective-permute-start(bf16[64,384]{1,0:T(8,128)(2,1)S(1)} %get-tuple-element.26), channel_id=1, source_target_pairs={{0,2},{1,3},{2,0},{3,1},{4,6},{5,7},{6,4},{7,5},{8,10},{9,11},{10,... | collective-permute-start | bytes 147464 | tf_op jit(solution)/shard_map/ppermute | solution.py:303
  18.0 8.0 %collective-permute-done.3.refs_2_ = bf16[64,384]{1,0:T(8,128)(2,1)S(1)} collective-permute-done((bf16[64,384]{1,0:T(8,128)(2,1)S(1)}, bf16[64,384]{1,0:T(8,128)(2,1)S(1)}, u32[]{:S(2)}, u32[]{:S(2)}) %collective-permute-start.3) | collective-permute-done | bytes 49184 | tf_op jit(solution)/shard_map/ppermute | solution.py:303
  26.1 1.7 %collective-permute-start.10 = (bf16[256,384]{1,0:T(8,128)(2,1)S(1)}, bf16[256,384]{1,0:T(8,128)(2,1)S(1)}, u32[]{:S(2)}, u32[]{:S(2)}) collective-permute-start(bf16[256,384]{1,0:T(8,128)(2,1)S(1)} %share_sum.1.refs_0_), channel_id=1, source_target_pairs={{0,8},{4,12},{8,0},{12,4},{1,9},{5,13},{9,1},{13,5},{2,10},{6,14},... | collective-permute-start | bytes 589832 | tf_op jit(solution)/shard_map/ppermute | solution.py:303
  27.9 1.6 %collective-permute-start.5 = (bf16[256,384]{1,0:T(8,128)(2,1)S(1)}, bf16[256,384]{1,0:T(8,128)(2,1)S(1)}, u32[]{:S(2)}, u32[]{:S(2)}) collective-permute-start(bf16[256,384]{1,0:T(8,128)(2,1)S(1)} %share_sum.1.refs_0_), channel_id=1, source_target_pairs={{0,1},{1,0},{2,3},{3,2},{4,5},{5,4},{6,7},{7,6},{8,9},{9,8},{10,11... | collective-permute-start | bytes 589832 | tf_op jit(solution)/shard_map/ppermute | solution.py:303
  29.6 2.3 %collective-permute-done.10.refs_1_ = bf16[256,384]{1,0:T(8,128)(2,1)S(1)} collective-permute-done((bf16[256,384]{1,0:T(8,128)(2,1)S(1)}, bf16[256,384]{1,0:T(8,128)(2,1)S(1)}, u32[]{:S(2)}, u32[]{:S(2)}) %collective-permute-start.10) | collective-permute-done | bytes 196640 | tf_op jit(solution)/shard_map/ppermute | solution.py:303
  31.8 3.9 %collective-permute-done.6.refs_2_ = bf16[256,384]{1,0:T(8,128)(2,1)S(1)} collective-permute-done((bf16[256,384]{1,0:T(8,128)(2,1)S(1)}, bf16[256,384]{1,0:T(8,128)(2,1)S(1)}, u32[]{:S(2)}, u32[]{:S(2)}) %collective-permute-start.6) | collective-permute-done | bytes 196640 | tf_op jit(solution)/shard_map/ppermute | solution.py:303
  35.8 1.3 %collective-permute-start.8 = (bf16[256,384]{1,0:T(8,128)(2,1)S(1)}, bf16[256,384]{1,0:T(8,128)(2,1)S(1)}, u32[]{:S(2)}, u32[]{:S(2)}) collective-permute-start(bf16[256,384]{1,0:T(8,128)(2,1)S(1)} %collective-permute-done.6.refs_2_), channel_id=1, source_target_pairs={{0,1},{1,0},{2,3},{3,2},{4,5},{5,4},{6,7},{7,6},{8,9},{9,8},{10,11... | collective-permute-start | bytes 589832 | tf_op jit(solution)/shard_map/ppermute | solution.py:303
  37.1 0.5 collective-permute-start.7
  37.8 1.5 %collective-permute-start.13 = (bf16[256,384]{1,0:T(8,128)(2,1)S(1)}, bf16[256,384]{1,0:T(8,128)(2,1)S(1)}, u32[]{:S(2)}, u32[]{:S(2)}) collective-permute-start(bf16[256,384]{1,0:T(8,128)(2,1)S(1)} %collective-permute-done.10.refs_1_), channel_id=1, source_target_pairs={{0,3},{1,2},{2,1},{3,0},{4,7},{5,6},{6,5},{7,4},{8,11},{9,10},{10,... | collective-permute-start | bytes 589832 | tf_op jit(solution)/shard_map/ppermute | solution.py:303
  39.3 1.5 %collective-permute-start.14 = (bf16[256,384]{1,0:T(8,128)(2,1)S(1)}, bf16[256,384]{1,0:T(8,128)(2,1)S(1)}, u32[]{:S(2)}, u32[]{:S(2)}) collective-permute-start(bf16[256,384]{1,0:T(8,128)(2,1)S(1)} %collective-permute-done.6.refs_2_), channel_id=1, source_target_pairs={{0,8},{4,12},{8,0},{12,4},{1,9},{5,13},{9,1},{13,5},{2,10},{6,14},... | collective-permute-start | bytes 589832 | tf_op jit(solution)/shard_map/ppermute | solution.py:303
  40.8 1.6 %early_rows.3.refs_2_ = f32[6,256,384]{2,1,0:T(8,128)S(1)} custom-call(s32[3,2]{1,0:T(4,128)S(1)} %copy.10.pairs_ref, s32[16,1,256]{2,1,0:T(1,128)S(1)} %bitcast.4, bf16[256,384]{1,0:T(8,128)(2,1)S(1)} %join.6.refs_0_, bf16[256,384]{1,0:T(8,128)(2,1)S(1)} %collective-permute-done.11.refs_1_), custom_call_target="tpu_custom_call" | custom-call | flops 1207959552 | bytes 4718592 | tf_op jit(solution)/shard_map/early_rows/pallas_call | solution.py:229
  42.3 0.8 %collective-permute-done.8.refs_1_ = bf16[256,384]{1,0:T(8,128)(2,1)S(1)} collective-permute-done((bf16[256,384]{1,0:T(8,128)(2,1)S(1)}, bf16[256,384]{1,0:T(8,128)(2,1)S(1)}, u32[]{:S(2)}, u32[]{:S(2)}) %collective-permute-start.8) | collective-permute-done | bytes 196640 | tf_op jit(solution)/shard_map/ppermute | solution.py:303
  43.2 1.7 %collective-permute-done.7.refs_0_ = bf16[256,384]{1,0:T(8,128)(2,1)S(1)} collective-permute-done((bf16[256,384]{1,0:T(8,128)(2,1)S(1)}, bf16[256,384]{1,0:T(8,128)(2,1)S(1)}, u32[]{:S(2)}, u32[]{:S(2)}) %collective-permute-start.7) | collective-permute-done | bytes 196640 | tf_op jit(solution)/shard_map/ppermute | solution.py:303
  45.0 3.2 %early_rows.4.refs_2_ = f32[6,256,384]{2,1,0:T(8,128)S(1)} custom-call(s32[3,2]{1,0:T(4,128)S(1)} %copy.10.pairs_ref, s32[16,1,256]{2,1,0:T(1,128)S(1)} %bitcast.5, bf16[768,384]{1,0:T(8,128)(2,1)S(1)} %join.5.refs_0_, bf16[768,384]{1,0:T(8,128)(2,1)S(1)} %collective-permute-done.12.refs_1_, f32[6,256,384]{2,1,0:T(8,128)S(1)} %early_rows.3.refs_2_), custom_call_target="tpu_custom_call" | custom-call | flops 3623878656 | bytes 4718592 | tf_op jit(solution)/shard_map/early_rows/pallas_call | solution.py:229
  48.3 0.5 collective-permute-start.15
  48.9 2.4 %early_rows.5.early_ref = f32[6,256,384]{2,1,0:T(8,128)S(1)} custom-call(s32[3,2]{1,0:T(4,128)S(1)} %copy.10.pairs_ref, s32[16,1,256]{2,1,0:T(1,128)S(1)} %bitcast.6, bf16[512,384]{1,0:T(8,128)(2,1)S(1)} %join.4.refs_0_, bf16[512,384]{1,0:T(8,128)(2,1)S(1)} %collective-permute-done.9.refs_1_, f32[6,256,384]{2,1,0:T(8,128)S(1)} %early_rows.4.refs_2_), custom_call_target="tpu_custom_call" | custom-call | flops 2415919104 | bytes 4718592 | tf_op jit(solution)/shard_map/early_rows/pallas_call | solution.py:229
  51.4 5.8 %cross.1 = bf16[3,2,768,768]{3,2,1,0:T(8,128)(2,1)} custom-call(s32[3,2]{1,0:T(4,128)S(1)} %copy.10.pairs_ref, s32[16,1,256]{2,1,0:T(1,128)S(1)} %bitcast.7, f32[1,128]{1,0:T(1,128)S(1)} %maximum_bitcast_fusion.weights_ref, f32[6,256,384]{2,1,0:T(8,128)S(1)} %early_rows.5.early_ref, bf16[512,384]{1,0:T(8,128)(2,1)S(1)} %join.7.refs_0_, ...), custom_call_target="tpu_custom_call" | custom-call | tf_op jit(solution)/shard_map/cross/pallas_call | solution.py:277
  (30 shorter events, 0.8 us)
Async XLA Ops:
  3.9 10.3 %collective-permute-start = (bf16[192,384]{1,0:T(8,128)(2,1)}, bf16[192,384]{1,0:T(8,128)(2,1)S(1)}, u32[]{:S(2)}, u32[]{:S(2)}) collective-permute-start(bf16[192,384]{1,0:T(8,128)(2,1)} %get-tuple-element.23), channel_id=1, source_target_pairs={{0,1},{1,0},{2,3},{3,2},{4,5},{5,4},{6,7},{7,6},{8,9},{9,8},{10,11... | collective-permute-start | bytes 442376 | tf_op jit(solution)/shard_map/ppermute | solution.py:303
  7.0 8.0 %collective-permute-start.2 = (bf16[64,384]{1,0:T(8,128)(2,1)}, bf16[64,384]{1,0:T(8,128)(2,1)S(1)}, u32[]{:S(2)}, u32[]{:S(2)}) collective-permute-start(bf16[64,384]{1,0:T(8,128)(2,1)} %get-tuple-element.25), channel_id=1, source_target_pairs={{0,3},{1,2},{2,1},{3,0},{4,7},{5,6},{6,5},{7,4},{8,11},{9,10},{10,... | collective-permute-start | bytes 147464 | tf_op jit(solution)/shard_map/ppermute | solution.py:303
  9.4 0.9 %copy-start = (bf16[1024,128]{1,0:T(8,128)(2,1)S(1)}, bf16[1024,128]{1,0:T(8,128)(2,1)}, u32[]{:S(2)}) copy-start(bf16[1024,128]{1,0:T(8,128)(2,1)} %get-tuple-element.20.my_loads_ref) | copy-start | bytes 786436
  14.2 23.5 %copy-start.2 = (s32[3,2]{0,1:T(2,128)S(1)}, s32[3,2]{0,1:T(2,128)}, u32[]{:S(2)}) copy-start(s32[3,2]{0,1:T(2,128)} %param.11) | copy-start | bytes 76
  14.2 26.6 %copy-start.1 = (s32[4096]{0:T(1024)S(1)}, s32[4096]{0:T(1024)}, u32[]{:S(2)}) copy-start(s32[4096]{0:T(1024)} %param.10) | copy-start | bytes 49156
  14.2 11.8 %collective-permute-start.1 = (bf16[256,384]{1,0:T(8,128)(2,1)S(1)}, bf16[256,384]{1,0:T(8,128)(2,1)S(1)}, u32[]{:S(2)}, u32[]{:S(2)}) collective-permute-start(bf16[256,384]{1,0:T(8,128)(2,1)S(1)} %get-tuple-element.24), channel_id=1, source_target_pairs={{0,1},{1,0},{2,3},{3,2},{4,5},{5,4},{6,7},{7,6},{8,9},{9,8},{10,11... | collective-permute-start | bytes 589832 | tf_op jit(solution)/shard_map/ppermute | solution.py:303
  15.0 11.0 %collective-permute-start.4 = (bf16[192,384]{1,0:T(8,128)(2,1)S(1)}, bf16[192,384]{1,0:T(8,128)(2,1)S(1)}, u32[]{:S(2)}, u32[]{:S(2)}) collective-permute-start(bf16[192,384]{1,0:T(8,128)(2,1)S(1)} %pass_sum.1), channel_id=1, source_target_pairs={{0,2},{1,3},{2,0},{3,1},{4,6},{5,7},{6,4},{7,5},{8,10},{9,11},{10,... | collective-permute-start | bytes 442376 | tf_op jit(solution)/shard_map/ppermute | solution.py:303
  16.5 9.5 %collective-permute-start.3 = (bf16[64,384]{1,0:T(8,128)(2,1)S(1)}, bf16[64,384]{1,0:T(8,128)(2,1)S(1)}, u32[]{:S(2)}, u32[]{:S(2)}) collective-permute-start(bf16[64,384]{1,0:T(8,128)(2,1)S(1)} %get-tuple-element.26), channel_id=1, source_target_pairs={{0,2},{1,3},{2,0},{3,1},{4,6},{5,7},{6,4},{7,5},{8,10},{9,11},{10,... | collective-permute-start | bytes 147464 | tf_op jit(solution)/shard_map/ppermute | solution.py:303
  26.1 5.7 %collective-permute-start.10 = (bf16[256,384]{1,0:T(8,128)(2,1)S(1)}, bf16[256,384]{1,0:T(8,128)(2,1)S(1)}, u32[]{:S(2)}, u32[]{:S(2)}) collective-permute-start(bf16[256,384]{1,0:T(8,128)(2,1)S(1)} %share_sum.1.refs_0_), channel_id=1, source_target_pairs={{0,8},{4,12},{8,0},{12,4},{1,9},{5,13},{9,1},{13,5},{2,10},{6,14},... | collective-permute-start | bytes 589832 | tf_op jit(solution)/shard_map/ppermute | solution.py:303
  27.8 7.9 %collective-permute-start.6 = (bf16[256,384]{1,0:T(8,128)(2,1)S(1)}, bf16[256,384]{1,0:T(8,128)(2,1)S(1)}, u32[]{:S(2)}, u32[]{:S(2)}) collective-permute-start(bf16[256,384]{1,0:T(8,128)(2,1)S(1)} %share_sum.1.refs_0_), channel_id=1, source_target_pairs={{0,2},{1,3},{2,0},{3,1},{4,6},{5,7},{6,4},{7,5},{8,10},{9,11},{10,... | collective-permute-start | bytes 589832 | tf_op jit(solution)/shard_map/ppermute | solution.py:303
  27.9 7.8 %collective-permute-start.5 = (bf16[256,384]{1,0:T(8,128)(2,1)S(1)}, bf16[256,384]{1,0:T(8,128)(2,1)S(1)}, u32[]{:S(2)}, u32[]{:S(2)}) collective-permute-start(bf16[256,384]{1,0:T(8,128)(2,1)S(1)} %share_sum.1.refs_0_), channel_id=1, source_target_pairs={{0,1},{1,0},{2,3},{3,2},{4,5},{5,4},{6,7},{7,6},{8,9},{9,8},{10,11... | collective-permute-start | bytes 589832 | tf_op jit(solution)/shard_map/ppermute | solution.py:303
  29.5 6.3 %collective-permute-start.11 = (bf16[256,384]{1,0:T(8,128)(2,1)S(1)}, bf16[256,384]{1,0:T(8,128)(2,1)S(1)}, u32[]{:S(2)}, u32[]{:S(2)}) collective-permute-start(bf16[256,384]{1,0:T(8,128)(2,1)S(1)} %join.6.refs_0_), channel_id=1, source_target_pairs={{0,4},{4,0},{8,12},{12,8},{1,5},{5,1},{9,13},{13,9},{2,6},{6,2},{1... | collective-permute-start | bytes 589832 | tf_op jit(solution)/shard_map/ppermute | solution.py:303
  35.8 9.2 %collective-permute-start.12 = (bf16[768,384]{1,0:T(8,128)(2,1)S(1)}, bf16[768,384]{1,0:T(8,128)(2,1)S(1)}, u32[]{:S(2)}, u32[]{:S(2)}) collective-permute-start(bf16[768,384]{1,0:T(8,128)(2,1)S(1)} %join.5.refs_0_), channel_id=1, source_target_pairs={{0,4},{4,0},{8,12},{12,8},{1,5},{5,1},{9,13},{13,9},{2,6},{6,2},{1... | collective-permute-start | bytes 1769480 | tf_op jit(solution)/shard_map/ppermute | solution.py:303
  35.8 7.3 %collective-permute-start.8 = (bf16[256,384]{1,0:T(8,128)(2,1)S(1)}, bf16[256,384]{1,0:T(8,128)(2,1)S(1)}, u32[]{:S(2)}, u32[]{:S(2)}) collective-permute-start(bf16[256,384]{1,0:T(8,128)(2,1)S(1)} %collective-permute-done.6.refs_2_), channel_id=1, source_target_pairs={{0,1},{1,0},{2,3},{3,2},{4,5},{5,4},{6,7},{7,6},{8,9},{9,8},{10,11... | collective-permute-start | bytes 589832 | tf_op jit(solution)/shard_map/ppermute | solution.py:303
  37.1 7.7 %collective-permute-start.7 = (bf16[256,384]{1,0:T(8,128)(2,1)S(1)}, bf16[256,384]{1,0:T(8,128)(2,1)S(1)}, u32[]{:S(2)}, u32[]{:S(2)}) collective-permute-start(bf16[256,384]{1,0:T(8,128)(2,1)S(1)} %collective-permute-done.5.refs_0_), channel_id=1, source_target_pairs={{0,8},{4,12},{8,0},{12,4},{1,9},{5,13},{9,1},{13,5},{2,10},{6,14},... | collective-permute-start | bytes 589832 | tf_op jit(solution)/shard_map/ppermute | solution.py:303
  37.8 10.6 %collective-permute-start.13 = (bf16[256,384]{1,0:T(8,128)(2,1)S(1)}, bf16[256,384]{1,0:T(8,128)(2,1)S(1)}, u32[]{:S(2)}, u32[]{:S(2)}) collective-permute-start(bf16[256,384]{1,0:T(8,128)(2,1)S(1)} %collective-permute-done.10.refs_1_), channel_id=1, source_target_pairs={{0,3},{1,2},{2,1},{3,0},{4,7},{5,6},{6,5},{7,4},{8,11},{9,10},{10,... | collective-permute-start | bytes 589832 | tf_op jit(solution)/shard_map/ppermute | solution.py:303
  39.3 9.0 %collective-permute-start.14 = (bf16[256,384]{1,0:T(8,128)(2,1)S(1)}, bf16[256,384]{1,0:T(8,128)(2,1)S(1)}, u32[]{:S(2)}, u32[]{:S(2)}) collective-permute-start(bf16[256,384]{1,0:T(8,128)(2,1)S(1)} %collective-permute-done.6.refs_2_), channel_id=1, source_target_pairs={{0,8},{4,12},{8,0},{12,4},{1,9},{5,13},{9,1},{13,5},{2,10},{6,14},... | collective-permute-start | bytes 589832 | tf_op jit(solution)/shard_map/ppermute | solution.py:303
  44.9 3.9 %copy-start.3 = (f32[64]{0:T(128)S(1)}, f32[64]{0:T(128)}, u32[]{:S(2)}) copy-start(f32[64]{0:T(128)} %param.9) | copy-start | bytes 772
  44.9 4.0 %collective-permute-start.9 = (bf16[512,384]{1,0:T(8,128)(2,1)S(1)}, bf16[512,384]{1,0:T(8,128)(2,1)S(1)}, u32[]{:S(2)}, u32[]{:S(2)}) collective-permute-start(bf16[512,384]{1,0:T(8,128)(2,1)S(1)} %join.4.refs_0_), channel_id=1, source_target_pairs={{0,4},{4,0},{8,12},{12,8},{1,5},{5,1},{9,13},{13,9},{2,6},{6,2},{1... | collective-permute-start | bytes 1179656 | tf_op jit(solution)/shard_map/ppermute | solution.py:303
  48.3 3.0 %collective-permute-start.15 = (bf16[512,384]{1,0:T(8,128)(2,1)S(1)}, bf16[512,384]{1,0:T(8,128)(2,1)S(1)}, u32[]{:S(2)}, u32[]{:S(2)}) collective-permute-start(bf16[512,384]{1,0:T(8,128)(2,1)S(1)} %join.7.refs_0_), channel_id=1, source_target_pairs={{0,4},{4,0},{8,12},{12,8},{1,5},{5,1},{9,13},{13,9},{2,6},{6,2},{1... | collective-permute-start | bytes 1179656 | tf_op jit(solution)/shard_map/ppermute | solution.py:303
